TPU v7x, 512 devices: a whole 4x4x16 slice. The times are simulated.
512 devices in a mesh: level: 4 (over z_lo), tx: 8 (over x, core), ty: 16 (over y, z_hi).
Axes of the slice: x: 4, y: 4, z: 16 (z_hi: 4, z_lo: 4; z = z_hi * 4 + z_lo), core: 2. Of those that a mesh axis runs over, the one named last changes fastest.
Arguments:
- initial: float32 [48, 256, 2048], P(None, 'tx', 'ty'), may hold values from -6 to 6
- layer_ids: int32 [48], replicated, may hold values from 0 to 5
- lateral_number: float32 [6], replicated, may hold values from 0.05 to 0.24
- vertical_number: float32 [6], replicated, may hold values from 0.5 to 8
- pulse_rates: float32 [8], replicated, may hold values from 0.5 to 4
- bore_x: int32 [1024], replicated, may hold values from 0 to 255
- bore_y: int32 [1024], replicated, may hold values from 0 to 2047
- plan: int32 [1024, 7], replicated, may hold values from 0 to 7
Outputs:
- states: float32 [4, 48, 256, 2048], P('level', None, 'tx', 'ty')
All inputs are finite; a program needn't handle non-finite values.
Results may differ from a plain program's by a relative error of at most 0.00022.
Values sent between devices are 32-bit elements; how exact they have to be, the bound alone decides.
No kernel may reach another device: no remote copies, remote signals or barrier semaphores. Data moves between devices by JAX's collectives and lax.ppermute only.
A program may use at most 128 MiB of HBM per device.

v0:
```python
import jax
import jax.numpy as jnp
from jax import lax
from jax.sharding import PartitionSpec as P

NZ = 48
STEPS = 6
NLAYER = 6
NPULSE = 8


def with_halo(array, sides, width):
    for axis, dim in sides:
        devices, length = (lax.axis_size(axis), array.shape[dim])
        up = [(i, (i + 1) % devices) for i in range(devices - 1)]
        down = [(j, i) for i, j in up]
        last = lax.slice_in_dim(array, length - width, length, axis=dim)
        initial = lax.slice_in_dim(array, 0, width, axis=dim)
        before = lax.ppermute(last, axis, up)
        after = lax.ppermute(initial, axis, down)
        array = jnp.concatenate([before, array, after], axis=dim)
    return array


def from_behind(value, axis, steps):
    count = lax.axis_size(axis)
    initial, last = (max(0, -steps), min(count, count - steps))
    return lax.ppermute(value, axis, [(source, source + steps) for source in range(initial, last)])


def vertical(layer_ids, lateral_number, vertical_number):
    kinds = jnp.arange(NLAYER, dtype=jnp.int32)
    onehot = (layer_ids[:, None] == kinds[None, :]).astype(jnp.float32)
    cond = jnp.sum(onehot * vertical_number[None, :], axis=1)
    lat_depth = jnp.sum(onehot * lateral_number[None, :], axis=1)
    link = 2.0 * cond[:-1] * cond[1:] / (cond[:-1] + cond[1:])
    zero_one = jnp.zeros((1,), jnp.float32)
    diagonal = jnp.concatenate([cond[:1], jnp.zeros((NZ - 1,), jnp.float32)])
    diagonal = diagonal + jnp.concatenate([link, zero_one]) + jnp.concatenate([zero_one, link])
    vertical_op = jnp.diag(diagonal) - jnp.diag(link, 1) - jnp.diag(link, -1)
    eye = jnp.eye(NZ, dtype=jnp.float32)
    lower_band = jnp.concatenate([zero_one, -link])
    upper_band = jnp.concatenate([-link, zero_one])
    inverse_block = lax.linalg.tridiagonal_solve(lower_band, 1.0 + diagonal, upper_band, eye)
    return (vertical_op, inverse_block, lat_depth)


def along_depth(matrix, field):
    return jnp.einsum("ij,jxy->ixy", matrix, field, precision=lax.Precision.HIGHEST)


def lateral_padded(padded, lat_depth):
    center = padded[:, 1:-1, 1:-1]
    beside = padded[:, 2:, 1:-1] + padded[:, :-2, 1:-1] + padded[:, 1:-1, 2:] + padded[:, 1:-1, :-2]
    return lat_depth[:, None, None] * (beside - 4.0 * center)


def on_device(
    initial, layer_ids, lateral_number, vertical_number, pulse_rates, bore_x, bore_y, plan
):
    vertical_op, inverse_block, lat_depth = vertical(layer_ids, lateral_number, vertical_number)
    depth_count, rows_x, rows_y = initial.shape
    depth = jnp.arange(depth_count, dtype=jnp.int32)
    profile = ((depth >= 2) & (depth < depth_count - 4)).astype(jnp.float32)
    cells_x = lax.axis_index("tx") * rows_x + jnp.arange(rows_x, dtype=jnp.int32)
    cells_y = lax.axis_index("ty") * rows_y + jnp.arange(rows_y, dtype=jnp.int32)
    hits_x = (bore_x[:, None] == cells_x[None, :]).astype(jnp.float32)
    hits_y = (bore_y[:, None] == cells_y[None, :]).astype(jnp.float32)
    pulse_kinds = jnp.arange(NPULSE, dtype=jnp.int32)
    my_level = lax.axis_index("level")
    level_count = lax.axis_size("level")
    ticks = STEPS + level_count - 1

    def source_at(point):
        point = jnp.clip(point, 0, STEPS)
        column = lax.dynamic_slice_in_dim(plan, point, 1, 1)[:, 0]
        picked = (column[:, None] == pulse_kinds[None, :]).astype(jnp.float32)
        rate_bore = jnp.sum(picked * pulse_rates[None, :], axis=1)
        plane = jnp.dot(hits_x.T, rate_bore[:, None] * hits_y, precision=lax.Precision.HIGHEST)
        return profile[:, None, None] * plane[None, :, :]

    def tick(tick_idx, carry):
        state, flux_now, flux_old, low_lat = carry
        step_idx = tick_idx - my_level
        active = (step_idx >= 0) & (step_idx < STEPS)
        padded = with_halo(state, (("tx", 1), ("ty", 2)), 1)
        own_lat = lateral_padded(padded, lat_depth)
        recv_state, recv_lat = from_behind((state, own_lat), "level", 1)
        own_vert = along_depth(vertical_op, state)
        recv_vert = along_depth(vertical_op, recv_state)
        source_now = source_at(step_idx)
        source_next = source_at(step_idx + 1)
        first = step_idx == 0
        flux_cur = jnp.where(first, own_lat - own_vert + source_now, flux_now)
        low_now = jnp.where(first, own_lat, low_lat)
        flux_new = recv_lat - recv_vert + source_next
        quad = jnp.where(
            first,
            0.5 * flux_cur + 0.5 * flux_new,
            -flux_old / 12.0 + 8.0 * flux_cur / 12.0 + 5.0 * flux_new / 12.0,
        )
        rhs = jnp.where(
            my_level == 0,
            state + own_lat + source_now,
            state + own_lat - low_now + recv_vert + quad,
        )
        updated = along_depth(inverse_block, rhs)
        return (
            jnp.where(active, updated, state),
            jnp.where(active, flux_new, flux_now),
            jnp.where(active, flux_cur, flux_old),
            jnp.where(active, recv_lat, low_lat),
        )

    blank = jnp.zeros_like(initial)
    final_state = lax.fori_loop(0, ticks, tick, (initial, blank, blank, blank))[0]
    return final_state[None]


def solution(mesh):
    return jax.shard_map(
        on_device,
        mesh=mesh,
        in_specs=(P(None, "tx", "ty"), P(), P(), P(), P(), P(), P(), P()),
        out_specs=P("level", None, "tx", "ty"),
        check_vma=False,
    )
```

profile of v0, /device:TPU:25, one launch (start us, length us, event | category | flops | bytes accessed | tf_op | source)
XLA Modules:
  0.0 638.0 jit_solution(4413613658007634711)
XLA Ops:
  94.4 30.3 %fusion.137 = (f32[1,48]{1,0:T(1,128)S(1)}, f32[48]{0:T(128)S(1)}, f32[48]{0:T(128)S(1)}, f32[48]{0:T(128)S(1)}, f32[48]{0:T(128)S(1)}, /*index=5*/f32[48]{0:T(1...) fusion(f32[]{:T(128)S(6)} %div.4813, ...), kind=kLoop, calls=%fused_computation.303 | loop fusion | flops 6912 | bytes 11904 | tf_op jit(solution)/shard_map/while/body/broadcast_in_dim | solution.py:44
  124.7 22.7 %subtract_divide_fusion = (f32[1,48]{1,0:T(1,128)S(1)}, f32[1,48]{1,0:T(1,128)S(1)}, f32[1,48]{1,0:T(1,128)S(1)}, f32[1,48]{1,0:T(1,128)S(1)}, f32[1,48]{1,0:T(1...) fusion(f32[48,48]{1,0:T(8,128)S(1)} %fusion.87, ...), kind=kLoop, calls=%fused_computation.261 | loop fusion | flops 5184 | bytes 14304 | tf_op jit(solution)/shard_map/eval_jaxpr/div | solution.py:44
  152.7 484.1 %while.15 = (s32[]{:T(128)}, f32[48,32,128]{2,0,1:T(8,128)S(1)}, f32[48,32,128]{2,0,1:T(8,128)}, f32[48,32,128]{2,0,1:T(8,128)}, f32[48,32,128]{2,0,1:T(8,128)},...) while((s32[]{:T(128)}, f32[48,32,128]{2,0,1:T(8,128)S(1)}, ...), condition=%wide.region_5.6_spmd.clone.clone, body=%wide.region_2.5_spmd.clone.clone.sunk | while | flops 450382016 | bytes 44845076 | solution.py:116
  167.3 11.8 %collective-permute-start.3 = (f32[48,34,1]{0,2,1:T(1,128)S(1)}, f32[48,34,1]{0,2,1:T(1,128)S(1)}, u32[]{:S(2)}, u32[]{:S(2)}) collective-permute-start(f32[48,34,1]{0,2,1:T(1,128)S(1)} %copy.31), channel_id=1, source_target_pairs={{1,0},{2,1},{3,2},{4,3},{5,4},{6,5},{7,6},{8,7},{9,8},{10,9},{11,1... | collective-permute-start | bytes 19592 | tf_op jit(solution)/shard_map/while/body/eval_jaxpr/ppermute | solution.py:20
  181.0 7.3 %collective-permute-done.2 = f32[48,34,1]{0,2,1:T(1,128)S(1)} collective-permute-done((f32[48,34,1]{0,2,1:T(1,128)S(1)}, f32[48,34,1]{0,2,1:T(1,128)S(1)}, u32[]{:S(2)}, u32[]{:S(2)}) %collective-permute-start.2) | collective-permute-done | bytes 6560 | tf_op jit(solution)/shard_map/while/body/eval_jaxpr/ppermute | solution.py:19
  195.6 13.2 %collective-permute-done.4 = f32[48,32,128]{2,0,1:T(8,128)S(1)} collective-permute-done((f32[48,32,128]{2,0,1:T(8,128)S(1)}, f32[48,32,128]{2,0,1:T(8,128)S(1)}, u32[]{:S(2)}, u32[]{:S(2)}) %collective-permute-start.4) | collective-permute-done | bytes 786464 | tf_op jit(solution)/shard_map/while/body/eval_jaxpr/ppermute | solution.py:28
  214.6 4.7 collective-permute-start.5
  234.2 4.9 collective-permute-start.2
  250.7 13.3 %collective-permute-done.4 = f32[48,32,128]{2,0,1:T(8,128)S(1)} collective-permute-done((f32[48,32,128]{2,0,1:T(8,128)S(1)}, f32[48,32,128]{2,0,1:T(8,128)S(1)}, u32[]{:S(2)}, u32[]{:S(2)}) %collective-permute-start.4) | collective-permute-done | bytes 786464 | tf_op jit(solution)/shard_map/while/body/eval_jaxpr/ppermute | solution.py:28
  269.7 4.7 collective-permute-start.5
  287.6 6.6 %collective-permute-start.2 = (f32[48,34,1]{0,2,1:T(1,128)S(1)}, f32[48,34,1]{0,2,1:T(1,128)S(1)}, u32[]{:S(2)}, u32[]{:S(2)}) collective-permute-start(f32[48,34,1]{0,2,1:T(1,128)S(1)} %copy.29), channel_id=1, source_target_pairs={{0,1},{1,2},{2,3},{3,4},{4,5},{5,6},{6,7},{7,8},{8,9},{9,10},{10,1... | collective-permute-start | bytes 19592 | tf_op jit(solution)/shard_map/while/body/eval_jaxpr/ppermute | solution.py:19
  303.4 13.3 %collective-permute-done.4 = f32[48,32,128]{2,0,1:T(8,128)S(1)} collective-permute-done((f32[48,32,128]{2,0,1:T(8,128)S(1)}, f32[48,32,128]{2,0,1:T(8,128)S(1)}, u32[]{:S(2)}, u32[]{:S(2)}) %collective-permute-start.4) | collective-permute-done | bytes 786464 | tf_op jit(solution)/shard_map/while/body/eval_jaxpr/ppermute | solution.py:28
  322.4 4.7 collective-permute-start.5
  339.0 5.7 collective-permute-start.2
  354.8 13.4 %collective-permute-done.4 = f32[48,32,128]{2,0,1:T(8,128)S(1)} collective-permute-done((f32[48,32,128]{2,0,1:T(8,128)S(1)}, f32[48,32,128]{2,0,1:T(8,128)S(1)}, u32[]{:S(2)}, u32[]{:S(2)}) %collective-permute-start.4) | collective-permute-done | bytes 786464 | tf_op jit(solution)/shard_map/while/body/eval_jaxpr/ppermute | solution.py:28
  374.0 4.7 collective-permute-start.5
  386.7 6.4 %collective-permute-start.3 = (f32[48,34,1]{0,2,1:T(1,128)S(1)}, f32[48,34,1]{0,2,1:T(1,128)S(1)}, u32[]{:S(2)}, u32[]{:S(2)}) collective-permute-start(f32[48,34,1]{0,2,1:T(1,128)S(1)} %copy.31), channel_id=1, source_target_pairs={{1,0},{2,1},{3,2},{4,3},{5,4},{6,5},{7,6},{8,7},{9,8},{10,9},{11,1... | collective-permute-start | bytes 19592 | tf_op jit(solution)/shard_map/while/body/eval_jaxpr/ppermute | solution.py:20
  395.9 6.5 %collective-permute-done.2 = f32[48,34,1]{0,2,1:T(1,128)S(1)} collective-permute-done((f32[48,34,1]{0,2,1:T(1,128)S(1)}, f32[48,34,1]{0,2,1:T(1,128)S(1)}, u32[]{:S(2)}, u32[]{:S(2)}) %collective-permute-start.2) | collective-permute-done | bytes 6560 | tf_op jit(solution)/shard_map/while/body/eval_jaxpr/ppermute | solution.py:19
  408.9 13.9 %collective-permute-done.4 = f32[48,32,128]{2,0,1:T(8,128)S(1)} collective-permute-done((f32[48,32,128]{2,0,1:T(8,128)S(1)}, f32[48,32,128]{2,0,1:T(8,128)S(1)}, u32[]{:S(2)}, u32[]{:S(2)}) %collective-permute-start.4) | collective-permute-done | bytes 786464 | tf_op jit(solution)/shard_map/while/body/eval_jaxpr/ppermute | solution.py:28
  428.4 5.0 collective-permute-start.5
  445.1 5.5 collective-permute-start.2
  461.2 13.7 %collective-permute-done.4 = f32[48,32,128]{2,0,1:T(8,128)S(1)} collective-permute-done((f32[48,32,128]{2,0,1:T(8,128)S(1)}, f32[48,32,128]{2,0,1:T(8,128)S(1)}, u32[]{:S(2)}, u32[]{:S(2)}) %collective-permute-start.4) | collective-permute-done | bytes 786464 | tf_op jit(solution)/shard_map/while/body/eval_jaxpr/ppermute | solution.py:28
  480.6 5.0 collective-permute-start.5
  495.6 7.3 %collective-permute-start.2 = (f32[48,34,1]{0,2,1:T(1,128)S(1)}, f32[48,34,1]{0,2,1:T(1,128)S(1)}, u32[]{:S(2)}, u32[]{:S(2)}) collective-permute-start(f32[48,34,1]{0,2,1:T(1,128)S(1)} %copy.29), channel_id=1, source_target_pairs={{0,1},{1,2},{2,3},{3,4},{4,5},{5,6},{6,7},{7,8},{8,9},{9,10},{10,1... | collective-permute-start | bytes 19592 | tf_op jit(solution)/shard_map/while/body/eval_jaxpr/ppermute | solution.py:19
  511.6 13.9 %collective-permute-done.4 = f32[48,32,128]{2,0,1:T(8,128)S(1)} collective-permute-done((f32[48,32,128]{2,0,1:T(8,128)S(1)}, f32[48,32,128]{2,0,1:T(8,128)S(1)}, u32[]{:S(2)}, u32[]{:S(2)}) %collective-permute-start.4) | collective-permute-done | bytes 786464 | tf_op jit(solution)/shard_map/while/body/eval_jaxpr/ppermute | solution.py:28
  531.2 4.9 collective-permute-start.5
  547.1 6.2 collective-permute-start.2
  563.0 13.9 %collective-permute-done.4 = f32[48,32,128]{2,0,1:T(8,128)S(1)} collective-permute-done((f32[48,32,128]{2,0,1:T(8,128)S(1)}, f32[48,32,128]{2,0,1:T(8,128)S(1)}, u32[]{:S(2)}, u32[]{:S(2)}) %collective-permute-start.4) | collective-permute-done | bytes 786464 | tf_op jit(solution)/shard_map/while/body/eval_jaxpr/ppermute | solution.py:28
  582.6 4.9 collective-permute-start.5
  595.5 5.7 collective-permute-start.3
  604.7 5.8 collective-permute-done.2
  617.3 13.9 %collective-permute-done.4 = f32[48,32,128]{2,0,1:T(8,128)S(1)} collective-permute-done((f32[48,32,128]{2,0,1:T(8,128)S(1)}, f32[48,32,128]{2,0,1:T(8,128)S(1)}, u32[]{:S(2)}, u32[]{:S(2)}) %collective-permute-start.4) | collective-permute-done | bytes 786464 | tf_op jit(solution)/shard_map/while/body/eval_jaxpr/ppermute | solution.py:28
  (372 shorter events, 252.8 us)
Async XLA Ops:
  152.8 42.9 %collective-permute-start.5 = (f32[48,32,128]{2,0,1:T(8,128)S(1)}, f32[48,32,128]{2,0,1:T(8,128)}, u32[]{:S(2)}, u32[]{:S(2)}) collective-permute-start(f32[48,32,128]{2,0,1:T(8,128)S(1)} %copy.50), channel_id=1, source_target_pairs={{0,128},{128,256},{256,384},{1,129},{129,257},{257,385},{2,130},{1... | collective-permute-start | bytes 2359304 | tf_op jit(solution)/shard_map/while/body/eval_jaxpr/ppermute | solution.py:28
  167.3 21.4 %collective-permute-start.3 = (f32[48,34,1]{0,2,1:T(1,128)S(1)}, f32[48,34,1]{0,2,1:T(1,128)S(1)}, u32[]{:S(2)}, u32[]{:S(2)}) collective-permute-start(f32[48,34,1]{0,2,1:T(1,128)S(1)} %copy.31), channel_id=1, source_target_pairs={{1,0},{2,1},{3,2},{4,3},{5,4},{6,5},{7,6},{8,7},{9,8},{10,9},{11,1... | collective-permute-start | bytes 19592 | tf_op jit(solution)/shard_map/while/body/eval_jaxpr/ppermute | solution.py:20
  189.8 19.1 %collective-permute-start.4 = (f32[48,32,128]{2,0,1:T(8,128)S(1)}, f32[48,32,128]{2,0,1:T(8,128)S(1)}, u32[]{:S(2)}, u32[]{:S(2)}) collective-permute-start(f32[48,32,128]{2,0,1:T(8,128)S(1)} %fusion.180), channel_id=1, source_target_pairs={{0,128},{128,256},{256,384},{1,129},{129,257},{257,385},{2,130},{1... | collective-permute-start | bytes 2359304 | tf_op jit(solution)/shard_map/while/body/eval_jaxpr/ppermute | solution.py:28
  214.6 36.1 %collective-permute-start.5 = (f32[48,32,128]{2,0,1:T(8,128)S(1)}, f32[48,32,128]{2,0,1:T(8,128)}, u32[]{:S(2)}, u32[]{:S(2)}) collective-permute-start(f32[48,32,128]{2,0,1:T(8,128)S(1)} %copy.50), channel_id=1, source_target_pairs={{0,128},{128,256},{256,384},{1,129},{129,257},{257,385},{2,130},{1... | collective-permute-start | bytes 2359304 | tf_op jit(solution)/shard_map/while/body/eval_jaxpr/ppermute | solution.py:28
  229.9 14.0 %collective-permute-start.3 = (f32[48,34,1]{0,2,1:T(1,128)S(1)}, f32[48,34,1]{0,2,1:T(1,128)S(1)}, u32[]{:S(2)}, u32[]{:S(2)}) collective-permute-start(f32[48,34,1]{0,2,1:T(1,128)S(1)} %copy.31), channel_id=1, source_target_pairs={{1,0},{2,1},{3,2},{4,3},{5,4},{6,5},{7,6},{8,7},{9,8},{10,9},{11,1... | collective-permute-start | bytes 19592 | tf_op jit(solution)/shard_map/while/body/eval_jaxpr/ppermute | solution.py:20
  244.9 19.1 %collective-permute-start.4 = (f32[48,32,128]{2,0,1:T(8,128)S(1)}, f32[48,32,128]{2,0,1:T(8,128)S(1)}, u32[]{:S(2)}, u32[]{:S(2)}) collective-permute-start(f32[48,32,128]{2,0,1:T(8,128)S(1)} %fusion.180), channel_id=1, source_target_pairs={{0,128},{128,256},{256,384},{1,129},{129,257},{257,385},{2,130},{1... | collective-permute-start | bytes 2359304 | tf_op jit(solution)/shard_map/while/body/eval_jaxpr/ppermute | solution.py:28
  269.7 33.6 %collective-permute-start.5 = (f32[48,32,128]{2,0,1:T(8,128)S(1)}, f32[48,32,128]{2,0,1:T(8,128)}, u32[]{:S(2)}, u32[]{:S(2)}) collective-permute-start(f32[48,32,128]{2,0,1:T(8,128)S(1)} %copy.50), channel_id=1, source_target_pairs={{0,128},{128,256},{256,384},{1,129},{129,257},{257,385},{2,130},{1... | collective-permute-start | bytes 2359304 | tf_op jit(solution)/shard_map/while/body/eval_jaxpr/ppermute | solution.py:28
  285.0 12.3 %collective-permute-start.3 = (f32[48,34,1]{0,2,1:T(1,128)S(1)}, f32[48,34,1]{0,2,1:T(1,128)S(1)}, u32[]{:S(2)}, u32[]{:S(2)}) collective-permute-start(f32[48,34,1]{0,2,1:T(1,128)S(1)} %copy.31), channel_id=1, source_target_pairs={{1,0},{2,1},{3,2},{4,3},{5,4},{6,5},{7,6},{8,7},{9,8},{10,9},{11,1... | collective-permute-start | bytes 19592 | tf_op jit(solution)/shard_map/while/body/eval_jaxpr/ppermute | solution.py:20
  287.6 9.3 %collective-permute-start.2 = (f32[48,34,1]{0,2,1:T(1,128)S(1)}, f32[48,34,1]{0,2,1:T(1,128)S(1)}, u32[]{:S(2)}, u32[]{:S(2)}) collective-permute-start(f32[48,34,1]{0,2,1:T(1,128)S(1)} %copy.29), channel_id=1, source_target_pairs={{0,1},{1,2},{2,3},{3,4},{4,5},{5,6},{6,7},{7,8},{8,9},{9,10},{10,1... | collective-permute-start | bytes 19592 | tf_op jit(solution)/shard_map/while/body/eval_jaxpr/ppermute | solution.py:19
  298.3 18.4 %collective-permute-start.4 = (f32[48,32,128]{2,0,1:T(8,128)S(1)}, f32[48,32,128]{2,0,1:T(8,128)S(1)}, u32[]{:S(2)}, u32[]{:S(2)}) collective-permute-start(f32[48,32,128]{2,0,1:T(8,128)S(1)} %fusion.180), channel_id=1, source_target_pairs={{0,128},{128,256},{256,384},{1,129},{129,257},{257,385},{2,130},{1... | collective-permute-start | bytes 2359304 | tf_op jit(solution)/shard_map/while/body/eval_jaxpr/ppermute | solution.py:28
  322.4 32.4 %collective-permute-start.5 = (f32[48,32,128]{2,0,1:T(8,128)S(1)}, f32[48,32,128]{2,0,1:T(8,128)}, u32[]{:S(2)}, u32[]{:S(2)}) collective-permute-start(f32[48,32,128]{2,0,1:T(8,128)S(1)} %copy.50), channel_id=1, source_target_pairs={{0,128},{128,256},{256,384},{1,129},{129,257},{257,385},{2,130},{1... | collective-permute-start | bytes 2359304 | tf_op jit(solution)/shard_map/while/body/eval_jaxpr/ppermute | solution.py:28
  335.5 13.2 %collective-permute-start.3 = (f32[48,34,1]{0,2,1:T(1,128)S(1)}, f32[48,34,1]{0,2,1:T(1,128)S(1)}, u32[]{:S(2)}, u32[]{:S(2)}) collective-permute-start(f32[48,34,1]{0,2,1:T(1,128)S(1)} %copy.31), channel_id=1, source_target_pairs={{1,0},{2,1},{3,2},{4,3},{5,4},{6,5},{7,6},{8,7},{9,8},{10,9},{11,1... | collective-permute-start | bytes 19592 | tf_op jit(solution)/shard_map/while/body/eval_jaxpr/ppermute | solution.py:20
  339.0 9.3 %collective-permute-start.2 = (f32[48,34,1]{0,2,1:T(1,128)S(1)}, f32[48,34,1]{0,2,1:T(1,128)S(1)}, u32[]{:S(2)}, u32[]{:S(2)}) collective-permute-start(f32[48,34,1]{0,2,1:T(1,128)S(1)} %copy.29), channel_id=1, source_target_pairs={{0,1},{1,2},{2,3},{3,4},{4,5},{5,6},{6,7},{7,8},{8,9},{9,10},{10,1... | collective-permute-start | bytes 19592 | tf_op jit(solution)/shard_map/while/body/eval_jaxpr/ppermute | solution.py:19
  349.7 18.5 %collective-permute-start.4 = (f32[48,32,128]{2,0,1:T(8,128)S(1)}, f32[48,32,128]{2,0,1:T(8,128)S(1)}, u32[]{:S(2)}, u32[]{:S(2)}) collective-permute-start(f32[48,32,128]{2,0,1:T(8,128)S(1)} %fusion.180), channel_id=1, source_target_pairs={{0,128},{128,256},{256,384},{1,129},{129,257},{257,385},{2,130},{1... | collective-permute-start | bytes 2359304 | tf_op jit(solution)/shard_map/while/body/eval_jaxpr/ppermute | solution.py:28
  374.0 34.9 %collective-permute-start.5 = (f32[48,32,128]{2,0,1:T(8,128)S(1)}, f32[48,32,128]{2,0,1:T(8,128)}, u32[]{:S(2)}, u32[]{:S(2)}) collective-permute-start(f32[48,32,128]{2,0,1:T(8,128)S(1)} %copy.50), channel_id=1, source_target_pairs={{0,128},{128,256},{256,384},{1,129},{129,257},{257,385},{2,130},{1... | collective-permute-start | bytes 2359304 | tf_op jit(solution)/shard_map/while/body/eval_jaxpr/ppermute | solution.py:28
  386.7 16.1 %collective-permute-start.3 = (f32[48,34,1]{0,2,1:T(1,128)S(1)}, f32[48,34,1]{0,2,1:T(1,128)S(1)}, u32[]{:S(2)}, u32[]{:S(2)}) collective-permute-start(f32[48,34,1]{0,2,1:T(1,128)S(1)} %copy.31), channel_id=1, source_target_pairs={{1,0},{2,1},{3,2},{4,3},{5,4},{6,5},{7,6},{8,7},{9,8},{10,9},{11,1... | collective-permute-start | bytes 19592 | tf_op jit(solution)/shard_map/while/body/eval_jaxpr/ppermute | solution.py:20
  393.1 9.3 %collective-permute-start.2 = (f32[48,34,1]{0,2,1:T(1,128)S(1)}, f32[48,34,1]{0,2,1:T(1,128)S(1)}, u32[]{:S(2)}, u32[]{:S(2)}) collective-permute-start(f32[48,34,1]{0,2,1:T(1,128)S(1)} %copy.29), channel_id=1, source_target_pairs={{0,1},{1,2},{2,3},{3,4},{4,5},{5,6},{6,7},{7,8},{8,9},{9,10},{10,1... | collective-permute-start | bytes 19592 | tf_op jit(solution)/shard_map/while/body/eval_jaxpr/ppermute | solution.py:19
  403.9 18.9 %collective-permute-start.4 = (f32[48,32,128]{2,0,1:T(8,128)S(1)}, f32[48,32,128]{2,0,1:T(8,128)S(1)}, u32[]{:S(2)}, u32[]{:S(2)}) collective-permute-start(f32[48,32,128]{2,0,1:T(8,128)S(1)} %fusion.180), channel_id=1, source_target_pairs={{0,128},{128,256},{256,384},{1,129},{129,257},{257,385},{2,130},{1... | collective-permute-start | bytes 2359304 | tf_op jit(solution)/shard_map/while/body/eval_jaxpr/ppermute | solution.py:28
  428.4 32.8 %collective-permute-start.5 = (f32[48,32,128]{2,0,1:T(8,128)S(1)}, f32[48,32,128]{2,0,1:T(8,128)}, u32[]{:S(2)}, u32[]{:S(2)}) collective-permute-start(f32[48,32,128]{2,0,1:T(8,128)S(1)} %copy.50), channel_id=1, source_target_pairs={{0,128},{128,256},{256,384},{1,129},{129,257},{257,385},{2,130},{1... | collective-permute-start | bytes 2359304 | tf_op jit(solution)/shard_map/while/body/eval_jaxpr/ppermute | solution.py:28
  441.5 13.3 %collective-permute-start.3 = (f32[48,34,1]{0,2,1:T(1,128)S(1)}, f32[48,34,1]{0,2,1:T(1,128)S(1)}, u32[]{:S(2)}, u32[]{:S(2)}) collective-permute-start(f32[48,34,1]{0,2,1:T(1,128)S(1)} %copy.31), channel_id=1, source_target_pairs={{1,0},{2,1},{3,2},{4,3},{5,4},{6,5},{7,6},{8,7},{9,8},{10,9},{11,1... | collective-permute-start | bytes 19592 | tf_op jit(solution)/shard_map/while/body/eval_jaxpr/ppermute | solution.py:20
  445.1 9.3 %collective-permute-start.2 = (f32[48,34,1]{0,2,1:T(1,128)S(1)}, f32[48,34,1]{0,2,1:T(1,128)S(1)}, u32[]{:S(2)}, u32[]{:S(2)}) collective-permute-start(f32[48,34,1]{0,2,1:T(1,128)S(1)} %copy.29), channel_id=1, source_target_pairs={{0,1},{1,2},{2,3},{3,4},{4,5},{5,6},{6,7},{7,8},{8,9},{9,10},{10,1... | collective-permute-start | bytes 19592 | tf_op jit(solution)/shard_map/while/body/eval_jaxpr/ppermute | solution.py:19
  455.9 19.0 %collective-permute-start.4 = (f32[48,32,128]{2,0,1:T(8,128)S(1)}, f32[48,32,128]{2,0,1:T(8,128)S(1)}, u32[]{:S(2)}, u32[]{:S(2)}) collective-permute-start(f32[48,32,128]{2,0,1:T(8,128)S(1)} %fusion.180), channel_id=1, source_target_pairs={{0,128},{128,256},{256,384},{1,129},{129,257},{257,385},{2,130},{1... | collective-permute-start | bytes 2359304 | tf_op jit(solution)/shard_map/while/body/eval_jaxpr/ppermute | solution.py:28
  480.6 31.0 %collective-permute-start.5 = (f32[48,32,128]{2,0,1:T(8,128)S(1)}, f32[48,32,128]{2,0,1:T(8,128)}, u32[]{:S(2)}, u32[]{:S(2)}) collective-permute-start(f32[48,32,128]{2,0,1:T(8,128)S(1)} %copy.50), channel_id=1, source_target_pairs={{0,128},{128,256},{256,384},{1,129},{129,257},{257,385},{2,130},{1... | collective-permute-start | bytes 2359304 | tf_op jit(solution)/shard_map/while/body/eval_jaxpr/ppermute | solution.py:28
  493.6 11.6 %collective-permute-start.3 = (f32[48,34,1]{0,2,1:T(1,128)S(1)}, f32[48,34,1]{0,2,1:T(1,128)S(1)}, u32[]{:S(2)}, u32[]{:S(2)}) collective-permute-start(f32[48,34,1]{0,2,1:T(1,128)S(1)} %copy.31), channel_id=1, source_target_pairs={{1,0},{2,1},{3,2},{4,3},{5,4},{6,5},{7,6},{8,7},{9,8},{10,9},{11,1... | collective-permute-start | bytes 19592 | tf_op jit(solution)/shard_map/while/body/eval_jaxpr/ppermute | solution.py:20
  506.3 19.2 %collective-permute-start.4 = (f32[48,32,128]{2,0,1:T(8,128)S(1)}, f32[48,32,128]{2,0,1:T(8,128)S(1)}, u32[]{:S(2)}, u32[]{:S(2)}) collective-permute-start(f32[48,32,128]{2,0,1:T(8,128)S(1)} %fusion.180), channel_id=1, source_target_pairs={{0,128},{128,256},{256,384},{1,129},{129,257},{257,385},{2,130},{1... | collective-permute-start | bytes 2359304 | tf_op jit(solution)/shard_map/while/body/eval_jaxpr/ppermute | solution.py:28
  531.2 31.8 %collective-permute-start.5 = (f32[48,32,128]{2,0,1:T(8,128)S(1)}, f32[48,32,128]{2,0,1:T(8,128)}, u32[]{:S(2)}, u32[]{:S(2)}) collective-permute-start(f32[48,32,128]{2,0,1:T(8,128)S(1)} %copy.50), channel_id=1, source_target_pairs={{0,128},{128,256},{256,384},{1,129},{129,257},{257,385},{2,130},{1... | collective-permute-start | bytes 2359304 | tf_op jit(solution)/shard_map/while/body/eval_jaxpr/ppermute | solution.py:28
  544.1 12.7 %collective-permute-start.3 = (f32[48,34,1]{0,2,1:T(1,128)S(1)}, f32[48,34,1]{0,2,1:T(1,128)S(1)}, u32[]{:S(2)}, u32[]{:S(2)}) collective-permute-start(f32[48,34,1]{0,2,1:T(1,128)S(1)} %copy.31), channel_id=1, source_target_pairs={{1,0},{2,1},{3,2},{4,3},{5,4},{6,5},{7,6},{8,7},{9,8},{10,9},{11,1... | collective-permute-start | bytes 19592 | tf_op jit(solution)/shard_map/while/body/eval_jaxpr/ppermute | solution.py:20
  557.9 19.0 %collective-permute-start.4 = (f32[48,32,128]{2,0,1:T(8,128)S(1)}, f32[48,32,128]{2,0,1:T(8,128)S(1)}, u32[]{:S(2)}, u32[]{:S(2)}) collective-permute-start(f32[48,32,128]{2,0,1:T(8,128)S(1)} %fusion.180), channel_id=1, source_target_pairs={{0,128},{128,256},{256,384},{1,129},{129,257},{257,385},{2,130},{1... | collective-permute-start | bytes 2359304 | tf_op jit(solution)/shard_map/while/body/eval_jaxpr/ppermute | solution.py:28
  582.6 34.7 %collective-permute-start.5 = (f32[48,32,128]{2,0,1:T(8,128)S(1)}, f32[48,32,128]{2,0,1:T(8,128)}, u32[]{:S(2)}, u32[]{:S(2)}) collective-permute-start(f32[48,32,128]{2,0,1:T(8,128)S(1)} %copy.50), channel_id=1, source_target_pairs={{0,128},{128,256},{256,384},{1,129},{129,257},{257,385},{2,130},{1... | collective-permute-start | bytes 2359304 | tf_op jit(solution)/shard_map/while/body/eval_jaxpr/ppermute | solution.py:28
  595.5 15.4 %collective-permute-start.3 = (f32[48,34,1]{0,2,1:T(1,128)S(1)}, f32[48,34,1]{0,2,1:T(1,128)S(1)}, u32[]{:S(2)}, u32[]{:S(2)}) collective-permute-start(f32[48,34,1]{0,2,1:T(1,128)S(1)} %copy.31), channel_id=1, source_target_pairs={{1,0},{2,1},{3,2},{4,3},{5,4},{6,5},{7,6},{8,7},{9,8},{10,9},{11,1... | collective-permute-start | bytes 19592 | tf_op jit(solution)/shard_map/while/body/eval_jaxpr/ppermute | solution.py:20
  601.2 9.4 %collective-permute-start.2 = (f32[48,34,1]{0,2,1:T(1,128)S(1)}, f32[48,34,1]{0,2,1:T(1,128)S(1)}, u32[]{:S(2)}, u32[]{:S(2)}) collective-permute-start(f32[48,34,1]{0,2,1:T(1,128)S(1)} %copy.29), channel_id=1, source_target_pairs={{0,1},{1,2},{2,3},{3,4},{4,5},{5,6},{6,7},{7,8},{8,9},{9,10},{10,1... | collective-permute-start | bytes 19592 | tf_op jit(solution)/shard_map/while/body/eval_jaxpr/ppermute | solution.py:19
  612.0 19.2 %collective-permute-start.4 = (f32[48,32,128]{2,0,1:T(8,128)S(1)}, f32[48,32,128]{2,0,1:T(8,128)S(1)}, u32[]{:S(2)}, u32[]{:S(2)}) collective-permute-start(f32[48,32,128]{2,0,1:T(8,128)S(1)} %fusion.180), channel_id=1, source_target_pairs={{0,128},{128,256},{256,384},{1,129},{129,257},{257,385},{2,130},{1... | collective-permute-start | bytes 2359304 | tf_op jit(solution)/shard_map/while/body/eval_jaxpr/ppermute | solution.py:28
  (63 other events, 519.7 us)
where the time goes:
time: 643 us; the launch traced here: 638 us
  starting transfers between devices  192 us (30%)
  waiting for transfers between devices  179 us (28%)
  between operations  89.2 us (14%)
  other arithmetic  65 us (10%)
  matrix products  64.4 us (10%)
  local copies, waits for them, and re-layouts  46.4 us (7%)
    ppermute x18, waiting for transfers between devices, from_behind(): lax.ppermute(value, axis, [(source, source + steps) for source in range(i...  123 us
    ppermute x18, starting transfers between devices, with_halo(): before = lax.ppermute(last, axis, up)  69.1 us
    ppermute x18, starting transfers between devices, with_halo(): after = lax.ppermute(initial, axis, down)  62.7 us
    ppermute x18, starting transfers between devices, from_behind(): lax.ppermute(value, axis, [(source, source + steps) for source in range(i...  60.3 us
    dot_general x27, matrix products, along_depth(): jnp.einsum('ij,jxy->ixy', matrix, field, precision=lax.Precision.HIGHEST)  43.8 us
    ppermute x18, waiting for transfers between devices, with_halo(): before = lax.ppermute(last, axis, up)  39.1 us
    broadcast_in_dim x3, other arithmetic, vertical(): lax.linalg.tridiagonal_solve(lower_band, 1.0 + diagonal, upper_band, eye)  30.3 us
    div x1, other arithmetic, vertical(): lax.linalg.tridiagonal_solve(lower_band, 1.0 + diagonal, upper_band, eye)  22.7 us
  transfers between devices with their start and end apart: 54, of which 27 were waited for; matrix products, arithmetic and copies ran while one was open for 9% of the time, Pallas kernels for 0%

commit v1 on v0

v1 whole, which is shorter than its diff:
```python
import functools

import jax
import jax.numpy as jnp
from jax import lax
from jax.experimental import pallas as pl
from jax.experimental.pallas import tpu as pltpu
from jax.sharding import PartitionSpec as P

NZ = 48
STEPS = 6
NLAYER = 6
NPULSE = 8
LEVELS = 4
POWERS = STEPS + LEVELS
HALO = POWERS - 1
ROWS = 32
LANES = 128
EXT = ROWS + 2 * HALO
ZS = NZ + 8
PER_TILE = LANES // HALO
TILES = -(-EXT // PER_TILE)
DEPTH = 1152
VMEM = 48 * 1024 * 1024
F32, BF16 = jnp.float32, jnp.bfloat16


def split(x):
    high = x.astype(BF16)
    return high, (x - high.astype(F32)).astype(BF16)


def edge_rows(u_ref, top_ref, bottom_ref):
    for i in range(HALO):
        top_ref[i] = u_ref[pl.ds(i, NZ, stride=ROWS), :]
        bottom_ref[i] = u_ref[pl.ds(ROWS - HALO + i, NZ, stride=ROWS), :]


def ext_row(r, u_ref, above_ref, below_ref):
    if r < HALO:
        return above_ref[r]
    if r < HALO + ROWS:
        return u_ref[pl.ds(r - HALO, NZ, stride=ROWS), :]
    return below_ref[r - HALO - ROWS]


def edge_columns(place_ref, u_ref, above_ref, below_ref, packed_ref):
    lane = lax.broadcasted_iota(jnp.int32, (NZ, LANES), 1)
    from_right = jnp.where(place_ref[0] >= 2, HALO, 0)
    for t in range(TILES):
        tile = jnp.zeros((NZ, LANES), F32)
        for s in range(min(PER_TILE, EXT - t * PER_TILE)):
            row = ext_row(t * PER_TILE + s, u_ref, above_ref, below_ref)
            row = pltpu.roll(row, HALO * s + from_right, axis=1)
            tile = jnp.where((lane >= HALO * s) & (lane < HALO * (s + 1)), row, tile)
        packed_ref[t] = tile


def sources(place_ref, rates_ref, plan_ref, x_ref, y_ref, centre_ref, side_ref):
    bores = plan_ref.shape[1]
    plan = plan_ref[...]
    rate = jnp.zeros(plan.shape, F32)
    for j in range(NPULSE):
        rate = jnp.where(plan == j, rates_ref[j], rate)
    rate_high = rate.astype(BF16).astype(F32)
    rate_low = rate - rate_high
    cell_x = place_ref[1] * ROWS - HALO + lax.broadcasted_iota(jnp.int32, (ZS, bores), 0)
    hit_x = x_ref[...] == cell_x
    cell_y = lax.broadcasted_iota(jnp.int32, (2 * LANES, bores), 0)
    cell_y = jnp.where(cell_y >= LANES + LANES // 2, cell_y - 2 * LANES, cell_y)
    hit_y = (y_ref[...] == cell_y + place_ref[2] * LANES).astype(F32).astype(BF16)

    def plane(rates):
        left = [jnp.where(hit_x, rates[m : m + 1], 0.0) for m in range(STEPS + 1)]
        left = jnp.concatenate(left, axis=0).astype(BF16)
        return lax.dot_general(left, hit_y, (((1,), (1,)), ((), ())), preferred_element_type=F32)

    both = plane(rate_high) + plane(rate_low)
    for m in range(STEPS + 1):
        rows = both[m * ZS : (m + 1) * ZS]
        centre_ref[pl.ds(m, ZS, stride=8), :] = rows[:, :LANES]
        side_ref[pl.ds(m, ZS, stride=8), :] = rows[:, LANES:]
    blank = jnp.zeros((ZS, LANES), F32)
    centre_ref[pl.ds(7, ZS, stride=8), :] = blank
    side_ref[pl.ds(7, ZS, stride=8), :] = blank


def coefs(place_ref, lateral_ref, vertical_ref, ids_ref, out_ref, poly_ref, final_ref):
    ids = jnp.broadcast_to(ids_ref[...], (8, LANES))
    lane = lax.broadcasted_iota(jnp.int32, (8, LANES), 1)
    cond, lat = jnp.zeros((8, LANES), F32), jnp.zeros((8, LANES), F32)
    for j in range(NLAYER):
        cond = jnp.where(ids == j, vertical_ref[j], cond)
        lat = jnp.where(ids == j, lateral_ref[j], lat)
    cond = jnp.where(lane < NZ, cond, 1.0)
    lat = jnp.where(lane < NZ, lat, 0.0)
    after = pltpu.roll(cond, LANES - 1, axis=1)
    link = jnp.where(lane < NZ - 1, 2.0 * cond * after / (cond + after), 0.0)
    before = pltpu.roll(link, 1, axis=1)
    low, up = -before, -link
    mid = 1.0 + (jnp.where(lane == 0, cond, 0.0) + link + before)
    mid = jnp.where(lane < NZ, mid, 1.0)
    row_id = lax.broadcasted_iota(jnp.int32, (NZ, LANES), 0)
    lane_id = lax.broadcasted_iota(jnp.int32, (NZ, LANES), 1)
    rhs = (row_id == lane_id).astype(F32)
    wide = lambda v: jnp.broadcast_to(v[:1], (NZ, LANES))
    for s in (1, 2, 4, 8, 16, 32):
        back = lambda v: pltpu.roll(v, s, axis=1)
        forth = lambda v: pltpu.roll(v, LANES - s, axis=1)
        alpha = -low / back(mid)
        gamma = -up / forth(mid)
        rhs = rhs + wide(alpha) * back(rhs) + wide(gamma) * forth(rhs)
        mid = mid + alpha * back(up) + gamma * forth(low)
        low, up = alpha * back(low), gamma * forth(up)
    inverse = rhs / wide(mid)
    inverse = jnp.concatenate([inverse, jnp.zeros((LANES - NZ, LANES), F32)], axis=0)
    high = inverse.astype(BF16).astype(F32)
    weights = high + pltpu.roll(inverse - high, 64, axis=1)
    weights = jnp.concatenate([weights, high], axis=0).astype(BF16)

    def solve(blocks):
        high, low = split(jnp.concatenate(blocks, axis=0))
        both = jnp.dot(jnp.concatenate([high, low], axis=1), weights, preferred_element_type=F32)
        return both + pltpu.roll(both, 64, axis=1)

    row_id = lax.broadcasted_iota(jnp.int32, (ZS, LANES), 0)
    lane_id = lax.broadcasted_iota(jnp.int32, (ZS, LANES), 1)
    eye = ((row_id == lane_id) & (row_id < NZ)).astype(F32)
    profile = (lane_id >= 2) & (lane_id < NZ - 4)
    source = [((row_id == NZ + n) & profile).astype(F32) for n in range(STEPS + 1)]
    slope = jnp.broadcast_to(lat[:1], (ZS, LANES))
    stay = 1.0 - 4.0 * slope

    degree = lambda p, n: 0 if n == 0 else n + p

    def get(p, n, k):
        if k > degree(p, n):
            return None
        return eye if n == 0 else poly_ref[p, n, k * ZS : (k + 1) * ZS, :]

    def total(*terms):
        terms = [(f, t) for f, t in terms if t is not None]
        result = None
        for f, t in terms:
            t = t if f in (1.0, -1.0) else f * t
            if result is None:
                result = -t if f == -1.0 else t
            else:
                result = result - t if f == -1.0 else result + t
        return result

    def step(p, n):
        count = degree(p, n + 1) + 1
        blocks, rest, last = [], [], None
        for k in range(count):
            if p == 0:
                g = get(0, n, k)
                tail, add = None, source[n]
            else:
                b, c = get(p - 1, n, k), get(p - 1, n + 1, k)
                if n == 0:
                    w = total((0.5, b), (0.5, c))
                    g, add = w, 0.5 * source[0] + 0.5 * source[1]
                else:
                    w = total((-1.0 / 12.0, get(p - 1, n - 1, k)), (8.0 / 12.0, b), (5.0 / 12.0, c))
                    g = total((1.0, get(p, n, k)), (-1.0, b), (1.0, w))
                    add = (-source[n - 1] + 8.0 * source[n] + 5.0 * source[n + 1]) * (1.0 / 12.0)
                tail = total((1.0, b), (-1.0, c))
                rest.append(total((1.0, c), (-1.0, w)))
            parts = [
                (1.0, None if g is None else stay * g),
                (1.0, None if last is None else slope * last),
                (1.0, tail),
                (1.0, add if k == 0 else None),
            ]
            blocks.append(total(*parts))
            last = g
        solved = solve(blocks)
        for k in range(count):
            block = solved[k * ZS : (k + 1) * ZS]
            if p > 0 and rest[k] is not None:
                block = block + rest[k]
            poly_ref[p, n + 1, k * ZS : (k + 1) * ZS, :] = block

    for p in range(LEVELS):
        first = (degree(p, STEPS) + 1) * ZS
        if first < POWERS * ZS:
            poly_ref[p, STEPS, first:, :] = jnp.zeros((POWERS * ZS - first, LANES), F32)
    for wave in range(STEPS + LEVELS - 1):
        for p in range(LEVELS):
            if 0 <= wave - p < STEPS:
                step(p, wave - p)

    level = place_ref[0]
    for k in range(POWERS):
        block = poly_ref[level, STEPS, k * ZS : (k + 1) * ZS, :]
        final_ref[2 * k * ZS : (2 * k + 1) * ZS, :] = block
        final_ref[(2 * k + 1) * ZS : (2 * k + 2) * ZS, :] = block
    final_ref[2 * POWERS * ZS :, :] = jnp.zeros((DEPTH - 2 * POWERS * ZS, LANES), F32)
    table = final_ref[...].T[:NZ]
    high = table.astype(BF16).astype(F32)
    out_ref[...] = jnp.concatenate([high, table - high], axis=0).astype(BF16)


def evolve(
    place_ref, u_ref, above_ref, below_ref, own_ref, other_ref, src_centre_ref, src_side_ref, coef_ref,
    out_ref, centre_ref, side_ref, terms_ref,
):
    level, tx, ty = place_ref[0], place_ref[1], place_ref[2]
    lane = lax.broadcasted_iota(jnp.int32, (ZS, LANES), 1)
    lane_z = lax.broadcasted_iota(jnp.int32, (NZ, LANES), 1)
    low_level = level < 2
    for t in range(TILES):
        own, other = own_ref[t], other_ref[t]
        left = jnp.where(low_level, own, other)
        right = jnp.where(low_level, other, own)
        for s in range(min(PER_TILE, EXT - t * PER_TILE)):
            r = t * PER_TILE + s
            from_right = pltpu.roll(right, (LANES - HALO * s) % LANES, axis=1)
            from_left = pltpu.roll(left, (LANES - HALO * s - HALO) % LANES, axis=1)
            side_ref[0, r, :NZ, :] = jnp.where(lane_z < LANES // 2, from_right, from_left)
            centre_ref[0, r, :NZ, :] = ext_row(r, u_ref, above_ref, below_ref)
            centre_ref[0, r, NZ:, :] = src_centre_ref[8 * r : 8 * r + 8, :]
            side_ref[0, r, NZ:, :] = src_side_ref[8 * r : 8 * r + 8, :]

    def keep_terms(k, pair, half, c):
        high = c.astype(BF16).astype(F32)
        both = jnp.concatenate([high, c - high], axis=0).astype(BF16)
        terms_ref[pair, 2 * k * ZS : 2 * (k + 1) * ZS, half * LANES : (half + 1) * LANES] = both

    @pl.loop(0, ROWS // 2)
    def _(pair):
        terms_ref[pair, 2 * POWERS * ZS :, :] = jnp.zeros((DEPTH - 2 * POWERS * ZS, 2 * LANES), BF16)
        for half in range(2):
            keep_terms(0, pair, half, centre_ref[0, HALO + 2 * pair + half])

    last_x, last_y = place_ref[3], place_ref[4]
    inside = ((lane >= LANES // 2) | (ty < last_y)) & ((lane < LANES // 2) | (ty > 0))
    inside = inside.astype(F32)
    above_in = jnp.where(tx > 0, 1.0, 0.0)
    below_in = jnp.where(tx < last_x, 1.0, 0.0)
    first_lane, last_lane = lane == 0, lane == LANES - 1

    def neighbours(source, r):
        c, h = centre_ref[source, r], side_ref[source, r]
        c1, h1 = pltpu.roll(c, 1, axis=1), pltpu.roll(h, 1, axis=1)
        c2, h2 = pltpu.roll(c, LANES - 1, axis=1), pltpu.roll(h, LANES - 1, axis=1)
        new_c = centre_ref[source, r - 1] + centre_ref[source, r + 1]
        new_c += jnp.where(first_lane, h1, c1) + jnp.where(last_lane, h2, c2)
        new_h = side_ref[source, r - 1] + side_ref[source, r + 1]
        new_h += jnp.where(first_lane, c1, h1) + jnp.where(last_lane, c2, h2)
        return new_c, new_h * inside

    for k in range(1, POWERS):
        source, target = (k - 1) % 2, k % 2

        @pl.loop(0, ROWS // 2)
        def _(pair):
            for half in range(2):
                r = HALO + 2 * pair + half
                new_c, new_h = neighbours(source, r)
                centre_ref[target, r] = new_c
                side_ref[target, r] = new_h
                keep_terms(k, pair, half, new_c)

        if k < HALO:

            @pl.loop(k, HALO)
            def _(r):
                for row, there in ((r, above_in), (EXT - 1 - r, below_in)):
                    new_c, new_h = neighbours(source, row)
                    centre_ref[target, row] = new_c * there
                    side_ref[target, row] = new_h * there

    table = coef_ref[...]

    @pl.loop(0, ROWS // 2)
    def _(pair):
        both = jnp.dot(table, terms_ref[pair], preferred_element_type=F32)
        both = both[:NZ] + both[NZ:]
        out_ref[pl.ds(2 * pair, NZ, stride=ROWS), :] = both[:, :LANES]
        out_ref[pl.ds(2 * pair + 1, NZ, stride=ROWS), :] = both[:, LANES:]


SMEM = pl.BlockSpec(memory_space=pltpu.SMEM)
WHOLE = pl.BlockSpec(memory_space=pltpu.VMEM)


def call(kernel, name, ins, outs, scratch=(), cost=0):
    return pl.pallas_call(
        kernel,
        out_shape=outs,
        in_specs=ins,
        out_specs=jax.tree.map(lambda _: WHOLE, outs),
        scratch_shapes=list(scratch),
        compiler_params=pltpu.CompilerParams(vmem_limit_bytes=VMEM),
        cost_estimate=pl.CostEstimate(flops=cost, bytes_accessed=1 << 20, transcendentals=0),
        name=name,
    )


def on_device(initial, layer_ids, lateral_number, vertical_number, pulse_rates, bore_x, bore_y, plan):
    shape = lambda *s, dtype=F32: jax.ShapeDtypeStruct(s, dtype)
    count_x, count_y = lax.axis_size("tx"), lax.axis_size("ty")
    indices = [lax.axis_index(name) for name in ("level", "tx", "ty")]
    place = jnp.stack(indices + [jnp.int32(count_x - 1), jnp.int32(count_y - 1)])
    flat = initial.reshape(NZ * ROWS, LANES)
    slab = shape(HALO, NZ, LANES)
    top, bottom = call(edge_rows, "edge_rows", [WHOLE], (slab, slab))(flat)
    up = [(i, i + 1) for i in range(count_x - 1)]
    above = lax.ppermute(bottom, "tx", up)
    below = lax.ppermute(top, "tx", [(j, i) for i, j in up])
    strips = call(edge_columns, "edge_columns", [SMEM] + [WHOLE] * 3, shape(TILES, NZ, LANES))(
        place, flat, above, below
    )
    route = []
    for i in range(count_y - 1):
        for l in (0, 1):
            route.append(((l + 2) * count_y + i, l * count_y + i + 1))
            route.append((l * count_y + i + 1, (l + 2) * count_y + i))
    own = lax.ppermute(strips, ("level", "ty"), route)
    other = lax.ppermute(own, "level", [(0, 2), (2, 0), (1, 3), (3, 1)])

    planes = shape(ZS * 8, LANES)
    src_centre, src_side = call(sources, "sources", [SMEM] * 2 + [WHOLE] * 3, (planes, planes), cost=1 << 28)(
        place, pulse_rates, plan.T, bore_x[None, :], bore_y[None, :]
    )
    ids = jnp.pad(layer_ids, (0, LANES - NZ))[None, :]
    table = call(
        coefs,
        "coefs",
        [SMEM] * 3 + [WHOLE],
        shape(2 * NZ, DEPTH, dtype=BF16),
        [pltpu.VMEM((LEVELS, STEPS + 1, POWERS * ZS, LANES), F32), pltpu.VMEM((DEPTH, LANES), F32)],
        cost=1 << 28,
    )(place, lateral_number, vertical_number, ids)
    buffer = pltpu.VMEM((2, EXT, ZS, LANES), F32)
    result = call(
        evolve,
        "evolve",
        [SMEM] + [WHOLE] * 8,
        shape(NZ * ROWS, LANES),
        [buffer, buffer, pltpu.VMEM((ROWS // 2, DEPTH, 2 * LANES), BF16)],
    )(place, flat, above, below, own, other, src_centre, src_side, table)
    return result.reshape(1, NZ, ROWS, LANES)


def solution(mesh):
    return jax.shard_map(
        on_device,
        mesh=mesh,
        in_specs=(P(None, "tx", "ty"), P(), P(), P(), P(), P(), P(), P()),
        out_specs=P("level", None, "tx", "ty"),
        check_vma=False,
    )
```

time: 643 us -> 73.1 us (0.11)
  the two profiles are of different devices: /device:TPU:25 before, /device:TPU:26 now
where the time goes in v1:
time: 73.1 us; the launch traced here: 72.7 us
  Pallas kernels  40.8 us (56%)
  starting transfers between devices  19.5 us (27%)
  waiting for transfers between devices  10.4 us (14%)
  local copies, waits for them, and re-layouts  1.91 us (3%)
    pallas_call x1, Pallas kernels, on_device(): call(evolve, 'evolve', [SMEM] + [WHOLE] * 8, shape(NZ * ROWS, LANES), [bu...  34.1 us
    ppermute x1, starting transfers between devices, on_device(): own = lax.ppermute(strips, ('level', 'ty'), route)  12 us
    ppermute x1, waiting for transfers between devices, on_device(): own = lax.ppermute(strips, ('level', 'ty'), route)  4.61 us
    pallas_call x1, Pallas kernels, on_device(): call(coefs, 'coefs', [SMEM] * 3 + [WHOLE], shape(2 * NZ, DEPTH, dtype=BF1...  4.06 us
    ppermute x1, starting transfers between devices, on_device(): below = lax.ppermute(top, 'tx', [(j, i) for i, j in up])  3.64 us
    ppermute x1, waiting for transfers between devices, on_device(): other = lax.ppermute(own, 'level', [(0, 2), (2, 0), (1, 3), (3, 1)])  2.43 us
    ppermute x1, starting transfers between devices, on_device(): above = lax.ppermute(bottom, 'tx', up)  1.92 us
    ppermute x1, starting transfers between devices, on_device(): other = lax.ppermute(own, 'level', [(0, 2), (2, 0), (1, 3), (3, 1)])  1.91 us
  transfers between devices with their start and end apart: 4, of which 4 were waited for; matrix products, arithmetic and copies ran while one was open for 0% of the time, Pallas kernels for 7%

profile of v1, /device:TPU:26, one launch (start us, length us, event | category | flops | bytes accessed | tf_op | source)
XLA Modules:
  0.0 72.7 jit_solution(6425601458596726034)
XLA Ops:
  0.0 0.0 copy-start
  0.0 1.1 %copy-done = f32[48,32,128]{2,1,0:T(8,128)S(1)} copy-done((f32[48,32,128]{2,1,0:T(8,128)S(1)}, f32[48,32,128]{2,1,0:T(8,128)}, u32[]{:S(2)}) %copy-start) | copy-done | bytes 786456
  1.1 0.0 copy-start.1
  1.1 0.3 edge_rows.1
  1.4 1.9 %collective-permute-start = (f32[9,48,128]{2,1,0:T(8,128)S(1)}, f32[9,48,128]{2,1,0:T(8,128)S(1)}, u32[]{:S(2)}, u32[]{:S(2)}) collective-permute-start(f32[9,48,128]{2,1,0:T(8,128)S(1)} %get-tuple-element.9), channel_id=1, source_target_pairs={{0,16},{16,32},{32,48},{48,64},{64,80},{80,96},{96,112},{1,17},{17... | collective-permute-start | bytes 663560 | tf_op jit(solution)/shard_map/ppermute | solution.py:311
  3.3 3.6 %collective-permute-start.1 = (f32[9,48,128]{2,1,0:T(8,128)S(1)}, f32[9,48,128]{2,1,0:T(8,128)S(1)}, u32[]{:S(2)}, u32[]{:S(2)}) collective-permute-start(f32[9,48,128]{2,1,0:T(8,128)S(1)} %get-tuple-element.10), channel_id=1, source_target_pairs={{16,0},{32,16},{48,32},{64,48},{80,64},{96,80},{112,96},{17,1},{33... | collective-permute-start | bytes 663560 | tf_op jit(solution)/shard_map/ppermute | solution.py:312
  7.0 0.1 stack.15.place_ref
  7.1 0.0 copy-start.8
  7.1 1.6 %collective-permute-done.above_ref = f32[9,48,128]{2,1,0:T(8,128)S(1)} collective-permute-done((f32[9,48,128]{2,1,0:T(8,128)S(1)}, f32[9,48,128]{2,1,0:T(8,128)S(1)}, u32[]{:S(2)}, u32[]{:S(2)}) %collective-permute-start) | collective-permute-done | bytes 221216 | tf_op jit(solution)/shard_map/ppermute | solution.py:311
  8.7 1.8 %collective-permute-done.1.below_ref = f32[9,48,128]{2,1,0:T(8,128)S(1)} collective-permute-done((f32[9,48,128]{2,1,0:T(8,128)S(1)}, f32[9,48,128]{2,1,0:T(8,128)S(1)}, u32[]{:S(2)}, u32[]{:S(2)}) %collective-permute-start.1) | collective-permute-done | bytes 221216 | tf_op jit(solution)/shard_map/ppermute | solution.py:312
  10.4 0.0 copy-done.1
  10.4 1.2 %edge_columns.1 = f32[4,48,128]{2,1,0:T(8,128)S(1)} custom-call(s32[5]{0:T(128)S(1)} %stack.15.place_ref, f32[1536,128]{1,0:T(8,128)S(1)} %bitcast.11, f32[9,48,128]{2,1,0:T(8,128)S(1)} %collective-permute-done.above_ref, f32[9,48,128]{2,1,0:T(8,128)S(1)} %collective-permute-done.1.below_ref), custom_call_target="tpu_custom_call" | custom-call | bytes 1048576 | tf_op jit(solution)/shard_map/edge_columns/pallas_call | solution.py:313
  11.6 0.0 copy-start.5
  11.7 0.0 copy-start.6
  11.7 12.0 %collective-permute-start.2 = (f32[4,48,128]{2,1,0:T(8,128)S(1)}, f32[4,48,128]{2,1,0:T(8,128)S(1)}, u32[]{:S(2)}, u32[]{:S(2)}) collective-permute-start(f32[4,48,128]{2,1,0:T(8,128)S(1)} %edge_columns.1), channel_id=1, source_target_pairs={{256,1},{1,256},{384,129},{129,384},{257,2},{2,257},{385,130},{130... | collective-permute-start | bytes 294920 | tf_op jit(solution)/shard_map/ppermute | solution.py:321
  23.7 4.6 %collective-permute-done.2.own_ref = f32[4,48,128]{2,1,0:T(8,128)S(1)} collective-permute-done((f32[4,48,128]{2,1,0:T(8,128)S(1)}, f32[4,48,128]{2,1,0:T(8,128)S(1)}, u32[]{:S(2)}, u32[]{:S(2)}) %collective-permute-start.2) | collective-permute-done | bytes 98336 | tf_op jit(solution)/shard_map/ppermute | solution.py:321
  28.3 1.9 %collective-permute-start.3 = (f32[4,48,128]{2,1,0:T(8,128)S(1)}, f32[4,48,128]{2,1,0:T(8,128)S(1)}, u32[]{:S(2)}, u32[]{:S(2)}) collective-permute-start(f32[4,48,128]{2,1,0:T(8,128)S(1)} %collective-permute-done.2.own_ref), channel_id=1, source_target_pairs={{0,256},{256,0},{128,384},{384,128},{1,257},{257,1},{129,385},{385... | collective-permute-start | bytes 294920 | tf_op jit(solution)/shard_map/ppermute | solution.py:322
  30.2 0.0 copy-done.8
  30.3 0.0 copy-done.5
  30.3 0.0 copy-done.6
  30.3 0.0 copy-start.2
  30.3 0.0 copy-start.4
  30.3 4.1 %coefs.1.coef_ref = bf16[96,1152]{1,0:T(8,128)(2,1)S(1)} custom-call(s32[5]{0:T(128)S(1)} %stack.15.place_ref, f32[6]{0:T(128)S(1)} %copy-done.5, f32[6]{0:T(128)S(1)} %copy-done.6, s32[1,128]{1,0:T(1,128)S(1)} %pad_bitcast_fusion.ids_ref), custom_call_target="tpu_custom_call" | custom-call | flops 268435456 | bytes 1048576 | tf_op jit(solution)/shard_map/coefs/pallas_call | solution.py:329
  34.4 0.0 copy-start.3
  34.4 0.0 copy-start.7
  34.4 0.0 copy-done.2
  34.4 0.0 copy-done.4
  34.4 0.6 copy-done.3
  35.1 0.0 copy-done.7
  35.1 1.2 %sources.1 = (f32[448,128]{1,0:T(8,128)S(1)}, f32[448,128]{1,0:T(8,128)S(1)}) custom-call(s32[5]{0:T(128)S(1)} %stack.15.place_ref, f32[8]{0:T(128)S(1)} %copy-done.7, s32[7,1024]{1,0:T(8,128)S(1)} %bitcast.13, s32[1,1024]{1,0:T(1,128)S(1)} %bitcast.14, s32[1,1024]{1,0:T(1,128)S(1)} %bitcast.15), custom_call_target="tpu_custom_call" | custom-call | flops 268435456 | bytes 1048576 | tf_op jit(solution)/shard_map/sources/pallas_call | solution.py:325
  36.2 2.4 %collective-permute-done.3.other_ref = f32[4,48,128]{2,1,0:T(8,128)S(1)} collective-permute-done((f32[4,48,128]{2,1,0:T(8,128)S(1)}, f32[4,48,128]{2,1,0:T(8,128)S(1)}, u32[]{:S(2)}, u32[]{:S(2)}) %collective-permute-start.3) | collective-permute-done | bytes 98336 | tf_op jit(solution)/shard_map/ppermute | solution.py:322
  38.7 34.1 %evolve.1 = f32[1536,128]{1,0:T(8,128)} custom-call(s32[5]{0:T(128)S(1)} %stack.15.place_ref, f32[1536,128]{1,0:T(8,128)S(1)} %bitcast.12, f32[9,48,128]{2,1,0:T(8,128)S(1)} %collective-permute-done.above_ref, f32[9,48,128]{2,1,0:T(8,128)S(1)} %collective-permute-done.1.below_ref, f32[4,48,128]{2,1,0:T(8,128)S(1)} %collective-permute-done.2.own_ref, ...), custom_call_target="tpu_custom_call" | custom-call | bytes 1048576 | tf_op jit(solution)/shard_map/evolve/pallas_call | solution.py:338
  (1 shorter events, 0.0 us)
Async XLA Ops:
  0.0 1.1 %copy-start = (f32[48,32,128]{2,1,0:T(8,128)S(1)}, f32[48,32,128]{2,1,0:T(8,128)}, u32[]{:S(2)}) copy-start(f32[48,32,128]{2,1,0:T(8,128)} %param.8) | copy-start | bytes 2359300
  1.1 9.3 %copy-start.1 = (f32[48,32,128]{2,1,0:T(8,128)S(1)}, f32[48,32,128]{2,1,0:T(8,128)}, u32[]{:S(2)}) copy-start(f32[48,32,128]{2,1,0:T(8,128)} %param.8) | copy-start | bytes 2359300
  1.4 7.3 %collective-permute-start = (f32[9,48,128]{2,1,0:T(8,128)S(1)}, f32[9,48,128]{2,1,0:T(8,128)S(1)}, u32[]{:S(2)}, u32[]{:S(2)}) collective-permute-start(f32[9,48,128]{2,1,0:T(8,128)S(1)} %get-tuple-element.9), channel_id=1, source_target_pairs={{0,16},{16,32},{32,48},{48,64},{64,80},{80,96},{96,112},{1,17},{17... | collective-permute-start | bytes 663560 | tf_op jit(solution)/shard_map/ppermute | solution.py:311
  3.3 7.1 %collective-permute-start.1 = (f32[9,48,128]{2,1,0:T(8,128)S(1)}, f32[9,48,128]{2,1,0:T(8,128)S(1)}, u32[]{:S(2)}, u32[]{:S(2)}) collective-permute-start(f32[9,48,128]{2,1,0:T(8,128)S(1)} %get-tuple-element.10), channel_id=1, source_target_pairs={{16,0},{32,16},{48,32},{64,48},{80,64},{96,80},{112,96},{17,1},{33... | collective-permute-start | bytes 663560 | tf_op jit(solution)/shard_map/ppermute | solution.py:312
  7.1 23.2 %copy-start.8 = (s32[48]{0:T(128)S(1)}, s32[48]{0:T(128)}, u32[]{:S(2)}) copy-start(s32[48]{0:T(128)} %param.9) | copy-start | bytes 580
  11.6 18.6 %copy-start.5 = (f32[6]{0:T(128)S(1)}, f32[6]{0:T(128)}, u32[]{:S(2)}) copy-start(f32[6]{0:T(128)} %lateral_ref.1) | copy-start | bytes 76
  11.7 18.6 %copy-start.6 = (f32[6]{0:T(128)S(1)}, f32[6]{0:T(128)}, u32[]{:S(2)}) copy-start(f32[6]{0:T(128)} %vertical_ref.1) | copy-start | bytes 76
  11.7 16.6 %collective-permute-start.2 = (f32[4,48,128]{2,1,0:T(8,128)S(1)}, f32[4,48,128]{2,1,0:T(8,128)S(1)}, u32[]{:S(2)}, u32[]{:S(2)}) collective-permute-start(f32[4,48,128]{2,1,0:T(8,128)S(1)} %edge_columns.1), channel_id=1, source_target_pairs={{256,1},{1,256},{384,129},{129,384},{257,2},{2,257},{385,130},{130... | collective-permute-start | bytes 294920 | tf_op jit(solution)/shard_map/ppermute | solution.py:321
  28.3 10.4 %collective-permute-start.3 = (f32[4,48,128]{2,1,0:T(8,128)S(1)}, f32[4,48,128]{2,1,0:T(8,128)S(1)}, u32[]{:S(2)}, u32[]{:S(2)}) collective-permute-start(f32[4,48,128]{2,1,0:T(8,128)S(1)} %collective-permute-done.2.own_ref), channel_id=1, source_target_pairs={{0,256},{256,0},{128,384},{384,128},{1,257},{257,1},{129,385},{385... | collective-permute-start | bytes 294920 | tf_op jit(solution)/shard_map/ppermute | solution.py:322
  30.3 4.1 %copy-start.2 = (s32[1024,7]{0,1:T(8,128)S(1)}, s32[1024,7]{0,1:T(8,128)}, u32[]{:S(2)}) copy-start(s32[1024,7]{0,1:T(8,128)} %param.15) | copy-start | bytes 86020
  30.3 4.1 %copy-start.4 = (s32[1024]{0:T(1024)S(1)}, s32[1024]{0:T(1024)}, u32[]{:S(2)}) copy-start(s32[1024]{0:T(1024)} %param.14) | copy-start | bytes 12292
  34.4 0.7 copy-start.3
  34.4 0.7 copy-start.7

commit v2 on v1

--- a/solution.py
+++ b/solution.py
@@ -1,7 +1,6 @@
-import functools
-
 import jax
 import jax.numpy as jnp
+import numpy as np
 from jax import lax
 from jax.experimental import pallas as pl
 from jax.experimental.pallas import tpu as pltpu
@@ -18,11 +17,33 @@
 LANES = 128
 EXT = ROWS + 2 * HALO
 ZS = NZ + 8
-PER_TILE = LANES // HALO
-TILES = -(-EXT // PER_TILE)
-DEPTH = 1152
+HALF = ROWS // 2
+PAIRS = HALF + 2 * HALO
+SLOT = LANES // 2
+BLOCKS = 8
+SPAN = -(-(LANES + 2 * HALO) // BLOCKS)
+WIDE = SPAN * BLOCKS
+CHUNK = 5
 VMEM = 48 * 1024 * 1024
 F32, BF16 = jnp.float32, jnp.bfloat16
+
+
+def pieces():
+    width = [HALO - max(HALO - r, r - (HALO + ROWS - 1), 0) for r in range(EXT)]
+    slots = [[r] for r in range(EXT) if width[r] == HALO]
+    for d in range(1, (HALO + 1) // 2):
+        slots.append([HALO - d, d])
+        slots.append([EXT - 1 - (HALO - d), EXT - 1 - d])
+    where, per_tile = {}, LANES // HALO
+    for n, rows in enumerate(slots):
+        lane = HALO * (n % per_tile)
+        for r in rows:
+            where[r] = (n // per_tile, lane, width[r])
+            lane += width[r]
+    return where, -(-len(slots) // per_tile)
+
+
+PIECES, TILES = pieces()
 
 
 def split(x):
@@ -46,46 +67,55 @@
 
 def edge_columns(place_ref, u_ref, above_ref, below_ref, packed_ref):
     lane = lax.broadcasted_iota(jnp.int32, (NZ, LANES), 1)
-    from_right = jnp.where(place_ref[0] >= 2, HALO, 0)
+    send_last = place_ref[0] >= 2
+    tiles = [jnp.zeros((NZ, LANES), F32) for _ in range(TILES)]
+    for r, (t, first, width) in PIECES.items():
+        row = ext_row(r, u_ref, above_ref, below_ref)
+        row = pltpu.roll(row, first + jnp.where(send_last, width, 0), axis=1)
+        tiles[t] = jnp.where((lane >= first) & (lane < first + width), row, tiles[t])
     for t in range(TILES):
-        tile = jnp.zeros((NZ, LANES), F32)
-        for s in range(min(PER_TILE, EXT - t * PER_TILE)):
-            row = ext_row(t * PER_TILE + s, u_ref, above_ref, below_ref)
-            row = pltpu.roll(row, HALO * s + from_right, axis=1)
-            tile = jnp.where((lane >= HALO * s) & (lane < HALO * (s + 1)), row, tile)
-        packed_ref[t] = tile
-
-
-def sources(place_ref, rates_ref, plan_ref, x_ref, y_ref, centre_ref, side_ref):
+        packed_ref[t] = tiles[t]
+
+
+def side_cells():
+    cells = np.full((3, TILES * LANES, 1), -(1 << 20), np.int32)
+    for r, (t, first, width) in PIECES.items():
+        for c in range(width):
+            cells[:, t * LANES + first + c, 0] = (r - HALO, c - width, LANES + c)
+    return cells
+
+
+def sources(place_ref, rates_ref, plan_ref, x_ref, y_ref, cells_ref, centre_ref, left_ref, right_ref):
     bores = plan_ref.shape[1]
     plan = plan_ref[...]
     rate = jnp.zeros(plan.shape, F32)
     for j in range(NPULSE):
         rate = jnp.where(plan == j, rates_ref[j], rate)
+    rate = jnp.concatenate([rate, jnp.zeros((1, bores), F32)], axis=0)
     rate_high = rate.astype(BF16).astype(F32)
     rate_low = rate - rate_high
-    cell_x = place_ref[1] * ROWS - HALO + lax.broadcasted_iota(jnp.int32, (ZS, bores), 0)
-    hit_x = x_ref[...] == cell_x
-    cell_y = lax.broadcasted_iota(jnp.int32, (2 * LANES, bores), 0)
-    cell_y = jnp.where(cell_y >= LANES + LANES // 2, cell_y - 2 * LANES, cell_y)
-    hit_y = (y_ref[...] == cell_y + place_ref[2] * LANES).astype(F32).astype(BF16)
+    x = x_ref[...] - place_ref[1] * ROWS
+    y = y_ref[...] - place_ref[2] * LANES
+    hit_x = x == lax.broadcasted_iota(jnp.int32, (ZS, bores), 0) - HALO
+    hit_y = (y == lax.broadcasted_iota(jnp.int32, (LANES, bores), 0)).astype(F32).astype(BF16)
+    contract = lambda p, q: lax.dot_general(p, q, (((1,), (1,)), ((), ())), preferred_element_type=F32)
 
     def plane(rates):
         left = [jnp.where(hit_x, rates[m : m + 1], 0.0) for m in range(STEPS + 1)]
-        left = jnp.concatenate(left, axis=0).astype(BF16)
-        return lax.dot_general(left, hit_y, (((1,), (1,)), ((), ())), preferred_element_type=F32)
+        return contract(jnp.concatenate(left, axis=0).astype(BF16), hit_y)
 
     both = plane(rate_high) + plane(rate_low)
     for m in range(STEPS + 1):
-        rows = both[m * ZS : (m + 1) * ZS]
-        centre_ref[pl.ds(m, ZS, stride=8), :] = rows[:, :LANES]
-        side_ref[pl.ds(m, ZS, stride=8), :] = rows[:, LANES:]
-    blank = jnp.zeros((ZS, LANES), F32)
-    centre_ref[pl.ds(7, ZS, stride=8), :] = blank
-    side_ref[pl.ds(7, ZS, stride=8), :] = blank
-
-
-def coefs(place_ref, lateral_ref, vertical_ref, ids_ref, out_ref, poly_ref, final_ref):
+        centre_ref[pl.ds(m, ZS, stride=8), :] = both[m * ZS : (m + 1) * ZS]
+    centre_ref[pl.ds(7, ZS, stride=8), :] = jnp.zeros((ZS, LANES), F32)
+    rates = jnp.concatenate([rate_high, rate_low], axis=0).astype(BF16)
+    for side, ref in ((1, left_ref), (2, right_ref)):
+        hit = (x == cells_ref[0]) & (y == cells_ref[side])
+        both = contract(rates, hit.astype(F32).astype(BF16))
+        ref[...] = both[:8] + both[8:]
+
+
+def coefs(place_ref, lateral_ref, vertical_ref, ids_ref, out_ref, poly_ref):
     ids = jnp.broadcast_to(ids_ref[...], (8, LANES))
     lane = lax.broadcasted_iota(jnp.int32, (8, LANES), 1)
     cond, lat = jnp.zeros((8, LANES), F32), jnp.zeros((8, LANES), F32)
@@ -192,94 +222,108 @@
                 step(p, wave - p)
 
     level = place_ref[0]
+    blank = jnp.zeros((SLOT - ZS, LANES), F32)
     for k in range(POWERS):
         block = poly_ref[level, STEPS, k * ZS : (k + 1) * ZS, :]
-        final_ref[2 * k * ZS : (2 * k + 1) * ZS, :] = block
-        final_ref[(2 * k + 1) * ZS : (2 * k + 2) * ZS, :] = block
-    final_ref[2 * POWERS * ZS :, :] = jnp.zeros((DEPTH - 2 * POWERS * ZS, LANES), F32)
-    table = final_ref[...].T[:NZ]
-    high = table.astype(BF16).astype(F32)
-    out_ref[...] = jnp.concatenate([high, table - high], axis=0).astype(BF16)
+        block = jnp.concatenate([jnp.where(lane_id < NZ, block, 0.0), blank], axis=0)
+        block = jnp.concatenate([block, pltpu.roll(block, SLOT, axis=1)], axis=0)
+        high = block.astype(BF16).astype(F32)
+        block = jnp.concatenate([high, block - high], axis=1).astype(BF16)
+        out_ref[k, :LANES, :] = block
+        out_ref[k, LANES:, :] = block
 
 
 def evolve(
-    place_ref, u_ref, above_ref, below_ref, own_ref, other_ref, src_centre_ref, src_side_ref, coef_ref,
-    out_ref, centre_ref, side_ref, terms_ref,
+    place_ref, u_ref, above_ref, below_ref, own_ref, other_ref, src_centre_ref, src_left_ref, src_right_ref, coef_ref,
+    out_ref, line_ref, side_ref, field_ref, other_field_ref, total_ref,
 ):
     level, tx, ty = place_ref[0], place_ref[1], place_ref[2]
-    lane = lax.broadcasted_iota(jnp.int32, (ZS, LANES), 1)
-    lane_z = lax.broadcasted_iota(jnp.int32, (NZ, LANES), 1)
+    lane = lax.broadcasted_iota(jnp.int32, (BLOCKS, LANES), 1)
+    sublane = lax.broadcasted_iota(jnp.int32, (BLOCKS, LANES), 0)
+    blank = jnp.zeros((SLOT - ZS, LANES), F32)
     low_level = level < 2
     for t in range(TILES):
         own, other = own_ref[t], other_ref[t]
-        left = jnp.where(low_level, own, other)
-        right = jnp.where(low_level, other, own)
-        for s in range(min(PER_TILE, EXT - t * PER_TILE)):
-            r = t * PER_TILE + s
-            from_right = pltpu.roll(right, (LANES - HALO * s) % LANES, axis=1)
-            from_left = pltpu.roll(left, (LANES - HALO * s - HALO) % LANES, axis=1)
-            side_ref[0, r, :NZ, :] = jnp.where(lane_z < LANES // 2, from_right, from_left)
-            centre_ref[0, r, :NZ, :] = ext_row(r, u_ref, above_ref, below_ref)
-            centre_ref[0, r, NZ:, :] = src_centre_ref[8 * r : 8 * r + 8, :]
-            side_ref[0, r, NZ:, :] = src_side_ref[8 * r : 8 * r + 8, :]
-
-    def keep_terms(k, pair, half, c):
-        high = c.astype(BF16).astype(F32)
-        both = jnp.concatenate([high, c - high], axis=0).astype(BF16)
-        terms_ref[pair, 2 * k * ZS : 2 * (k + 1) * ZS, half * LANES : (half + 1) * LANES] = both
-
-    @pl.loop(0, ROWS // 2)
-    def _(pair):
-        terms_ref[pair, 2 * POWERS * ZS :, :] = jnp.zeros((DEPTH - 2 * POWERS * ZS, 2 * LANES), BF16)
-        for half in range(2):
-            keep_terms(0, pair, half, centre_ref[0, HALO + 2 * pair + half])
-
-    last_x, last_y = place_ref[3], place_ref[4]
-    inside = ((lane >= LANES // 2) | (ty < last_y)) & ((lane < LANES // 2) | (ty > 0))
-    inside = inside.astype(F32)
-    above_in = jnp.where(tx > 0, 1.0, 0.0)
-    below_in = jnp.where(tx < last_x, 1.0, 0.0)
-    first_lane, last_lane = lane == 0, lane == LANES - 1
-
-    def neighbours(source, r):
-        c, h = centre_ref[source, r], side_ref[source, r]
-        c1, h1 = pltpu.roll(c, 1, axis=1), pltpu.roll(h, 1, axis=1)
-        c2, h2 = pltpu.roll(c, LANES - 1, axis=1), pltpu.roll(h, LANES - 1, axis=1)
-        new_c = centre_ref[source, r - 1] + centre_ref[source, r + 1]
-        new_c += jnp.where(first_lane, h1, c1) + jnp.where(last_lane, h2, c2)
-        new_h = side_ref[source, r - 1] + side_ref[source, r + 1]
-        new_h += jnp.where(first_lane, c1, h1) + jnp.where(last_lane, c2, h2)
-        return new_c, new_h * inside
-
-    for k in range(1, POWERS):
-        source, target = (k - 1) % 2, k % 2
-
-        @pl.loop(0, ROWS // 2)
-        def _(pair):
-            for half in range(2):
-                r = HALO + 2 * pair + half
-                new_c, new_h = neighbours(source, r)
-                centre_ref[target, r] = new_c
-                side_ref[target, r] = new_h
-                keep_terms(k, pair, half, new_c)
-
-        if k < HALO:
-
-            @pl.loop(k, HALO)
-            def _(r):
-                for row, there in ((r, above_in), (EXT - 1 - r, below_in)):
-                    new_c, new_h = neighbours(source, row)
-                    centre_ref[target, row] = new_c * there
-                    side_ref[target, row] = new_h * there
-
-    table = coef_ref[...]
-
-    @pl.loop(0, ROWS // 2)
-    def _(pair):
-        both = jnp.dot(table, terms_ref[pair], preferred_element_type=F32)
-        both = both[:NZ] + both[NZ:]
-        out_ref[pl.ds(2 * pair, NZ, stride=ROWS), :] = both[:, :LANES]
-        out_ref[pl.ds(2 * pair + 1, NZ, stride=ROWS), :] = both[:, LANES:]
+        part = slice(t * LANES, (t + 1) * LANES)
+        left = [jnp.where(low_level, own, other), src_left_ref[:, part], blank]
+        right = [jnp.where(low_level, other, own), src_right_ref[:, part], blank]
+        side_ref[0, part, :] = jnp.concatenate(left + left, axis=0).T
+        side_ref[1, part, :] = jnp.concatenate(right + right, axis=0).T
+
+    def halo_of(side, r):
+        t, first, width = PIECES.get(r, (0, 0, HALO))
+        first = t * LANES + first + (width - HALO if side == 0 else 0)
+        return side_ref[side, first : first + HALO, :]
+
+    in_low_half = lax.broadcasted_iota(jnp.int32, (HALO, LANES), 1) < SLOT
+    for i in range(PAIRS):
+        rows = []
+        for r in (i, i + HALF):
+            rows += [ext_row(r, u_ref, above_ref, below_ref), src_centre_ref[8 * r : 8 * r + 8, :], blank]
+        line_ref[i, HALO : HALO + LANES, :] = jnp.concatenate(rows, axis=0).T
+        line_ref[i, :HALO, :] = jnp.where(in_low_half, halo_of(0, i), halo_of(0, i + HALF))
+        right = jnp.where(in_low_half, halo_of(1, i), halo_of(1, i + HALF))
+        line_ref[i, HALO + LANES : 2 * HALO + LANES, :] = right
+        line_ref[i, 2 * HALO + LANES :, :] = jnp.zeros((WIDE - 2 * HALO - LANES, LANES), F32)
+        for j in range(SPAN):
+            field_ref[i, 8 * j : 8 * j + 8, :] = line_ref[i, pl.ds(j, BLOCKS, stride=SPAN), :]
+
+    above = jnp.where((lane < SLOT) & (tx == 0), 0.0, 1.0)
+    below = jnp.where((lane >= SLOT) & (tx == place_ref[3]), 0.0, 1.0)
+    left = jnp.where((sublane == 0) & (ty == 0), 0.0, 1.0)
+    right = jnp.where((sublane == BLOCKS - 1) & (ty == place_ref[4]), 0.0, 1.0)
+    first_right = HALO + LANES - (BLOCKS - 1) * SPAN
+
+    def advance(source, target, first, count, mask=None):
+        left_in, right_in = (left, right) if mask is None else (left * mask, right * mask)
+        load = lambda i, j: source[first + i, 8 * j : 8 * j + 8, :]
+        for start in range(0, SPAN, CHUNK):
+            inner = range(start, min(start + CHUNK, SPAN))
+            before = [load(-1, j) for j in inner]
+            centre = [load(0, j) for j in inner]
+            for i in range(count):
+                after = [load(i + 1, j) for j in inner]
+                if start == 0:
+                    low = pltpu.roll(load(i, SPAN - 1), 1, axis=0)
+                else:
+                    low = load(i, start - 1)
+                if inner[-1] == SPAN - 1:
+                    high = pltpu.roll(load(i, 0), BLOCKS - 1, axis=0)
+                else:
+                    high = load(i, inner[-1] + 1)
+                line = [low] + centre + [high]
+                for n, j in enumerate(inner):
+                    new = (before[n] + after[n]) + (line[n] + line[n + 2])
+                    if j < HALO:
+                        new = new * (left_in if j < first_right else left_in * right)
+                    else:
+                        new = new * right_in
+                    target[first + i, 8 * j : 8 * j + 8, :] = new
+                before, centre = centre, after
+
+    def collect(k, source):
+        cells = source[HALO : HALO + HALF].reshape(HALF * WIDE, LANES)
+        high, low = split(cells)
+        both = jnp.dot(jnp.concatenate([high, low], axis=1), coef_ref[k], preferred_element_type=F32)
+        both = (both[:, :LANES] + both[:, LANES:]).reshape(HALF, WIDE, LANES)
+        total_ref[...] = both if k == 0 else total_ref[...] + both
+
+    for k in range(POWERS):
+        source, target = (field_ref, other_field_ref)[:: 1 if k % 2 == 0 else -1]
+
+        collect(k, source)
+        if k + 1 < POWERS:
+            advance(source, target, HALO, HALF)
+        if k + 1 < HALO:
+            advance(source, target, k + 1, HALO - k - 1, above)
+            advance(source, target, HALO + HALF, HALO - k - 1, below)
+
+    for i in range(HALF):
+        for j in range(SPAN):
+            line_ref[i, pl.ds(j, BLOCKS, stride=SPAN), :] = total_ref[i, 8 * j : 8 * j + 8, :]
+        result = line_ref[i, HALO : HALO + LANES, :].T
+        out_ref[pl.ds(i, NZ, stride=ROWS), :] = result[:NZ]
+        out_ref[pl.ds(i + HALF, NZ, stride=ROWS), :] = result[SLOT : SLOT + NZ]
 
 
 SMEM = pl.BlockSpec(memory_space=pltpu.SMEM)
@@ -321,27 +365,32 @@
     own = lax.ppermute(strips, ("level", "ty"), route)
     other = lax.ppermute(own, "level", [(0, 2), (2, 0), (1, 3), (3, 1)])
 
-    planes = shape(ZS * 8, LANES)
-    src_centre, src_side = call(sources, "sources", [SMEM] * 2 + [WHOLE] * 3, (planes, planes), cost=1 << 28)(
-        place, pulse_rates, plan.T, bore_x[None, :], bore_y[None, :]
+    sides = shape(8, TILES * LANES)
+    src = call(sources, "sources", [SMEM] * 2 + [WHOLE] * 4, (shape(ZS * 8, LANES), sides, sides), cost=1 << 28)(
+        place, pulse_rates, plan.T, bore_x[None, :], bore_y[None, :], side_cells()
     )
     ids = jnp.pad(layer_ids, (0, LANES - NZ))[None, :]
     table = call(
         coefs,
         "coefs",
         [SMEM] * 3 + [WHOLE],
-        shape(2 * NZ, DEPTH, dtype=BF16),
-        [pltpu.VMEM((LEVELS, STEPS + 1, POWERS * ZS, LANES), F32), pltpu.VMEM((DEPTH, LANES), F32)],
+        shape(POWERS, 2 * LANES, 2 * LANES, dtype=BF16),
+        [pltpu.VMEM((LEVELS, STEPS + 1, POWERS * ZS, LANES), F32)],
         cost=1 << 28,
     )(place, lateral_number, vertical_number, ids)
-    buffer = pltpu.VMEM((2, EXT, ZS, LANES), F32)
     result = call(
         evolve,
         "evolve",
-        [SMEM] + [WHOLE] * 8,
+        [SMEM] + [WHOLE] * 9,
         shape(NZ * ROWS, LANES),
-        [buffer, buffer, pltpu.VMEM((ROWS // 2, DEPTH, 2 * LANES), BF16)],
-    )(place, flat, above, below, own, other, src_centre, src_side, table)
+        [
+            pltpu.VMEM((PAIRS, WIDE, LANES), F32),
+            pltpu.VMEM((2, TILES * LANES, LANES), F32),
+            pltpu.VMEM((PAIRS, WIDE, LANES), F32),
+            pltpu.VMEM((PAIRS, WIDE, LANES), F32),
+            pltpu.VMEM((HALF, WIDE, LANES), F32),
+        ],
+    )(place, flat, above, below, own, other, *src, table)
     return result.reshape(1, NZ, ROWS, LANES)
 
 

time: 73.1 us -> 44.6 us (0.61)
  Pallas kernels: 40.8 us -> 14.6 us
  waiting for transfers between devices: 10.4 us -> 8.65 us
    pallas_call x3, Pallas kernels: 39.3 us -> 13.2 us  [the longest x1 7.67 us: on_device(): call(evolve, 'evolve', [SMEM] + [WHOLE] * 9, shape(NZ * ROWS, LANES), [pl...]
    ppermute x1, waiting for transfers between devices: 4.61 us -> 3.56 us  [on_device(): own = lax.ppermute(strips, ('level', 'ty'), route)]
    unnamed x18 -> x20, local copies, waits for them, and re-layouts: 1.82 us -> 1.2 us
  transfers between devices with their start and end apart: 4 -> 4, of which waited for: 4 -> 4; matrix products, arithmetic and copies ran while one was open for 0% -> 0% of each run, Pallas kernels for 7% -> 12%
where the time goes in v2:
time: 44.6 us; the launch traced here: 44.3 us
  starting transfers between devices  19.5 us (44%)
  Pallas kernels  14.6 us (33%)
  waiting for transfers between devices  8.65 us (19%)
  local copies, waits for them, and re-layouts  1.29 us (3%)
    ppermute x1, starting transfers between devices, on_device(): own = lax.ppermute(strips, ('level', 'ty'), route)  12 us
    pallas_call x1, Pallas kernels, on_device(): call(evolve, 'evolve', [SMEM] + [WHOLE] * 9, shape(NZ * ROWS, LANES), [pl...  7.67 us
    pallas_call x1, Pallas kernels, on_device(): call(coefs, 'coefs', [SMEM] * 3 + [WHOLE], shape(POWERS, 2 * LANES, 2 * L...  3.99 us
    ppermute x1, starting transfers between devices, on_device(): below = lax.ppermute(top, 'tx', [(j, i) for i, j in up])  3.64 us
    ppermute x1, waiting for transfers between devices, on_device(): own = lax.ppermute(strips, ('level', 'ty'), route)  3.56 us
    ppermute x1, starting transfers between devices, on_device(): above = lax.ppermute(bottom, 'tx', up)  1.92 us
    ppermute x1, starting transfers between devices, on_device(): other = lax.ppermute(own, 'level', [(0, 2), (2, 0), (1, 3), (3, 1)])  1.91 us
    ppermute x1, waiting for transfers between devices, on_device(): other = lax.ppermute(own, 'level', [(0, 2), (2, 0), (1, 3), (3, 1)])  1.78 us
  transfers between devices with their start and end apart: 4, of which 4 were waited for; matrix products, arithmetic and copies ran while one was open for 0% of the time, Pallas kernels for 12%

profile of v2, /device:TPU:26, one launch (start us, length us, event | category | flops | bytes accessed | tf_op | source)
XLA Modules:
  0.0 44.3 jit_solution(10030341715285146743)
XLA Ops:
  0.0 0.0 copy-start.9
  0.0 0.0 copy-start.3
  0.0 0.0 copy-start.2
  0.0 0.0 copy-start
  0.0 1.2 %copy-done = f32[48,32,128]{2,1,0:T(8,128)S(1)} copy-done((f32[48,32,128]{2,1,0:T(8,128)S(1)}, f32[48,32,128]{2,1,0:T(8,128)}, u32[]{:S(2)}) %copy-start) | copy-done | bytes 786456
  1.2 0.0 copy-start.1
  1.2 0.3 edge_rows.1
  1.4 1.9 %collective-permute-start = (f32[9,48,128]{2,1,0:T(8,128)S(1)}, f32[9,48,128]{2,1,0:T(8,128)S(1)}, u32[]{:S(2)}, u32[]{:S(2)}) collective-permute-start(f32[9,48,128]{2,1,0:T(8,128)S(1)} %get-tuple-element.10), channel_id=1, source_target_pairs={{0,16},{16,32},{32,48},{48,64},{64,80},{80,96},{96,112},{1,17},{17... | collective-permute-start | bytes 663560 | tf_op jit(solution)/shard_map/ppermute | solution.py:355
  3.4 3.6 %collective-permute-start.1 = (f32[9,48,128]{2,1,0:T(8,128)S(1)}, f32[9,48,128]{2,1,0:T(8,128)S(1)}, u32[]{:S(2)}, u32[]{:S(2)}) collective-permute-start(f32[9,48,128]{2,1,0:T(8,128)S(1)} %get-tuple-element.11), channel_id=1, source_target_pairs={{16,0},{32,16},{48,32},{64,48},{80,64},{96,80},{112,96},{17,1},{33... | collective-permute-start | bytes 663560 | tf_op jit(solution)/shard_map/ppermute | solution.py:356
  7.0 0.1 stack.15.place_ref
  7.1 0.0 copy-start.4
  7.1 0.0 copy-start.7
  7.1 0.0 copy-start.8
  7.1 1.6 %collective-permute-done.above_ref = f32[9,48,128]{2,1,0:T(8,128)S(1)} collective-permute-done((f32[9,48,128]{2,1,0:T(8,128)S(1)}, f32[9,48,128]{2,1,0:T(8,128)S(1)}, u32[]{:S(2)}, u32[]{:S(2)}) %collective-permute-start) | collective-permute-done | bytes 221216 | tf_op jit(solution)/shard_map/ppermute | solution.py:355
  8.7 1.8 %collective-permute-done.1.below_ref = f32[9,48,128]{2,1,0:T(8,128)S(1)} collective-permute-done((f32[9,48,128]{2,1,0:T(8,128)S(1)}, f32[9,48,128]{2,1,0:T(8,128)S(1)}, u32[]{:S(2)}, u32[]{:S(2)}) %collective-permute-start.1) | collective-permute-done | bytes 221216 | tf_op jit(solution)/shard_map/ppermute | solution.py:356
  10.5 0.0 copy-done.1
  10.5 1.2 %edge_columns.1 = f32[3,48,128]{2,1,0:T(8,128)S(1)} custom-call(s32[5]{0:T(128)S(1)} %stack.15.place_ref, f32[1536,128]{1,0:T(8,128)S(1)} %bitcast.11, f32[9,48,128]{2,1,0:T(8,128)S(1)} %collective-permute-done.above_ref, f32[9,48,128]{2,1,0:T(8,128)S(1)} %collective-permute-done.1.below_ref), custom_call_target="tpu_custom_call" | custom-call | bytes 1048576 | tf_op jit(solution)/shard_map/edge_columns/pallas_call | solution.py:357
  11.7 12.0 %collective-permute-start.2 = (f32[3,48,128]{2,1,0:T(8,128)S(1)}, f32[3,48,128]{2,1,0:T(8,128)S(1)}, u32[]{:S(2)}, u32[]{:S(2)}) collective-permute-start(f32[3,48,128]{2,1,0:T(8,128)S(1)} %edge_columns.1), channel_id=1, source_target_pairs={{256,1},{1,256},{384,129},{129,384},{257,2},{2,257},{385,130},{130... | collective-permute-start | bytes 221192 | tf_op jit(solution)/shard_map/ppermute | solution.py:365
  23.7 3.6 %collective-permute-done.2.own_ref = f32[3,48,128]{2,1,0:T(8,128)S(1)} collective-permute-done((f32[3,48,128]{2,1,0:T(8,128)S(1)}, f32[3,48,128]{2,1,0:T(8,128)S(1)}, u32[]{:S(2)}, u32[]{:S(2)}) %collective-permute-start.2) | collective-permute-done | bytes 73760 | tf_op jit(solution)/shard_map/ppermute | solution.py:365
  27.3 1.9 %collective-permute-start.3 = (f32[3,48,128]{2,1,0:T(8,128)S(1)}, f32[3,48,128]{2,1,0:T(8,128)S(1)}, u32[]{:S(2)}, u32[]{:S(2)}) collective-permute-start(f32[3,48,128]{2,1,0:T(8,128)S(1)} %collective-permute-done.2.own_ref), channel_id=1, source_target_pairs={{0,256},{256,0},{128,384},{384,128},{1,257},{257,1},{129,385},{385... | collective-permute-start | bytes 221192 | tf_op jit(solution)/shard_map/ppermute | solution.py:366
  29.2 0.0 copy-done.9
  29.2 0.0 copy-done.3
  29.2 0.0 copy-done.2
  29.2 4.0 %coefs.1.coef_ref = bf16[10,256,256]{2,1,0:T(8,128)(2,1)S(1)} custom-call(s32[5]{0:T(128)S(1)} %stack.15.place_ref, f32[6]{0:T(128)S(1)} %copy-done.2, f32[6]{0:T(128)S(1)} %copy-done.3, s32[1,128]{1,0:T(1,128)S(1)} %pad_bitcast_fusion.ids_ref), custom_call_target="tpu_custom_call" | custom-call | flops 268435456 | bytes 1048576 | tf_op jit(solution)/shard_map/coefs/pallas_call | solution.py:373
  33.2 0.0 copy-done.4
  33.2 0.0 copy-done.5
  33.2 0.0 copy-done.6
  33.3 0.0 copy-done.7
  33.3 0.0 copy-done.8
  33.3 1.5 %sources.1 = (f32[448,128]{1,0:T(8,128)S(1)}, f32[8,384]{1,0:T(8,128)S(1)}, f32[8,384]{1,0:T(8,128)S(1)}) custom-call(s32[5]{0:T(128)S(1)} %stack.15.place_ref, f32[8]{0:T(128)S(1)} %copy-done.7, s32[7,1024]{1,0:T(8,128)S(1)} %bitcast.13, s32[1,1024]{1,0:T(1,128)S(1)} %bitcast.14, s32[1,1024]{1,0:T(1,128)S(1)} %bitcast.15, s32[3,384,1]{2,1,0:T(8,128)S(1)} %copy-done.8), custom_call_target="tpu_custom_call" | custom-call | flops 268435456 | bytes 1048576 | tf_op jit(solution)/shard_map/sources/pallas_call | solution.py:369
  34.8 1.8 %collective-permute-done.3.other_ref = f32[3,48,128]{2,1,0:T(8,128)S(1)} collective-permute-done((f32[3,48,128]{2,1,0:T(8,128)S(1)}, f32[3,48,128]{2,1,0:T(8,128)S(1)}, u32[]{:S(2)}, u32[]{:S(2)}) %collective-permute-start.3) | collective-permute-done | bytes 73760 | tf_op jit(solution)/shard_map/ppermute | solution.py:366
  36.6 7.7 %evolve.1 = f32[1536,128]{1,0:T(8,128)} custom-call(s32[5]{0:T(128)S(1)} %stack.15.place_ref, f32[1536,128]{1,0:T(8,128)S(1)} %bitcast.12, f32[9,48,128]{2,1,0:T(8,128)S(1)} %collective-permute-done.above_ref, f32[9,48,128]{2,1,0:T(8,128)S(1)} %collective-permute-done.1.below_ref, f32[3,48,128]{2,1,0:T(8,128)S(1)} %collective-permute-done.2.own_ref, ...), custom_call_target="tpu_custom_call" | custom-call | bytes 1048576 | tf_op jit(solution)/shard_map/evolve/pallas_call | solution.py:381
  (3 shorter events, 0.0 us)
Async XLA Ops:
  0.0 29.2 %copy-start.9 = (s32[48]{0:T(128)S(1)}, s32[48]{0:T(128)}, u32[]{:S(2)}) copy-start(s32[48]{0:T(128)} %param.10) | copy-start | bytes 580
  0.0 29.2 %copy-start.3 = (f32[6]{0:T(128)S(1)}, f32[6]{0:T(128)}, u32[]{:S(2)}) copy-start(f32[6]{0:T(128)} %vertical_ref.1) | copy-start | bytes 76
  0.0 29.2 %copy-start.2 = (f32[6]{0:T(128)S(1)}, f32[6]{0:T(128)}, u32[]{:S(2)}) copy-start(f32[6]{0:T(128)} %lateral_ref.1) | copy-start | bytes 76
  0.0 1.2 %copy-start = (f32[48,32,128]{2,1,0:T(8,128)S(1)}, f32[48,32,128]{2,1,0:T(8,128)}, u32[]{:S(2)}) copy-start(f32[48,32,128]{2,1,0:T(8,128)} %param.9) | copy-start | bytes 2359300
  1.2 9.3 %copy-start.1 = (f32[48,32,128]{2,1,0:T(8,128)S(1)}, f32[48,32,128]{2,1,0:T(8,128)}, u32[]{:S(2)}) copy-start(f32[48,32,128]{2,1,0:T(8,128)} %param.9) | copy-start | bytes 2359300
  1.4 7.3 %collective-permute-start = (f32[9,48,128]{2,1,0:T(8,128)S(1)}, f32[9,48,128]{2,1,0:T(8,128)S(1)}, u32[]{:S(2)}, u32[]{:S(2)}) collective-permute-start(f32[9,48,128]{2,1,0:T(8,128)S(1)} %get-tuple-element.10), channel_id=1, source_target_pairs={{0,16},{16,32},{32,48},{48,64},{64,80},{80,96},{96,112},{1,17},{17... | collective-permute-start | bytes 663560 | tf_op jit(solution)/shard_map/ppermute | solution.py:355
  3.4 7.1 %collective-permute-start.1 = (f32[9,48,128]{2,1,0:T(8,128)S(1)}, f32[9,48,128]{2,1,0:T(8,128)S(1)}, u32[]{:S(2)}, u32[]{:S(2)}) collective-permute-start(f32[9,48,128]{2,1,0:T(8,128)S(1)} %get-tuple-element.11), channel_id=1, source_target_pairs={{16,0},{32,16},{48,32},{64,48},{80,64},{96,80},{112,96},{17,1},{33... | collective-permute-start | bytes 663560 | tf_op jit(solution)/shard_map/ppermute | solution.py:356
  7.1 26.1 %copy-start.4 = (s32[1024,7]{0,1:T(8,128)S(1)}, s32[1024,7]{0,1:T(8,128)}, u32[]{:S(2)}) copy-start(s32[1024,7]{0,1:T(8,128)} %param.16) | copy-start | bytes 86020
  7.1 26.1 %copy-start.5 = (s32[1024]{0:T(1024)S(1)}, s32[1024]{0:T(1024)}, u32[]{:S(2)}) copy-start(s32[1024]{0:T(1024)} %param.14) | copy-start | bytes 12292
  7.1 26.1 %copy-start.6 = (s32[1024]{0:T(1024)S(1)}, s32[1024]{0:T(1024)}, u32[]{:S(2)}) copy-start(s32[1024]{0:T(1024)} %param.15) | copy-start | bytes 12292
  7.1 26.1 %copy-start.7 = (f32[8]{0:T(128)S(1)}, f32[8]{0:T(128)}, u32[]{:S(2)}) copy-start(f32[8]{0:T(128)} %rates_ref.1) | copy-start | bytes 100
  7.1 26.1 %copy-start.8 = (s32[3,384,1]{2,1,0:T(8,128)S(1)}, s32[3,384,1]{2,1,0:T(8,128)}, u32[]{:S(2)}) copy-start(s32[3,384,1]{2,1,0:T(8,128)} %constant.22.clone.cells_ref) | copy-start | bytes 13828
  11.7 15.6 %collective-permute-start.2 = (f32[3,48,128]{2,1,0:T(8,128)S(1)}, f32[3,48,128]{2,1,0:T(8,128)S(1)}, u32[]{:S(2)}, u32[]{:S(2)}) collective-permute-start(f32[3,48,128]{2,1,0:T(8,128)S(1)} %edge_columns.1), channel_id=1, source_target_pairs={{256,1},{1,256},{384,129},{129,384},{257,2},{2,257},{385,130},{130... | collective-permute-start | bytes 221192 | tf_op jit(solution)/shard_map/ppermute | solution.py:365
  27.3 9.3 %collective-permute-start.3 = (f32[3,48,128]{2,1,0:T(8,128)S(1)}, f32[3,48,128]{2,1,0:T(8,128)S(1)}, u32[]{:S(2)}, u32[]{:S(2)}) collective-permute-start(f32[3,48,128]{2,1,0:T(8,128)S(1)} %collective-permute-done.2.own_ref), channel_id=1, source_target_pairs={{0,256},{256,0},{128,384},{384,128},{1,257},{257,1},{129,385},{385... | collective-permute-start | bytes 221192 | tf_op jit(solution)/shard_map/ppermute | solution.py:366

commit v3 on v2

--- a/solution.py
+++ b/solution.py
@@ -21,8 +21,10 @@
 PAIRS = HALF + 2 * HALO
 SLOT = LANES // 2
 BLOCKS = 8
-SPAN = -(-(LANES + 2 * HALO) // BLOCKS)
-WIDE = SPAN * BLOCKS
+BACK = (POWERS - 1) // 2
+SPAN = (LANES + 2 * BACK) // BLOCKS
+RIM = 20
+RIM_SPAN = 2 * RIM // BLOCKS
 CHUNK = 5
 VMEM = 48 * 1024 * 1024
 F32, BF16 = jnp.float32, jnp.bfloat16
@@ -51,37 +53,52 @@
     return high, (x - high.astype(F32)).astype(BF16)
 
 
-def edge_rows(u_ref, top_ref, bottom_ref):
+def edge_rows(place_ref, u_ref, far_ref, near_ref, kept_ref):
+    even = lax.rem(place_ref[1], 2) == 0
     for i in range(HALO):
-        top_ref[i] = u_ref[pl.ds(i, NZ, stride=ROWS), :]
-        bottom_ref[i] = u_ref[pl.ds(ROWS - HALO + i, NZ, stride=ROWS), :]
-
-
-def ext_row(r, u_ref, above_ref, below_ref):
+        first = u_ref[pl.ds(i, NZ, stride=ROWS), :]
+        last = u_ref[pl.ds(ROWS - HALO + i, NZ, stride=ROWS), :]
+        far_ref[i] = jnp.where(even, first, last)
+        near_ref[i] = jnp.where(even, last, first)
+    kept_ref[...] = u_ref[...]
+
+
+def ext_row(r, even, u_ref, far_ref, near_ref):
     if r < HALO:
-        return above_ref[r]
+        return jnp.where(even, far_ref[r], near_ref[r])
     if r < HALO + ROWS:
         return u_ref[pl.ds(r - HALO, NZ, stride=ROWS), :]
-    return below_ref[r - HALO - ROWS]
-
-
-def edge_columns(place_ref, u_ref, above_ref, below_ref, packed_ref):
+    return jnp.where(even, near_ref[r - HALO - ROWS], far_ref[r - HALO - ROWS])
+
+
+def pack(place_ref, rows, row_of, packed_ref, tiles):
     lane = lax.broadcasted_iota(jnp.int32, (NZ, LANES), 1)
     send_last = place_ref[0] >= 2
-    tiles = [jnp.zeros((NZ, LANES), F32) for _ in range(TILES)]
-    for r, (t, first, width) in PIECES.items():
-        row = ext_row(r, u_ref, above_ref, below_ref)
-        row = pltpu.roll(row, first + jnp.where(send_last, width, 0), axis=1)
+    for r in rows:
+        t, first, width = PIECES[r]
+        row = pltpu.roll(row_of(r), first + jnp.where(send_last, width, 0), axis=1)
         tiles[t] = jnp.where((lane >= first) & (lane < first + width), row, tiles[t])
     for t in range(TILES):
         packed_ref[t] = tiles[t]
 
 
+def own_columns(place_ref, u_ref, packed_ref):
+    row_of = lambda r: u_ref[pl.ds(r - HALO, NZ, stride=ROWS), :]
+    pack(place_ref, range(HALO, HALO + ROWS), row_of, packed_ref, [jnp.zeros((NZ, LANES), F32)] * TILES)
+
+
+def edge_columns(place_ref, strips_ref, far_ref, near_ref, packed_ref):
+    even = lax.rem(place_ref[1], 2) == 0
+    rows = [r for r in PIECES if not HALO <= r < HALO + ROWS]
+    row_of = lambda r: ext_row(r, even, None, far_ref, near_ref)
+    pack(place_ref, rows, row_of, packed_ref, [strips_ref[t] for t in range(TILES)])
+
+
 def side_cells():
-    cells = np.full((3, TILES * LANES, 1), -(1 << 20), np.int32)
+    cells = np.full((8, TILES * LANES), -(1 << 20), np.float32)
     for r, (t, first, width) in PIECES.items():
         for c in range(width):
-            cells[:, t * LANES + first + c, 0] = (r - HALO, c - width, LANES + c)
+            cells[:3, t * LANES + first + c] = (r - HALO, c - width, LANES + c)
     return cells
 
 
@@ -109,8 +126,10 @@
         centre_ref[pl.ds(m, ZS, stride=8), :] = both[m * ZS : (m + 1) * ZS]
     centre_ref[pl.ds(7, ZS, stride=8), :] = jnp.zeros((ZS, LANES), F32)
     rates = jnp.concatenate([rate_high, rate_low], axis=0).astype(BF16)
+    columns = [cells_ref[:, t * LANES : (t + 1) * LANES].T for t in range(TILES)]
+    columns = jnp.concatenate(columns, axis=0).astype(jnp.int32)
     for side, ref in ((1, left_ref), (2, right_ref)):
-        hit = (x == cells_ref[0]) & (y == cells_ref[side])
+        hit = (x == columns[:, :1]) & (y == columns[:, side : side + 1])
         both = contract(rates, hit.astype(F32).astype(BF16))
         ref[...] = both[:8] + both[8:]
 
@@ -233,22 +252,94 @@
         out_ref[k, LANES:, :] = block
 
 
-def evolve(
-    place_ref, u_ref, above_ref, below_ref, own_ref, other_ref, src_centre_ref, src_left_ref, src_right_ref, coef_ref,
+def advance(source, target, span, first, count, edge=lambda j, new: new):
+    load = lambda i, j: source[first + i, 8 * j : 8 * j + 8, :]
+    sublane = lax.broadcasted_iota(jnp.int32, (BLOCKS, LANES), 0)
+    for start in range(0, span, CHUNK):
+        inner = range(start, min(start + CHUNK, span))
+        before = [load(-1, j) for j in inner]
+        centre = [load(0, j) for j in inner]
+        for i in range(count):
+            after = [load(i + 1, j) for j in inner]
+            if start == 0:
+                low = jnp.where(sublane == 0, 0.0, pltpu.roll(load(i, span - 1), 1, axis=0))
+            else:
+                low = load(i, start - 1)
+            if inner[-1] == span - 1:
+                high = jnp.where(sublane == BLOCKS - 1, 0.0, pltpu.roll(load(i, 0), BLOCKS - 1, axis=0))
+            else:
+                high = load(i, inner[-1] + 1)
+            line = [low] + centre + [high]
+            for n, j in enumerate(inner):
+                new = (before[n] + after[n]) + (line[n] + line[n + 2])
+                target[first + i, 8 * j : 8 * j + 8, :] = edge(j, new)
+            before, centre = centre, after
+
+
+def powers(fields, total_ref, coef_ref, span, edge, above, below):
+    for k in range(POWERS):
+        source, target = fields[k % 2], fields[1 - k % 2]
+        cells = source[HALO : HALO + HALF].reshape(HALF * span * BLOCKS, LANES)
+        high, low = split(cells)
+        both = jnp.dot(jnp.concatenate([high, low], axis=1), coef_ref[k], preferred_element_type=F32)
+        both = (both[:, :LANES] + both[:, LANES:]).reshape(HALF, span * BLOCKS, LANES)
+        total_ref[...] = both if k == 0 else total_ref[...] + both
+        if k + 1 < POWERS:
+            advance(source, target, span, HALO, HALF, edge)
+        if k + 1 < HALO:
+            count = HALO - k - 1
+            advance(source, target, span, k + 1, count, lambda j, new: edge(j, new) * above)
+            advance(source, target, span, HALO + HALF, count, lambda j, new: edge(j, new) * below)
+
+
+def grid_rows(place_ref):
+    lane = lax.broadcasted_iota(jnp.int32, (BLOCKS, LANES), 1)
+    above = jnp.where((lane < SLOT) & (place_ref[1] == 0), 0.0, 1.0)
+    below = jnp.where((lane >= SLOT) & (place_ref[1] == place_ref[3]), 0.0, 1.0)
+    return above, below
+
+
+def bulk(
+    place_ref, u_ref, far_ref, near_ref, src_ref, coef_ref, out_ref, line_ref, field_ref, other_field_ref, total_ref
+):
+    ty = place_ref[2]
+    even = lax.rem(place_ref[1], 2) == 0
+    sublane = lax.broadcasted_iota(jnp.int32, (BLOCKS, LANES), 0)
+    blank = jnp.zeros((SLOT - ZS, LANES), F32)
+    room = jnp.zeros((BACK, LANES), F32)
+    for i in range(PAIRS):
+        rows = []
+        for r in (i, i + HALF):
+            rows += [ext_row(r, even, u_ref, far_ref, near_ref), src_ref[8 * r : 8 * r + 8, :], blank]
+        line_ref[i, :BACK, :] = room
+        line_ref[i, BACK : BACK + LANES, :] = jnp.concatenate(rows, axis=0).T
+        line_ref[i, BACK + LANES :, :] = room
+        for j in range(SPAN):
+            field_ref[i, 8 * j : 8 * j + 8, :] = line_ref[i, pl.ds(j, BLOCKS, stride=SPAN), :]
+    left = jnp.where((sublane == 0) & (ty == 0), 0.0, 1.0)
+    right = jnp.where((sublane == BLOCKS - 1) & (ty == place_ref[4]), 0.0, 1.0)
+
+    def edge(j, new):
+        return new * left if j < BACK else new * right if j >= SPAN - BACK else new
+
+    powers((field_ref, other_field_ref), total_ref, coef_ref, SPAN, edge, *grid_rows(place_ref))
+    for i in range(HALF):
+        for j in range(SPAN):
+            line_ref[i, pl.ds(j, BLOCKS, stride=SPAN), :] = total_ref[i, 8 * j : 8 * j + 8, :]
+        out_ref[i] = line_ref[i, BACK : BACK + LANES, :]
+
+
+def rim(
+    place_ref, own_ref, other_ref, src_left_ref, src_right_ref, coef_ref, bulk_ref,
     out_ref, line_ref, side_ref, field_ref, other_field_ref, total_ref,
 ):
-    level, tx, ty = place_ref[0], place_ref[1], place_ref[2]
-    lane = lax.broadcasted_iota(jnp.int32, (BLOCKS, LANES), 1)
-    sublane = lax.broadcasted_iota(jnp.int32, (BLOCKS, LANES), 0)
+    low_level = place_ref[0] < 2
     blank = jnp.zeros((SLOT - ZS, LANES), F32)
-    low_level = level < 2
-    for t in range(TILES):
-        own, other = own_ref[t], other_ref[t]
-        part = slice(t * LANES, (t + 1) * LANES)
-        left = [jnp.where(low_level, own, other), src_left_ref[:, part], blank]
-        right = [jnp.where(low_level, other, own), src_right_ref[:, part], blank]
-        side_ref[0, part, :] = jnp.concatenate(left + left, axis=0).T
-        side_ref[1, part, :] = jnp.concatenate(right + right, axis=0).T
+    for side, src_ref in enumerate((src_left_ref, src_right_ref)):
+        for t in range(TILES):
+            part = slice(t * LANES, (t + 1) * LANES)
+            tile = jnp.where(low_level == (side == 0), own_ref[t], other_ref[t])
+            side_ref[side, part, :] = jnp.concatenate([tile, src_ref[:, part], blank] * 2, axis=0).T
 
     def halo_of(side, r):
         t, first, width = PIECES.get(r, (0, 0, HALO))
@@ -256,72 +347,20 @@
         return side_ref[side, first : first + HALO, :]
 
     in_low_half = lax.broadcasted_iota(jnp.int32, (HALO, LANES), 1) < SLOT
+    room = jnp.zeros((2 * (RIM - HALO), LANES), F32)
     for i in range(PAIRS):
-        rows = []
-        for r in (i, i + HALF):
-            rows += [ext_row(r, u_ref, above_ref, below_ref), src_centre_ref[8 * r : 8 * r + 8, :], blank]
-        line_ref[i, HALO : HALO + LANES, :] = jnp.concatenate(rows, axis=0).T
         line_ref[i, :HALO, :] = jnp.where(in_low_half, halo_of(0, i), halo_of(0, i + HALF))
-        right = jnp.where(in_low_half, halo_of(1, i), halo_of(1, i + HALF))
-        line_ref[i, HALO + LANES : 2 * HALO + LANES, :] = right
-        line_ref[i, 2 * HALO + LANES :, :] = jnp.zeros((WIDE - 2 * HALO - LANES, LANES), F32)
-        for j in range(SPAN):
-            field_ref[i, 8 * j : 8 * j + 8, :] = line_ref[i, pl.ds(j, BLOCKS, stride=SPAN), :]
-
-    above = jnp.where((lane < SLOT) & (tx == 0), 0.0, 1.0)
-    below = jnp.where((lane >= SLOT) & (tx == place_ref[3]), 0.0, 1.0)
-    left = jnp.where((sublane == 0) & (ty == 0), 0.0, 1.0)
-    right = jnp.where((sublane == BLOCKS - 1) & (ty == place_ref[4]), 0.0, 1.0)
-    first_right = HALO + LANES - (BLOCKS - 1) * SPAN
-
-    def advance(source, target, first, count, mask=None):
-        left_in, right_in = (left, right) if mask is None else (left * mask, right * mask)
-        load = lambda i, j: source[first + i, 8 * j : 8 * j + 8, :]
-        for start in range(0, SPAN, CHUNK):
-            inner = range(start, min(start + CHUNK, SPAN))
-            before = [load(-1, j) for j in inner]
-            centre = [load(0, j) for j in inner]
-            for i in range(count):
-                after = [load(i + 1, j) for j in inner]
-                if start == 0:
-                    low = pltpu.roll(load(i, SPAN - 1), 1, axis=0)
-                else:
-                    low = load(i, start - 1)
-                if inner[-1] == SPAN - 1:
-                    high = pltpu.roll(load(i, 0), BLOCKS - 1, axis=0)
-                else:
-                    high = load(i, inner[-1] + 1)
-                line = [low] + centre + [high]
-                for n, j in enumerate(inner):
-                    new = (before[n] + after[n]) + (line[n] + line[n + 2])
-                    if j < HALO:
-                        new = new * (left_in if j < first_right else left_in * right)
-                    else:
-                        new = new * right_in
-                    target[first + i, 8 * j : 8 * j + 8, :] = new
-                before, centre = centre, after
-
-    def collect(k, source):
-        cells = source[HALO : HALO + HALF].reshape(HALF * WIDE, LANES)
-        high, low = split(cells)
-        both = jnp.dot(jnp.concatenate([high, low], axis=1), coef_ref[k], preferred_element_type=F32)
-        both = (both[:, :LANES] + both[:, LANES:]).reshape(HALF, WIDE, LANES)
-        total_ref[...] = both if k == 0 else total_ref[...] + both
-
-    for k in range(POWERS):
-        source, target = (field_ref, other_field_ref)[:: 1 if k % 2 == 0 else -1]
-
-        collect(k, source)
-        if k + 1 < POWERS:
-            advance(source, target, HALO, HALF)
-        if k + 1 < HALO:
-            advance(source, target, k + 1, HALO - k - 1, above)
-            advance(source, target, HALO + HALF, HALO - k - 1, below)
-
+        line_ref[i, HALO : 2 * RIM - HALO, :] = room
+        line_ref[i, 2 * RIM - HALO :, :] = jnp.where(in_low_half, halo_of(1, i), halo_of(1, i + HALF))
+        for j in range(RIM_SPAN):
+            field_ref[i, 8 * j : 8 * j + 8, :] = line_ref[i, pl.ds(j, BLOCKS, stride=RIM_SPAN), :]
+    powers((field_ref, other_field_ref), total_ref, coef_ref, RIM_SPAN, lambda j, new: new, *grid_rows(place_ref))
     for i in range(HALF):
-        for j in range(SPAN):
-            line_ref[i, pl.ds(j, BLOCKS, stride=SPAN), :] = total_ref[i, 8 * j : 8 * j + 8, :]
-        result = line_ref[i, HALO : HALO + LANES, :].T
+        for j in range(RIM_SPAN):
+            line_ref[i, pl.ds(j, BLOCKS, stride=RIM_SPAN), :] = total_ref[i, 8 * j : 8 * j + 8, :]
+        inner = LANES - 2 * (RIM - HALO)
+        change = [line_ref[i, HALO:RIM, :], jnp.zeros((inner, LANES), F32), line_ref[i, RIM : 2 * RIM - HALO, :]]
+        result = (bulk_ref[i] + jnp.concatenate(change, axis=0)).T
         out_ref[pl.ds(i, NZ, stride=ROWS), :] = result[:NZ]
         out_ref[pl.ds(i + HALF, NZ, stride=ROWS), :] = result[SLOT : SLOT + NZ]
 
@@ -350,47 +389,57 @@
     place = jnp.stack(indices + [jnp.int32(count_x - 1), jnp.int32(count_y - 1)])
     flat = initial.reshape(NZ * ROWS, LANES)
     slab = shape(HALO, NZ, LANES)
-    top, bottom = call(edge_rows, "edge_rows", [WHOLE], (slab, slab))(flat)
-    up = [(i, i + 1) for i in range(count_x - 1)]
-    above = lax.ppermute(bottom, "tx", up)
-    below = lax.ppermute(top, "tx", [(j, i) for i, j in up])
-    strips = call(edge_columns, "edge_columns", [SMEM] + [WHOLE] * 3, shape(TILES, NZ, LANES))(
-        place, flat, above, below
+    whole = shape(NZ * ROWS, LANES)
+    far, near, kept = call(edge_rows, "edge_rows", [SMEM, WHOLE], (slab, slab, whole), cost=800 << 20)(place, flat)
+    pairs = lambda first: [(i + a, i + 1 - a) for i in range(first, count_x - 1, 2) for a in (0, 1)]
+    far = lax.ppermute(far, "tx", pairs(1))
+    near = lax.ppermute(near, "tx", pairs(0))
+    packed = shape(TILES, NZ, LANES)
+    strips = call(own_columns, "own_columns", [SMEM, WHOLE], packed, cost=1000 << 20)(place, kept)
+    sides = shape(8, TILES * LANES)
+    src, src_left, src_right = call(
+        sources, "sources", [SMEM] * 2 + [WHOLE] * 4, (shape(ZS * 8, LANES), sides, sides), cost=1700 << 20
+    )(place, pulse_rates, plan.T, bore_x[None, :], bore_y[None, :], side_cells())
+    strips, src = lax.optimization_barrier((strips, src))
+    strips = call(edge_columns, "edge_columns", [SMEM] + [WHOLE] * 3, packed, cost=800 << 20)(
+        place, strips, far, near
     )
+    ids = jnp.pad(layer_ids, (0, LANES - NZ))[None, :]
+    strips, ids = lax.optimization_barrier((strips, ids))
     route = []
     for i in range(count_y - 1):
         for l in (0, 1):
             route.append(((l + 2) * count_y + i, l * count_y + i + 1))
             route.append((l * count_y + i + 1, (l + 2) * count_y + i))
     own = lax.ppermute(strips, ("level", "ty"), route)
-    other = lax.ppermute(own, "level", [(0, 2), (2, 0), (1, 3), (3, 1)])
-
-    sides = shape(8, TILES * LANES)
-    src = call(sources, "sources", [SMEM] * 2 + [WHOLE] * 4, (shape(ZS * 8, LANES), sides, sides), cost=1 << 28)(
-        place, pulse_rates, plan.T, bore_x[None, :], bore_y[None, :], side_cells()
-    )
-    ids = jnp.pad(layer_ids, (0, LANES - NZ))[None, :]
     table = call(
         coefs,
         "coefs",
         [SMEM] * 3 + [WHOLE],
         shape(POWERS, 2 * LANES, 2 * LANES, dtype=BF16),
         [pltpu.VMEM((LEVELS, STEPS + 1, POWERS * ZS, LANES), F32)],
-        cost=1 << 28,
+        cost=4600 << 20,
     )(place, lateral_number, vertical_number, ids)
+    own, table = lax.optimization_barrier((own, table))
+    other = lax.ppermute(own, "level", [(0, 2), (2, 0), (1, 3), (3, 1)])
+    room = lambda span: [pltpu.VMEM((PAIRS, span * BLOCKS, LANES), F32)]
+    total = lambda span: [pltpu.VMEM((HALF, span * BLOCKS, LANES), F32)]
+    inner = call(
+        bulk,
+        "bulk",
+        [SMEM] + [WHOLE] * 5,
+        shape(HALF, LANES, LANES),
+        room(SPAN) * 3 + total(SPAN),
+        cost=8000 << 20,
+    )(place, kept, far, near, src, table)
     result = call(
-        evolve,
-        "evolve",
-        [SMEM] + [WHOLE] * 9,
-        shape(NZ * ROWS, LANES),
-        [
-            pltpu.VMEM((PAIRS, WIDE, LANES), F32),
-            pltpu.VMEM((2, TILES * LANES, LANES), F32),
-            pltpu.VMEM((PAIRS, WIDE, LANES), F32),
-            pltpu.VMEM((PAIRS, WIDE, LANES), F32),
-            pltpu.VMEM((HALF, WIDE, LANES), F32),
-        ],
-    )(place, flat, above, below, own, other, *src, table)
+        rim,
+        "rim",
+        [SMEM] + [WHOLE] * 6,
+        whole,
+        room(RIM_SPAN) + [pltpu.VMEM((2, TILES * LANES, LANES), F32)] + room(RIM_SPAN) * 2 + total(RIM_SPAN),
+        cost=4000 << 20,
+    )(place, own, other, src_left, src_right, table, inner)
     return result.reshape(1, NZ, ROWS, LANES)
 
 

time: 44.6 us -> 39.3 us (0.88)
  the two profiles are of different devices: /device:TPU:26 before, /device:TPU:24 now
where the time goes in v3:
time: 39.3 us; the launch traced here: 39.1 us
  starting transfers between devices  19.6 us (50%)
  Pallas kernels  17.8 us (45%)
  local copies, waits for them, and re-layouts  1.26 us (3%)
    ppermute x1, starting transfers between devices, on_device(): own = lax.ppermute(strips, ('level', 'ty'), route)  12 us
    pallas_call x1, Pallas kernels, on_device(): call(bulk, 'bulk', [SMEM] + [WHOLE] * 5, shape(HALF, LANES, LANES), room(...  5.87 us
    ppermute x1, starting transfers between devices, on_device(): near = lax.ppermute(near, 'tx', pairs(0))  4.75 us
    pallas_call x1, Pallas kernels, on_device(): call(coefs, 'coefs', [SMEM] * 3 + [WHOLE], shape(POWERS, 2 * LANES, 2 * L...  3.99 us
    pallas_call x1, Pallas kernels, on_device(): call(rim, 'rim', [SMEM] + [WHOLE] * 6, whole, room(RIM_SPAN) + [pltpu.VME...  3.59 us
    ppermute x1, starting transfers between devices, on_device(): other = lax.ppermute(own, 'level', [(0, 2), (2, 0), (1, 3), (3, 1)])  2.1 us
    pallas_call x1, Pallas kernels, on_device(): call(sources, 'sources', [SMEM] * 2 + [WHOLE] * 4, (shape(ZS * 8, LANES),...  1.66 us
    unnamed x18, local copies, waits for them, and re-layouts  1.17 us
  transfers between devices with their start and end apart: 4, of which 1 were waited for; matrix products, arithmetic and copies ran while one was open for 0% of the time, Pallas kernels for 32%

profile of v3, /device:TPU:24, one launch (start us, length us, event | category | flops | bytes accessed | tf_op | source)
XLA Modules:
  0.0 39.1 jit_solution(6452945219486333291)
XLA Ops:
  0.0 0.1 stack.15.place_ref
  0.1 0.0 copy-start
  0.1 1.1 %copy-done = f32[48,32,128]{2,1,0:T(8,128)S(1)} copy-done((f32[48,32,128]{2,1,0:T(8,128)S(1)}, f32[48,32,128]{2,1,0:T(8,128)}, u32[]{:S(2)}) %copy-start) | copy-done | bytes 786456
  1.2 0.0 copy-start.1
  1.2 0.0 copy-start.2
  1.2 0.0 copy-start.3
  1.2 0.0 copy-start.7
  1.2 0.8 %edge_rows.1 = (f32[9,48,128]{2,1,0:T(8,128)S(1)}, f32[9,48,128]{2,1,0:T(8,128)S(1)}, f32[1536,128]{1,0:T(8,128)S(1)}) custom-call(s32[5]{0:T(128)S(1)} %stack.15.place_ref, f32[1536,128]{1,0:T(8,128)S(1)} %bitcast.10), custom_call_target="tpu_custom_call" | custom-call | flops 838860800 | bytes 1048576 | tf_op jit(solution)/shard_map/edge_rows/pallas_call | solution.py:393
  2.1 0.7 %collective-permute-start = (f32[9,48,128]{2,1,0:T(8,128)S(1)}, f32[9,48,128]{2,1,0:T(8,128)S(1)}, u32[]{:S(2)}, u32[]{:S(2)}) collective-permute-start(f32[9,48,128]{2,1,0:T(8,128)S(1)} %get-tuple-element.20), channel_id=1, source_target_pairs={{16,32},{32,16},{48,64},{64,48},{80,96},{96,80},{17,33},{33,17},{4... | collective-permute-start | bytes 663560 | tf_op jit(solution)/shard_map/ppermute | solution.py:395
  2.8 4.7 %collective-permute-start.1 = (f32[9,48,128]{2,1,0:T(8,128)S(1)}, f32[9,48,128]{2,1,0:T(8,128)S(1)}, u32[]{:S(2)}, u32[]{:S(2)}) collective-permute-start(f32[9,48,128]{2,1,0:T(8,128)S(1)} %get-tuple-element.21), channel_id=1, source_target_pairs={{0,16},{16,0},{32,48},{48,32},{64,80},{80,64},{96,112},{112,96},{1... | collective-permute-start | bytes 663560 | tf_op jit(solution)/shard_map/ppermute | solution.py:396
  7.5 0.0 copy-done.1
  7.5 0.0 copy-done.2
  7.5 0.0 copy-done.3
  7.6 0.0 copy-done.4
  7.6 0.0 copy-done.7
  7.6 1.7 %sources.1 = (f32[448,128]{1,0:T(8,128)S(1)}, f32[8,384]{1,0:T(8,128)S(1)}, f32[8,384]{1,0:T(8,128)S(1)}) custom-call(s32[5]{0:T(128)S(1)} %stack.15.place_ref, f32[8]{0:T(128)S(1)} %copy-done.4, s32[7,1024]{1,0:T(8,128)S(1)} %bitcast.11, s32[1,1024]{1,0:T(1,128)S(1)} %bitcast.12, s32[1,1024]{1,0:T(1,128)S(1)} %bitcast.13, f32[8,384]{1,0:T(8,128)S(1)} %copy-done.7), custom_call_target="tpu_custom_call" | custom-call | flops 1782579200 | bytes 1048576 | tf_op jit(solution)/shard_map/sources/pallas_call | solution.py:400
  9.2 1.1 %own_columns.1.strips_ref = f32[3,48,128]{2,1,0:T(8,128)S(1)} custom-call(s32[5]{0:T(128)S(1)} %stack.15.place_ref, f32[1536,128]{1,0:T(8,128)S(1)} %get-tuple-element.17.u_ref), custom_call_target="tpu_custom_call" | custom-call | flops 1048576000 | bytes 1048576 | tf_op jit(solution)/shard_map/own_columns/pallas_call | solution.py:398
  10.3 0.0 copy-done.8
  10.4 0.0 copy-start.5
  10.4 0.0 copy-start.6
  10.4 0.0 collective-permute-done.far_ref
  10.4 0.0 collective-permute-done.1.near_ref
  10.4 0.7 %edge_columns.1 = f32[3,48,128]{2,1,0:T(8,128)S(1)} custom-call(s32[5]{0:T(128)S(1)} %stack.15.place_ref, f32[3,48,128]{2,1,0:T(8,128)S(1)} %own_columns.1.strips_ref, f32[9,48,128]{2,1,0:T(8,128)S(1)} %collective-permute-done.far_ref, f32[9,48,128]{2,1,0:T(8,128)S(1)} %collective-permute-done.1.near_ref), custom_call_target="tpu_custom_call" | custom-call | flops 838860800 | bytes 1048576 | tf_op jit(solution)/shard_map/edge_columns/pallas_call | solution.py:404
  11.1 12.0 %collective-permute-start.2 = (f32[3,48,128]{2,1,0:T(8,128)S(1)}, f32[3,48,128]{2,1,0:T(8,128)S(1)}, u32[]{:S(2)}, u32[]{:S(2)}) collective-permute-start(f32[3,48,128]{2,1,0:T(8,128)S(1)} %edge_columns.1), channel_id=1, source_target_pairs={{256,1},{1,256},{384,129},{129,384},{257,2},{2,257},{385,130},{130... | collective-permute-start | bytes 221192 | tf_op jit(solution)/shard_map/ppermute | solution.py:414
  23.2 0.0 copy-done.5
  23.2 0.0 copy-done.6
  23.2 4.0 %coefs.1.coef_ref = bf16[10,256,256]{2,1,0:T(8,128)(2,1)S(1)} custom-call(s32[5]{0:T(128)S(1)} %stack.15.place_ref, f32[6]{0:T(128)S(1)} %copy-done.5, f32[6]{0:T(128)S(1)} %copy-done.6, s32[1,128]{1,0:T(1,128)S(1)} %pad_bitcast_fusion.ids_ref), custom_call_target="tpu_custom_call" | custom-call | flops 4823449600 | bytes 1048576 | tf_op jit(solution)/shard_map/coefs/pallas_call | solution.py:415
  27.2 0.0 collective-permute-done.2.own_ref
  27.2 2.1 %collective-permute-start.3 = (f32[3,48,128]{2,1,0:T(8,128)S(1)}, f32[3,48,128]{2,1,0:T(8,128)S(1)}, u32[]{:S(2)}, u32[]{:S(2)}) collective-permute-start(f32[3,48,128]{2,1,0:T(8,128)S(1)} %collective-permute-done.2.own_ref), channel_id=1, source_target_pairs={{0,256},{256,0},{128,384},{384,128},{1,257},{257,1},{129,385},{385... | collective-permute-start | bytes 221192 | tf_op jit(solution)/shard_map/ppermute | solution.py:424
  29.3 5.9 %bulk.1.bulk_ref = f32[16,128,128]{2,1,0:T(8,128)S(1)} custom-call(s32[5]{0:T(128)S(1)} %stack.15.place_ref, f32[1536,128]{1,0:T(8,128)S(1)} %get-tuple-element.17.u_ref, f32[9,48,128]{2,1,0:T(8,128)S(1)} %collective-permute-done.far_ref, f32[9,48,128]{2,1,0:T(8,128)S(1)} %collective-permute-done.1.near_ref, f32[448,128]{1,0:T(8,128)S(1)} %get-tuple-element.28.src_ref, ...), custom_call_target="tpu_custom_call" | custom-call | flops 8388608000 | bytes 1048576 | tf_op jit(solution)/shard_map/bulk/pallas_call | solution.py:427
  35.2 0.3 collective-permute-done.3.other_ref
  35.5 3.6 %rim.1 = f32[1536,128]{1,0:T(8,128)} custom-call(s32[5]{0:T(128)S(1)} %stack.15.place_ref, f32[3,48,128]{2,1,0:T(8,128)S(1)} %collective-permute-done.2.own_ref, f32[3,48,128]{2,1,0:T(8,128)S(1)} %collective-permute-done.3.other_ref, f32[8,384]{1,0:T(8,128)S(1)} %get-tuple-element.25.src_left_ref, f32[8,384]{1,0:T(8,128)S(1)} %get-tuple-element.26.src_right_ref, ...), custom_call_target="tpu_custom_call" | custom-call | flops 4194304000 | bytes 1048576 | tf_op jit(solution)/shard_map/rim/pallas_call | solution.py:435
  (3 shorter events, 0.0 us)
Async XLA Ops:
  0.1 1.1 %copy-start = (f32[48,32,128]{2,1,0:T(8,128)S(1)}, f32[48,32,128]{2,1,0:T(8,128)}, u32[]{:S(2)}) copy-start(f32[48,32,128]{2,1,0:T(8,128)} %param.9) | copy-start | bytes 2359300
  1.2 6.3 %copy-start.1 = (s32[1024,7]{0,1:T(8,128)S(1)}, s32[1024,7]{0,1:T(8,128)}, u32[]{:S(2)}) copy-start(s32[1024,7]{0,1:T(8,128)} %param.16) | copy-start | bytes 86020
  1.2 6.3 %copy-start.2 = (s32[1024]{0:T(1024)S(1)}, s32[1024]{0:T(1024)}, u32[]{:S(2)}) copy-start(s32[1024]{0:T(1024)} %param.14) | copy-start | bytes 12292
  1.2 6.3 %copy-start.3 = (s32[1024]{0:T(1024)S(1)}, s32[1024]{0:T(1024)}, u32[]{:S(2)}) copy-start(s32[1024]{0:T(1024)} %param.15) | copy-start | bytes 12292
  1.2 6.3 %copy-start.4 = (f32[8]{0:T(128)S(1)}, f32[8]{0:T(128)}, u32[]{:S(2)}) copy-start(f32[8]{0:T(128)} %rates_ref.1) | copy-start | bytes 100
  1.2 6.3 %copy-start.7 = (f32[8,384]{1,0:T(8,128)S(1)}, f32[8,384]{1,0:T(8,128)}, u32[]{:S(2)}) copy-start(f32[8,384]{1,0:T(8,128)} %constant.22.clone.cells_ref) | copy-start | bytes 36868
  2.1 8.3 %collective-permute-start = (f32[9,48,128]{2,1,0:T(8,128)S(1)}, f32[9,48,128]{2,1,0:T(8,128)S(1)}, u32[]{:S(2)}, u32[]{:S(2)}) collective-permute-start(f32[9,48,128]{2,1,0:T(8,128)S(1)} %get-tuple-element.20), channel_id=1, source_target_pairs={{16,32},{32,16},{48,64},{64,48},{80,96},{96,80},{17,33},{33,17},{4... | collective-permute-start | bytes 663560 | tf_op jit(solution)/shard_map/ppermute | solution.py:395
  2.8 7.6 %collective-permute-start.1 = (f32[9,48,128]{2,1,0:T(8,128)S(1)}, f32[9,48,128]{2,1,0:T(8,128)S(1)}, u32[]{:S(2)}, u32[]{:S(2)}) collective-permute-start(f32[9,48,128]{2,1,0:T(8,128)S(1)} %get-tuple-element.21), channel_id=1, source_target_pairs={{0,16},{16,0},{32,48},{48,32},{64,80},{80,64},{96,112},{112,96},{1... | collective-permute-start | bytes 663560 | tf_op jit(solution)/shard_map/ppermute | solution.py:396
  9.2 1.1 %copy-start.8 = (s32[48]{0:T(128)S(1)}, s32[48]{0:T(128)}, u32[]{:S(2)}) copy-start(s32[48]{0:T(128)} %param.10) | copy-start | bytes 580
  10.4 12.8 %copy-start.5 = (f32[6]{0:T(128)S(1)}, f32[6]{0:T(128)}, u32[]{:S(2)}) copy-start(f32[6]{0:T(128)} %lateral_ref.1) | copy-start | bytes 76
  10.4 12.8 %copy-start.6 = (f32[6]{0:T(128)S(1)}, f32[6]{0:T(128)}, u32[]{:S(2)}) copy-start(f32[6]{0:T(128)} %vertical_ref.1) | copy-start | bytes 76
  11.1 16.1 %collective-permute-start.2 = (f32[3,48,128]{2,1,0:T(8,128)S(1)}, f32[3,48,128]{2,1,0:T(8,128)S(1)}, u32[]{:S(2)}, u32[]{:S(2)}) collective-permute-start(f32[3,48,128]{2,1,0:T(8,128)S(1)} %edge_columns.1), channel_id=1, source_target_pairs={{256,1},{1,256},{384,129},{129,384},{257,2},{2,257},{385,130},{130... | collective-permute-start | bytes 221192 | tf_op jit(solution)/shard_map/ppermute | solution.py:414
  27.2 8.3 %collective-permute-start.3 = (f32[3,48,128]{2,1,0:T(8,128)S(1)}, f32[3,48,128]{2,1,0:T(8,128)S(1)}, u32[]{:S(2)}, u32[]{:S(2)}) collective-permute-start(f32[3,48,128]{2,1,0:T(8,128)S(1)} %collective-permute-done.2.own_ref), channel_id=1, source_target_pairs={{0,256},{256,0},{128,384},{384,128},{1,257},{257,1},{129,385},{385... | collective-permute-start | bytes 221192 | tf_op jit(solution)/shard_map/ppermute | solution.py:424

commit v4 on v3

--- a/solution.py
+++ b/solution.py
@@ -164,13 +164,13 @@
     inverse = rhs / wide(mid)
     inverse = jnp.concatenate([inverse, jnp.zeros((LANES - NZ, LANES), F32)], axis=0)
     high = inverse.astype(BF16).astype(F32)
-    weights = high + pltpu.roll(inverse - high, 64, axis=1)
-    weights = jnp.concatenate([weights, high], axis=0).astype(BF16)
+    weights = jnp.concatenate([high, inverse - high], axis=1)
+    weights = jnp.concatenate([weights, weights], axis=0).astype(BF16)
 
     def solve(blocks):
         high, low = split(jnp.concatenate(blocks, axis=0))
         both = jnp.dot(jnp.concatenate([high, low], axis=1), weights, preferred_element_type=F32)
-        return both + pltpu.roll(both, 64, axis=1)
+        return both[:, :LANES] + both[:, LANES:]
 
     row_id = lax.broadcasted_iota(jnp.int32, (ZS, LANES), 0)
     lane_id = lax.broadcasted_iota(jnp.int32, (ZS, LANES), 1)
@@ -178,7 +178,6 @@
     profile = (lane_id >= 2) & (lane_id < NZ - 4)
     source = [((row_id == NZ + n) & profile).astype(F32) for n in range(STEPS + 1)]
     slope = jnp.broadcast_to(lat[:1], (ZS, LANES))
-    stay = 1.0 - 4.0 * slope
 
     degree = lambda p, n: 0 if n == 0 else n + p
 
@@ -202,27 +201,22 @@
         count = degree(p, n + 1) + 1
         blocks, rest, last = [], [], None
         for k in range(count):
+            u = get(p, n, k)
             if p == 0:
-                g = get(0, n, k)
-                tail, add = None, source[n]
+                kept, g, add = u, u, source[n]
             else:
                 b, c = get(p - 1, n, k), get(p - 1, n + 1, k)
                 if n == 0:
-                    w = total((0.5, b), (0.5, c))
-                    g, add = w, 0.5 * source[0] + 0.5 * source[1]
+                    q = total((0.5, c), (-0.5, b))
+                    add = 0.5 * source[0] + 0.5 * source[1]
                 else:
-                    w = total((-1.0 / 12.0, get(p - 1, n - 1, k)), (8.0 / 12.0, b), (5.0 / 12.0, c))
-                    g = total((1.0, get(p, n, k)), (-1.0, b), (1.0, w))
+                    q = total((7.0 / 12.0, c), (-8.0 / 12.0, b), (1.0 / 12.0, get(p - 1, n - 1, k)))
                     add = (-source[n - 1] + 8.0 * source[n] + 5.0 * source[n + 1]) * (1.0 / 12.0)
-                tail = total((1.0, b), (-1.0, c))
-                rest.append(total((1.0, c), (-1.0, w)))
-            parts = [
-                (1.0, None if g is None else stay * g),
-                (1.0, None if last is None else slope * last),
-                (1.0, tail),
-                (1.0, add if k == 0 else None),
-            ]
-            blocks.append(total(*parts))
+                kept = total((1.0, u), (-1.0, q))
+                g = total((1.0, kept), (1.0, c), (-1.0, b))
+                rest.append(q)
+            spread = total((1.0, last), (-4.0, g))
+            blocks.append(total((1.0, kept), (1.0, None if spread is None else slope * spread), (1.0, add if k == 0 else None)))
             last = g
         solved = solve(blocks)
         for k in range(count):
@@ -331,7 +325,7 @@
 
 def rim(
     place_ref, own_ref, other_ref, src_left_ref, src_right_ref, coef_ref, bulk_ref,
-    out_ref, line_ref, side_ref, field_ref, other_field_ref, total_ref,
+    out_ref, line_ref, side_ref, field_ref, other_field_ref, total_ref, result_ref, sems,
 ):
     low_level = place_ref[0] < 2
     blank = jnp.zeros((SLOT - ZS, LANES), F32)
@@ -355,26 +349,34 @@
         for j in range(RIM_SPAN):
             field_ref[i, 8 * j : 8 * j + 8, :] = line_ref[i, pl.ds(j, BLOCKS, stride=RIM_SPAN), :]
     powers((field_ref, other_field_ref), total_ref, coef_ref, RIM_SPAN, lambda j, new: new, *grid_rows(place_ref))
+    copies = []
     for i in range(HALF):
         for j in range(RIM_SPAN):
             line_ref[i, pl.ds(j, BLOCKS, stride=RIM_SPAN), :] = total_ref[i, 8 * j : 8 * j + 8, :]
         inner = LANES - 2 * (RIM - HALO)
         change = [line_ref[i, HALO:RIM, :], jnp.zeros((inner, LANES), F32), line_ref[i, RIM : 2 * RIM - HALO, :]]
         result = (bulk_ref[i] + jnp.concatenate(change, axis=0)).T
-        out_ref[pl.ds(i, NZ, stride=ROWS), :] = result[:NZ]
-        out_ref[pl.ds(i + HALF, NZ, stride=ROWS), :] = result[SLOT : SLOT + NZ]
+        group, row = divmod(i, 8)
+        result_ref[group, pl.ds(row, NZ, stride=8), :] = result[:NZ]
+        result_ref[group + 2, pl.ds(row, NZ, stride=8), :] = result[SLOT : SLOT + NZ]
+        if row == 7:
+            for g in (group, group + 2):
+                copies.append(pltpu.make_async_copy(result_ref.at[g].reshape(NZ, 8, LANES), out_ref.at[:, pl.ds(8 * g, 8), :], sems.at[g]))
+                copies[-1].start()
+    for copy in copies:
+        copy.wait()
 
 
 SMEM = pl.BlockSpec(memory_space=pltpu.SMEM)
 WHOLE = pl.BlockSpec(memory_space=pltpu.VMEM)
 
 
-def call(kernel, name, ins, outs, scratch=(), cost=0):
+def call(kernel, name, ins, outs, scratch=(), cost=0, out_spec=None):
     return pl.pallas_call(
         kernel,
         out_shape=outs,
         in_specs=ins,
-        out_specs=jax.tree.map(lambda _: WHOLE, outs),
+        out_specs=out_spec or jax.tree.map(lambda _: WHOLE, outs),
         scratch_shapes=list(scratch),
         compiler_params=pltpu.CompilerParams(vmem_limit_bytes=VMEM),
         cost_estimate=pl.CostEstimate(flops=cost, bytes_accessed=1 << 20, transcendentals=0),
@@ -436,8 +438,13 @@
         rim,
         "rim",
         [SMEM] + [WHOLE] * 6,
-        whole,
-        room(RIM_SPAN) + [pltpu.VMEM((2, TILES * LANES, LANES), F32)] + room(RIM_SPAN) * 2 + total(RIM_SPAN),
+        shape(NZ, ROWS, LANES),
+        room(RIM_SPAN)
+        + [pltpu.VMEM((2, TILES * LANES, LANES), F32)]
+        + room(RIM_SPAN) * 2
+        + total(RIM_SPAN)
+        + [pltpu.VMEM((ROWS // 8, NZ * 8, LANES), F32), pltpu.SemaphoreType.DMA((ROWS // 8,))],
+        out_spec=pl.BlockSpec(memory_space=pl.ANY),
         cost=4000 << 20,
     )(place, own, other, src_left, src_right, table, inner)
     return result.reshape(1, NZ, ROWS, LANES)

time: 39.3 us -> 38.3 us (0.975)
  the two profiles are of different devices: /device:TPU:24 before, /device:TPU:26 now
where the time goes in v4:
time: 38.3 us; the launch traced here: 38.1 us
  starting transfers between devices  19.4 us (51%)
  Pallas kernels  16.8 us (44%)
  local copies, waits for them, and re-layouts  1.26 us (3%)
  waiting for transfers between devices  0.49 us (1%)
    ppermute x1, starting transfers between devices, on_device(): own = lax.ppermute(strips, ('level', 'ty'), route)  12 us
    pallas_call x1, Pallas kernels, on_device(): call(bulk, 'bulk', [SMEM] + [WHOLE] * 5, shape(HALF, LANES, LANES), room(...  5.87 us
    pallas_call x1, Pallas kernels, on_device(): call(coefs, 'coefs', [SMEM] * 3 + [WHOLE], shape(POWERS, 2 * LANES, 2 * L...  3.52 us
    ppermute x1, starting transfers between devices, on_device(): near = lax.ppermute(near, 'tx', pairs(0))  3.5 us
    pallas_call x1, Pallas kernels, on_device(): call(rim, 'rim', [SMEM] + [WHOLE] * 6, shape(NZ, ROWS, LANES), room(RIM_S...  3.1 us
    ppermute x1, starting transfers between devices, on_device(): far = lax.ppermute(far, 'tx', pairs(1))  1.92 us
    ppermute x1, starting transfers between devices, on_device(): other = lax.ppermute(own, 'level', [(0, 2), (2, 0), (1, 3), (3, 1)])  1.92 us
    pallas_call x1, Pallas kernels, on_device(): call(sources, 'sources', [SMEM] * 2 + [WHOLE] * 4, (shape(ZS * 8, LANES),...  1.66 us
  transfers between devices with their start and end apart: 4, of which 1 were waited for; matrix products, arithmetic and copies ran while one was open for 0% of the time, Pallas kernels for 32%

profile of v4, /device:TPU:26, one launch (start us, length us, event | category | flops | bytes accessed | tf_op | source)
XLA Modules:
  0.0 38.1 jit_solution(7301353034172575827)
XLA Ops:
  0.0 0.1 stack.15.place_ref
  0.1 0.0 copy-start
  0.1 1.1 %copy-done = f32[48,32,128]{2,1,0:T(8,128)S(1)} copy-done((f32[48,32,128]{2,1,0:T(8,128)S(1)}, f32[48,32,128]{2,1,0:T(8,128)}, u32[]{:S(2)}) %copy-start) | copy-done | bytes 786456
  1.2 0.0 copy-start.1
  1.2 0.0 copy-start.3
  1.2 0.0 copy-start.4
  1.2 0.0 copy-start.7
  1.2 0.8 %edge_rows.1 = (f32[9,48,128]{2,1,0:T(8,128)S(1)}, f32[9,48,128]{2,1,0:T(8,128)S(1)}, f32[1536,128]{1,0:T(8,128)S(1)}) custom-call(s32[5]{0:T(128)S(1)} %stack.15.place_ref, f32[1536,128]{1,0:T(8,128)S(1)} %bitcast.10), custom_call_target="tpu_custom_call" | custom-call | flops 838860800 | bytes 1048576 | tf_op jit(solution)/shard_map/edge_rows/pallas_call | solution.py:395
  2.1 1.9 %collective-permute-start = (f32[9,48,128]{2,1,0:T(8,128)S(1)}, f32[9,48,128]{2,1,0:T(8,128)S(1)}, u32[]{:S(2)}, u32[]{:S(2)}) collective-permute-start(f32[9,48,128]{2,1,0:T(8,128)S(1)} %get-tuple-element.20), channel_id=1, source_target_pairs={{16,32},{32,16},{48,64},{64,48},{80,96},{96,80},{17,33},{33,17},{4... | collective-permute-start | bytes 663560 | tf_op jit(solution)/shard_map/ppermute | solution.py:397
  4.0 3.5 %collective-permute-start.1 = (f32[9,48,128]{2,1,0:T(8,128)S(1)}, f32[9,48,128]{2,1,0:T(8,128)S(1)}, u32[]{:S(2)}, u32[]{:S(2)}) collective-permute-start(f32[9,48,128]{2,1,0:T(8,128)S(1)} %get-tuple-element.21), channel_id=1, source_target_pairs={{0,16},{16,0},{32,48},{48,32},{64,80},{80,64},{96,112},{112,96},{1... | collective-permute-start | bytes 663560 | tf_op jit(solution)/shard_map/ppermute | solution.py:398
  7.5 0.0 copy-done.1
  7.5 0.0 copy-done.2
  7.5 0.0 copy-done.3
  7.6 0.0 copy-done.4
  7.6 0.0 copy-done.7
  7.6 1.7 %sources.1 = (f32[448,128]{1,0:T(8,128)S(1)}, f32[8,384]{1,0:T(8,128)S(1)}, f32[8,384]{1,0:T(8,128)S(1)}) custom-call(s32[5]{0:T(128)S(1)} %stack.15.place_ref, f32[8]{0:T(128)S(1)} %copy-done.4, s32[7,1024]{1,0:T(8,128)S(1)} %bitcast.11, s32[1,1024]{1,0:T(1,128)S(1)} %bitcast.12, s32[1,1024]{1,0:T(1,128)S(1)} %bitcast.13, f32[8,384]{1,0:T(8,128)S(1)} %copy-done.7), custom_call_target="tpu_custom_call" | custom-call | flops 1782579200 | bytes 1048576 | tf_op jit(solution)/shard_map/sources/pallas_call | solution.py:402
  9.2 1.1 %own_columns.1.strips_ref = f32[3,48,128]{2,1,0:T(8,128)S(1)} custom-call(s32[5]{0:T(128)S(1)} %stack.15.place_ref, f32[1536,128]{1,0:T(8,128)S(1)} %get-tuple-element.17.u_ref), custom_call_target="tpu_custom_call" | custom-call | flops 1048576000 | bytes 1048576 | tf_op jit(solution)/shard_map/own_columns/pallas_call | solution.py:400
  10.3 0.0 copy-done.8
  10.4 0.0 copy-start.5
  10.4 0.0 copy-start.6
  10.4 0.0 collective-permute-done.far_ref
  10.4 0.0 collective-permute-done.1.near_ref
  10.4 0.7 %edge_columns.1 = f32[3,48,128]{2,1,0:T(8,128)S(1)} custom-call(s32[5]{0:T(128)S(1)} %stack.15.place_ref, f32[3,48,128]{2,1,0:T(8,128)S(1)} %own_columns.1.strips_ref, f32[9,48,128]{2,1,0:T(8,128)S(1)} %collective-permute-done.far_ref, f32[9,48,128]{2,1,0:T(8,128)S(1)} %collective-permute-done.1.near_ref), custom_call_target="tpu_custom_call" | custom-call | flops 838860800 | bytes 1048576 | tf_op jit(solution)/shard_map/edge_columns/pallas_call | solution.py:406
  11.1 12.0 %collective-permute-start.2 = (f32[3,48,128]{2,1,0:T(8,128)S(1)}, f32[3,48,128]{2,1,0:T(8,128)S(1)}, u32[]{:S(2)}, u32[]{:S(2)}) collective-permute-start(f32[3,48,128]{2,1,0:T(8,128)S(1)} %edge_columns.1), channel_id=1, source_target_pairs={{256,1},{1,256},{384,129},{129,384},{257,2},{2,257},{385,130},{130... | collective-permute-start | bytes 221192 | tf_op jit(solution)/shard_map/ppermute | solution.py:416
  23.2 0.0 copy-done.5
  23.2 0.0 copy-done.6
  23.2 3.5 %coefs.1.coef_ref = bf16[10,256,256]{2,1,0:T(8,128)(2,1)S(1)} custom-call(s32[5]{0:T(128)S(1)} %stack.15.place_ref, f32[6]{0:T(128)S(1)} %copy-done.5, f32[6]{0:T(128)S(1)} %copy-done.6, s32[1,128]{1,0:T(1,128)S(1)} %pad_bitcast_fusion.ids_ref), custom_call_target="tpu_custom_call" | custom-call | flops 4823449600 | bytes 1048576 | tf_op jit(solution)/shard_map/coefs/pallas_call | solution.py:417
  26.7 0.0 collective-permute-done.2.own_ref
  26.7 1.9 %collective-permute-start.3 = (f32[3,48,128]{2,1,0:T(8,128)S(1)}, f32[3,48,128]{2,1,0:T(8,128)S(1)}, u32[]{:S(2)}, u32[]{:S(2)}) collective-permute-start(f32[3,48,128]{2,1,0:T(8,128)S(1)} %collective-permute-done.2.own_ref), channel_id=1, source_target_pairs={{0,256},{256,0},{128,384},{384,128},{1,257},{257,1},{129,385},{385... | collective-permute-start | bytes 221192 | tf_op jit(solution)/shard_map/ppermute | solution.py:426
  28.7 5.9 %bulk.1.bulk_ref = f32[16,128,128]{2,1,0:T(8,128)S(1)} custom-call(s32[5]{0:T(128)S(1)} %stack.15.place_ref, f32[1536,128]{1,0:T(8,128)S(1)} %get-tuple-element.17.u_ref, f32[9,48,128]{2,1,0:T(8,128)S(1)} %collective-permute-done.far_ref, f32[9,48,128]{2,1,0:T(8,128)S(1)} %collective-permute-done.1.near_ref, f32[448,128]{1,0:T(8,128)S(1)} %get-tuple-element.28.src_ref, ...), custom_call_target="tpu_custom_call" | custom-call | flops 8388608000 | bytes 1048576 | tf_op jit(solution)/shard_map/bulk/pallas_call | solution.py:429
  34.5 0.5 %collective-permute-done.3.other_ref = f32[3,48,128]{2,1,0:T(8,128)S(1)} collective-permute-done((f32[3,48,128]{2,1,0:T(8,128)S(1)}, f32[3,48,128]{2,1,0:T(8,128)S(1)}, u32[]{:S(2)}, u32[]{:S(2)}) %collective-permute-start.3) | collective-permute-done | bytes 73760 | tf_op jit(solution)/shard_map/ppermute | solution.py:426
  35.0 3.1 %rim.1 = f32[48,32,128]{2,1,0:T(8,128)} custom-call(s32[5]{0:T(128)S(1)} %stack.15.place_ref, f32[3,48,128]{2,1,0:T(8,128)S(1)} %collective-permute-done.2.own_ref, f32[3,48,128]{2,1,0:T(8,128)S(1)} %collective-permute-done.3.other_ref, f32[8,384]{1,0:T(8,128)S(1)} %get-tuple-element.25.src_left_ref, f32[8,384]{1,0:T(8,128)S(1)} %get-tuple-element.26.src_right_ref, ...), custom_call_target="tpu_custom_call" | custom-call | flops 4194304000 | bytes 1048576 | tf_op jit(solution)/shard_map/rim/pallas_call | solution.py:437
  (3 shorter events, 0.0 us)
Async XLA Ops:
  0.1 1.1 %copy-start = (f32[48,32,128]{2,1,0:T(8,128)S(1)}, f32[48,32,128]{2,1,0:T(8,128)}, u32[]{:S(2)}) copy-start(f32[48,32,128]{2,1,0:T(8,128)} %param.9) | copy-start | bytes 2359300
  1.2 6.3 %copy-start.1 = (s32[1024,7]{0,1:T(8,128)S(1)}, s32[1024,7]{0,1:T(8,128)}, u32[]{:S(2)}) copy-start(s32[1024,7]{0,1:T(8,128)} %param.16) | copy-start | bytes 86020
  1.2 6.3 %copy-start.2 = (s32[1024]{0:T(1024)S(1)}, s32[1024]{0:T(1024)}, u32[]{:S(2)}) copy-start(s32[1024]{0:T(1024)} %param.14) | copy-start | bytes 12292
  1.2 6.3 %copy-start.3 = (s32[1024]{0:T(1024)S(1)}, s32[1024]{0:T(1024)}, u32[]{:S(2)}) copy-start(s32[1024]{0:T(1024)} %param.15) | copy-start | bytes 12292
  1.2 6.3 %copy-start.4 = (f32[8]{0:T(128)S(1)}, f32[8]{0:T(128)}, u32[]{:S(2)}) copy-start(f32[8]{0:T(128)} %rates_ref.1) | copy-start | bytes 100
  1.2 6.3 %copy-start.7 = (f32[8,384]{1,0:T(8,128)S(1)}, f32[8,384]{1,0:T(8,128)}, u32[]{:S(2)}) copy-start(f32[8,384]{1,0:T(8,128)} %constant.22.clone.cells_ref) | copy-start | bytes 36868
  2.1 8.3 %collective-permute-start = (f32[9,48,128]{2,1,0:T(8,128)S(1)}, f32[9,48,128]{2,1,0:T(8,128)S(1)}, u32[]{:S(2)}, u32[]{:S(2)}) collective-permute-start(f32[9,48,128]{2,1,0:T(8,128)S(1)} %get-tuple-element.20), channel_id=1, source_target_pairs={{16,32},{32,16},{48,64},{64,48},{80,96},{96,80},{17,33},{33,17},{4... | collective-permute-start | bytes 663560 | tf_op jit(solution)/shard_map/ppermute | solution.py:397
  4.0 6.4 %collective-permute-start.1 = (f32[9,48,128]{2,1,0:T(8,128)S(1)}, f32[9,48,128]{2,1,0:T(8,128)S(1)}, u32[]{:S(2)}, u32[]{:S(2)}) collective-permute-start(f32[9,48,128]{2,1,0:T(8,128)S(1)} %get-tuple-element.21), channel_id=1, source_target_pairs={{0,16},{16,0},{32,48},{48,32},{64,80},{80,64},{96,112},{112,96},{1... | collective-permute-start | bytes 663560 | tf_op jit(solution)/shard_map/ppermute | solution.py:398
  9.2 1.1 %copy-start.8 = (s32[48]{0:T(128)S(1)}, s32[48]{0:T(128)}, u32[]{:S(2)}) copy-start(s32[48]{0:T(128)} %param.10) | copy-start | bytes 580
  10.4 12.8 %copy-start.5 = (f32[6]{0:T(128)S(1)}, f32[6]{0:T(128)}, u32[]{:S(2)}) copy-start(f32[6]{0:T(128)} %lateral_ref.1) | copy-start | bytes 76
  10.4 12.8 %copy-start.6 = (f32[6]{0:T(128)S(1)}, f32[6]{0:T(128)}, u32[]{:S(2)}) copy-start(f32[6]{0:T(128)} %vertical_ref.1) | copy-start | bytes 76
  11.1 15.6 %collective-permute-start.2 = (f32[3,48,128]{2,1,0:T(8,128)S(1)}, f32[3,48,128]{2,1,0:T(8,128)S(1)}, u32[]{:S(2)}, u32[]{:S(2)}) collective-permute-start(f32[3,48,128]{2,1,0:T(8,128)S(1)} %edge_columns.1), channel_id=1, source_target_pairs={{256,1},{1,256},{384,129},{129,384},{257,2},{2,257},{385,130},{130... | collective-permute-start | bytes 221192 | tf_op jit(solution)/shard_map/ppermute | solution.py:416
  26.7 8.3 %collective-permute-start.3 = (f32[3,48,128]{2,1,0:T(8,128)S(1)}, f32[3,48,128]{2,1,0:T(8,128)S(1)}, u32[]{:S(2)}, u32[]{:S(2)}) collective-permute-start(f32[3,48,128]{2,1,0:T(8,128)S(1)} %collective-permute-done.2.own_ref), channel_id=1, source_target_pairs={{0,256},{256,0},{128,384},{384,128},{1,257},{257,1},{129,385},{385... | collective-permute-start | bytes 221192 | tf_op jit(solution)/shard_map/ppermute | solution.py:426

commit v5 on v4

--- a/solution.py
+++ b/solution.py
@@ -20,6 +20,7 @@
 HALF = ROWS // 2
 PAIRS = HALF + 2 * HALO
 SLOT = LANES // 2
+LINE = 4
 BLOCKS = 8
 BACK = (POWERS - 1) // 2
 SPAN = (LANES + 2 * BACK) // BLOCKS
@@ -100,6 +101,14 @@
         for c in range(width):
             cells[:3, t * LANES + first + c] = (r - HALO, c - width, LANES + c)
     return cells
+
+
+def is_late(place_ref):
+    return lax.rem(place_ref[2], LINE) == LINE - 1
+
+
+def early_sources(place_ref, *refs):
+    pl.when(jnp.logical_not(is_late(place_ref)))(lambda: sources(place_ref, *refs))
 
 
 def sources(place_ref, rates_ref, plan_ref, x_ref, y_ref, cells_ref, centre_ref, left_ref, right_ref):
@@ -294,8 +303,22 @@
 
 
 def bulk(
-    place_ref, u_ref, far_ref, near_ref, src_ref, coef_ref, out_ref, line_ref, field_ref, other_field_ref, total_ref
+    place_ref, rates_ref, plan_ref, x_ref, y_ref, cells_ref, u_ref, far_ref, near_ref,
+    early_centre_ref, early_left_ref, early_right_ref, coef_ref, out_ref, left_ref, right_ref,
+    line_ref, field_ref, other_field_ref, total_ref, src_ref,
 ):
+    late = is_late(place_ref)
+
+    @pl.when(late)
+    def _():
+        sources(place_ref, rates_ref, plan_ref, x_ref, y_ref, cells_ref, src_ref, left_ref, right_ref)
+
+    @pl.when(jnp.logical_not(late))
+    def _():
+        src_ref[...] = early_centre_ref[...]
+        left_ref[...] = early_left_ref[...]
+        right_ref[...] = early_right_ref[...]
+
     ty = place_ref[2]
     even = lax.rem(place_ref[1], 2) == 0
     sublane = lax.broadcasted_iota(jnp.int32, (BLOCKS, LANES), 0)
@@ -399,9 +422,9 @@
     packed = shape(TILES, NZ, LANES)
     strips = call(own_columns, "own_columns", [SMEM, WHOLE], packed, cost=1000 << 20)(place, kept)
     sides = shape(8, TILES * LANES)
-    src, src_left, src_right = call(
-        sources, "sources", [SMEM] * 2 + [WHOLE] * 4, (shape(ZS * 8, LANES), sides, sides), cost=1700 << 20
-    )(place, pulse_rates, plan.T, bore_x[None, :], bore_y[None, :], side_cells())
+    planes = (shape(ZS * 8, LANES), sides, sides)
+    bores = (pulse_rates, plan.T, bore_x[None, :], bore_y[None, :], side_cells())
+    src = call(early_sources, "early_sources", [SMEM] * 2 + [WHOLE] * 4, planes, cost=1700 << 20)(place, *bores)
     strips, src = lax.optimization_barrier((strips, src))
     strips = call(edge_columns, "edge_columns", [SMEM] + [WHOLE] * 3, packed, cost=800 << 20)(
         place, strips, far, near
@@ -426,14 +449,14 @@
     other = lax.ppermute(own, "level", [(0, 2), (2, 0), (1, 3), (3, 1)])
     room = lambda span: [pltpu.VMEM((PAIRS, span * BLOCKS, LANES), F32)]
     total = lambda span: [pltpu.VMEM((HALF, span * BLOCKS, LANES), F32)]
-    inner = call(
+    inner, src_left, src_right = call(
         bulk,
         "bulk",
-        [SMEM] + [WHOLE] * 5,
-        shape(HALF, LANES, LANES),
-        room(SPAN) * 3 + total(SPAN),
+        [SMEM] * 2 + [WHOLE] * 11,
+        (shape(HALF, LANES, LANES), sides, sides),
+        room(SPAN) * 3 + total(SPAN) + [pltpu.VMEM((ZS * 8, LANES), F32)],
         cost=8000 << 20,
-    )(place, kept, far, near, src, table)
+    )(place, *bores, kept, far, near, *src, table)
     result = call(
         rim,
         "rim",

time: 38.3 us -> 37.5 us (0.979)
  starting transfers between devices: 19.4 us -> 18.3 us
    ppermute x1, starting transfers between devices: 12 us -> 10.9 us  [on_device(): own = lax.ppermute(strips, ('level', 'ty'), route)]
  transfers between devices with their start and end apart: 4 -> 4, of which waited for: 1 -> 1; matrix products, arithmetic and copies ran while one was open for 0% -> 0% of each run, Pallas kernels for 32% -> 33%
where the time goes in v5:
time: 37.5 us; the launch traced here: 37.3 us
  starting transfers between devices  18.3 us (49%)
  Pallas kernels  17 us (45%)
  local copies, waits for them, and re-layouts  1.26 us (3%)
  waiting for transfers between devices  0.39 us (1%)
    ppermute x1, starting transfers between devices, on_device(): own = lax.ppermute(strips, ('level', 'ty'), route)  10.9 us
    pallas_call x1, Pallas kernels, on_device(): call(bulk, 'bulk', [SMEM] * 2 + [WHOLE] * 11, (shape(HALF, LANES, LANES),...  6.08 us
    pallas_call x1, Pallas kernels, on_device(): call(coefs, 'coefs', [SMEM] * 3 + [WHOLE], shape(POWERS, 2 * LANES, 2 * L...  3.52 us
    ppermute x1, starting transfers between devices, on_device(): near = lax.ppermute(near, 'tx', pairs(0))  3.5 us
    pallas_call x1, Pallas kernels, on_device(): call(rim, 'rim', [SMEM] + [WHOLE] * 6, shape(NZ, ROWS, LANES), room(RIM_S...  3.08 us
    ppermute x1, starting transfers between devices, on_device(): far = lax.ppermute(far, 'tx', pairs(1))  1.92 us
    ppermute x1, starting transfers between devices, on_device(): other = lax.ppermute(own, 'level', [(0, 2), (2, 0), (1, 3), (3, 1)])  1.92 us
    pallas_call x1, Pallas kernels, on_device(): call(early_sources, 'early_sources', [SMEM] * 2 + [WHOLE] * 4, planes, co...  1.67 us
  transfers between devices with their start and end apart: 4, of which 1 were waited for; matrix products, arithmetic and copies ran while one was open for 0% of the time, Pallas kernels for 33%

profile of v5, /device:TPU:26, one launch (start us, length us, event | category | flops | bytes accessed | tf_op | source)
XLA Modules:
  0.0 37.3 jit_solution(319082729776063894)
XLA Ops:
  0.0 0.1 stack.15.place_ref
  0.1 0.0 copy-start
  0.1 1.1 %copy-done = f32[48,32,128]{2,1,0:T(8,128)S(1)} copy-done((f32[48,32,128]{2,1,0:T(8,128)S(1)}, f32[48,32,128]{2,1,0:T(8,128)}, u32[]{:S(2)}) %copy-start) | copy-done | bytes 786456
  1.2 0.0 copy-start.1
  1.2 0.0 copy-start.2
  1.2 0.0 copy-start.3
  1.2 0.0 copy-start.7
  1.2 0.8 %edge_rows.1 = (f32[9,48,128]{2,1,0:T(8,128)S(1)}, f32[9,48,128]{2,1,0:T(8,128)S(1)}, f32[1536,128]{1,0:T(8,128)S(1)}) custom-call(s32[5]{0:T(128)S(1)} %stack.15.place_ref, f32[1536,128]{1,0:T(8,128)S(1)} %bitcast.10), custom_call_target="tpu_custom_call" | custom-call | flops 838860800 | bytes 1048576 | tf_op jit(solution)/shard_map/edge_rows/pallas_call | solution.py:418
  2.1 1.9 %collective-permute-start = (f32[9,48,128]{2,1,0:T(8,128)S(1)}, f32[9,48,128]{2,1,0:T(8,128)S(1)}, u32[]{:S(2)}, u32[]{:S(2)}) collective-permute-start(f32[9,48,128]{2,1,0:T(8,128)S(1)} %get-tuple-element.27), channel_id=1, source_target_pairs={{16,32},{32,16},{48,64},{64,48},{80,96},{96,80},{17,33},{33,17},{4... | collective-permute-start | bytes 663560 | tf_op jit(solution)/shard_map/ppermute | solution.py:420
  4.0 3.5 %collective-permute-start.1 = (f32[9,48,128]{2,1,0:T(8,128)S(1)}, f32[9,48,128]{2,1,0:T(8,128)S(1)}, u32[]{:S(2)}, u32[]{:S(2)}) collective-permute-start(f32[9,48,128]{2,1,0:T(8,128)S(1)} %get-tuple-element.28), channel_id=1, source_target_pairs={{0,16},{16,0},{32,48},{48,32},{64,80},{80,64},{96,112},{112,96},{1... | collective-permute-start | bytes 663560 | tf_op jit(solution)/shard_map/ppermute | solution.py:421
  7.5 0.0 copy-done.1
  7.5 0.0 copy-done.2
  7.5 0.0 copy-done.3
  7.6 0.0 copy-done.6
  7.6 0.0 copy-done.7
  7.6 1.7 %early_sources.1 = (f32[448,128]{1,0:T(8,128)S(1)}, f32[8,384]{1,0:T(8,128)S(1)}, f32[8,384]{1,0:T(8,128)S(1)}) custom-call(s32[5]{0:T(128)S(1)} %stack.15.place_ref, f32[8]{0:T(128)S(1)} %copy-done.6, s32[7,1024]{1,0:T(8,128)S(1)} %bitcast.11, s32[1,1024]{1,0:T(1,128)S(1)} %bitcast.13, s32[1,1024]{1,0:T(1,128)S(1)} %bitcast.15, f32[8,384]{1,0:T(8,128)S(1)} %copy-done.7), custom_call_target="tpu_custom_call" | custom-call | flops 1782579200 | bytes 1048576 | tf_op jit(solution)/shard_map/early_sources/pallas_call | solution.py:427
  9.2 1.1 %own_columns.1.strips_ref = f32[3,48,128]{2,1,0:T(8,128)S(1)} custom-call(s32[5]{0:T(128)S(1)} %stack.15.place_ref, f32[1536,128]{1,0:T(8,128)S(1)} %get-tuple-element.22.u_ref), custom_call_target="tpu_custom_call" | custom-call | flops 1048576000 | bytes 1048576 | tf_op jit(solution)/shard_map/own_columns/pallas_call | solution.py:423
  10.4 0.0 copy-done.8
  10.4 0.0 copy-start.4
  10.4 0.0 copy-start.5
  10.4 0.0 collective-permute-done.far_ref
  10.4 0.0 collective-permute-done.1.near_ref
  10.4 0.7 %edge_columns.1 = f32[3,48,128]{2,1,0:T(8,128)S(1)} custom-call(s32[5]{0:T(128)S(1)} %stack.15.place_ref, f32[3,48,128]{2,1,0:T(8,128)S(1)} %own_columns.1.strips_ref, f32[9,48,128]{2,1,0:T(8,128)S(1)} %collective-permute-done.far_ref, f32[9,48,128]{2,1,0:T(8,128)S(1)} %collective-permute-done.1.near_ref), custom_call_target="tpu_custom_call" | custom-call | flops 838860800 | bytes 1048576 | tf_op jit(solution)/shard_map/edge_columns/pallas_call | solution.py:429
  11.1 10.9 %collective-permute-start.2 = (f32[3,48,128]{2,1,0:T(8,128)S(1)}, f32[3,48,128]{2,1,0:T(8,128)S(1)}, u32[]{:S(2)}, u32[]{:S(2)}) collective-permute-start(f32[3,48,128]{2,1,0:T(8,128)S(1)} %edge_columns.1), channel_id=1, source_target_pairs={{256,1},{1,256},{384,129},{129,384},{257,2},{2,257},{385,130},{130... | collective-permute-start | bytes 221192 | tf_op jit(solution)/shard_map/ppermute | solution.py:439
  22.1 0.0 copy-done.4
  22.1 0.0 copy-done.5
  22.1 3.5 %coefs.1.coef_ref = bf16[10,256,256]{2,1,0:T(8,128)(2,1)S(1)} custom-call(s32[5]{0:T(128)S(1)} %stack.15.place_ref, f32[6]{0:T(128)S(1)} %copy-done.4, f32[6]{0:T(128)S(1)} %copy-done.5, s32[1,128]{1,0:T(1,128)S(1)} %pad_bitcast_fusion.ids_ref), custom_call_target="tpu_custom_call" | custom-call | flops 4823449600 | bytes 1048576 | tf_op jit(solution)/shard_map/coefs/pallas_call | solution.py:440
  25.6 0.0 collective-permute-done.2.own_ref
  25.6 1.9 %collective-permute-start.3 = (f32[3,48,128]{2,1,0:T(8,128)S(1)}, f32[3,48,128]{2,1,0:T(8,128)S(1)}, u32[]{:S(2)}, u32[]{:S(2)}) collective-permute-start(f32[3,48,128]{2,1,0:T(8,128)S(1)} %collective-permute-done.2.own_ref), channel_id=1, source_target_pairs={{0,256},{256,0},{128,384},{384,128},{1,257},{257,1},{129,385},{385... | collective-permute-start | bytes 221192 | tf_op jit(solution)/shard_map/ppermute | solution.py:449
  27.6 6.1 %bulk.1 = (f32[16,128,128]{2,1,0:T(8,128)S(1)}, f32[8,384]{1,0:T(8,128)S(1)}, f32[8,384]{1,0:T(8,128)S(1)}) custom-call(s32[5]{0:T(128)S(1)} %stack.15.place_ref, f32[8]{0:T(128)S(1)} %copy-done.6, s32[7,1024]{1,0:T(8,128)S(1)} %bitcast.12, s32[1,1024]{1,0:T(1,128)S(1)} %bitcast.14, s32[1,1024]{1,0:T(1,128)S(1)} %bitcast.16, f32[8,384]{1,0:T(8,128)S(1)} %copy-done.7, ...), custom_call_target="tpu_custom_call" | custom-call | flops 8388608000 | bytes 1048576 | tf_op jit(solution)/shard_map/bulk/pallas_call | solution.py:452
  33.7 0.4 %collective-permute-done.3.other_ref = f32[3,48,128]{2,1,0:T(8,128)S(1)} collective-permute-done((f32[3,48,128]{2,1,0:T(8,128)S(1)}, f32[3,48,128]{2,1,0:T(8,128)S(1)}, u32[]{:S(2)}, u32[]{:S(2)}) %collective-permute-start.3) | collective-permute-done | bytes 73760 | tf_op jit(solution)/shard_map/ppermute | solution.py:449
  34.0 3.1 %rim.1 = f32[48,32,128]{2,1,0:T(8,128)} custom-call(s32[5]{0:T(128)S(1)} %stack.15.place_ref, f32[3,48,128]{2,1,0:T(8,128)S(1)} %collective-permute-done.2.own_ref, f32[3,48,128]{2,1,0:T(8,128)S(1)} %collective-permute-done.3.other_ref, f32[8,384]{1,0:T(8,128)S(1)} %get-tuple-element.36.src_left_ref, f32[8,384]{1,0:T(8,128)S(1)} %get-tuple-element.37.src_right_ref, ...), custom_call_target="tpu_custom_call" | custom-call | flops 4194304000 | bytes 1048576 | tf_op jit(solution)/shard_map/rim/pallas_call | solution.py:460
  (3 shorter events, 0.0 us)
Async XLA Ops:
  0.1 1.1 %copy-start = (f32[48,32,128]{2,1,0:T(8,128)S(1)}, f32[48,32,128]{2,1,0:T(8,128)}, u32[]{:S(2)}) copy-start(f32[48,32,128]{2,1,0:T(8,128)} %param.9) | copy-start | bytes 2359300
  1.2 6.3 %copy-start.1 = (s32[1024,7]{0,1:T(8,128)S(1)}, s32[1024,7]{0,1:T(8,128)}, u32[]{:S(2)}) copy-start(s32[1024,7]{0,1:T(8,128)} %param.16) | copy-start | bytes 86020
  1.2 6.3 %copy-start.2 = (s32[1024]{0:T(1024)S(1)}, s32[1024]{0:T(1024)}, u32[]{:S(2)}) copy-start(s32[1024]{0:T(1024)} %param.14) | copy-start | bytes 12292
  1.2 6.3 %copy-start.3 = (s32[1024]{0:T(1024)S(1)}, s32[1024]{0:T(1024)}, u32[]{:S(2)}) copy-start(s32[1024]{0:T(1024)} %param.15) | copy-start | bytes 12292
  1.2 6.3 %copy-start.6 = (f32[8]{0:T(128)S(1)}, f32[8]{0:T(128)}, u32[]{:S(2)}) copy-start(f32[8]{0:T(128)} %rates_ref.1) | copy-start | bytes 100
  1.2 6.3 %copy-start.7 = (f32[8,384]{1,0:T(8,128)S(1)}, f32[8,384]{1,0:T(8,128)}, u32[]{:S(2)}) copy-start(f32[8,384]{1,0:T(8,128)} %constant.22.clone.refs_4_.cells_ref) | copy-start | bytes 36868
  2.1 8.3 %collective-permute-start = (f32[9,48,128]{2,1,0:T(8,128)S(1)}, f32[9,48,128]{2,1,0:T(8,128)S(1)}, u32[]{:S(2)}, u32[]{:S(2)}) collective-permute-start(f32[9,48,128]{2,1,0:T(8,128)S(1)} %get-tuple-element.27), channel_id=1, source_target_pairs={{16,32},{32,16},{48,64},{64,48},{80,96},{96,80},{17,33},{33,17},{4... | collective-permute-start | bytes 663560 | tf_op jit(solution)/shard_map/ppermute | solution.py:420
  4.0 6.4 %collective-permute-start.1 = (f32[9,48,128]{2,1,0:T(8,128)S(1)}, f32[9,48,128]{2,1,0:T(8,128)S(1)}, u32[]{:S(2)}, u32[]{:S(2)}) collective-permute-start(f32[9,48,128]{2,1,0:T(8,128)S(1)} %get-tuple-element.28), channel_id=1, source_target_pairs={{0,16},{16,0},{32,48},{48,32},{64,80},{80,64},{96,112},{112,96},{1... | collective-permute-start | bytes 663560 | tf_op jit(solution)/shard_map/ppermute | solution.py:421
  9.2 1.1 %copy-start.8 = (s32[48]{0:T(128)S(1)}, s32[48]{0:T(128)}, u32[]{:S(2)}) copy-start(s32[48]{0:T(128)} %param.10) | copy-start | bytes 580
  10.4 11.7 %copy-start.4 = (f32[6]{0:T(128)S(1)}, f32[6]{0:T(128)}, u32[]{:S(2)}) copy-start(f32[6]{0:T(128)} %lateral_ref.1) | copy-start | bytes 76
  10.4 11.7 %copy-start.5 = (f32[6]{0:T(128)S(1)}, f32[6]{0:T(128)}, u32[]{:S(2)}) copy-start(f32[6]{0:T(128)} %vertical_ref.1) | copy-start | bytes 76
  11.1 14.5 %collective-permute-start.2 = (f32[3,48,128]{2,1,0:T(8,128)S(1)}, f32[3,48,128]{2,1,0:T(8,128)S(1)}, u32[]{:S(2)}, u32[]{:S(2)}) collective-permute-start(f32[3,48,128]{2,1,0:T(8,128)S(1)} %edge_columns.1), channel_id=1, source_target_pairs={{256,1},{1,256},{384,129},{129,384},{257,2},{2,257},{385,130},{130... | collective-permute-start | bytes 221192 | tf_op jit(solution)/shard_map/ppermute | solution.py:439
  25.6 8.4 %collective-permute-start.3 = (f32[3,48,128]{2,1,0:T(8,128)S(1)}, f32[3,48,128]{2,1,0:T(8,128)S(1)}, u32[]{:S(2)}, u32[]{:S(2)}) collective-permute-start(f32[3,48,128]{2,1,0:T(8,128)S(1)} %collective-permute-done.2.own_ref), channel_id=1, source_target_pairs={{0,256},{256,0},{128,384},{384,128},{1,257},{257,1},{129,385},{385... | collective-permute-start | bytes 221192 | tf_op jit(solution)/shard_map/ppermute | solution.py:449

commit v6 on v5

--- a/solution.py
+++ b/solution.py
@@ -54,8 +54,8 @@
     return high, (x - high.astype(F32)).astype(BF16)
 
 
-def edge_rows(place_ref, u_ref, far_ref, near_ref, kept_ref):
-    even = lax.rem(place_ref[1], 2) == 0
+def edge_rows(place, u_ref, far_ref, near_ref, kept_ref):
+    even = lax.rem(place[1], 2) == 0
     for i in range(HALO):
         first = u_ref[pl.ds(i, NZ, stride=ROWS), :]
         last = u_ref[pl.ds(ROWS - HALO + i, NZ, stride=ROWS), :]
@@ -72,9 +72,9 @@
     return jnp.where(even, near_ref[r - HALO - ROWS], far_ref[r - HALO - ROWS])
 
 
-def pack(place_ref, rows, row_of, packed_ref, tiles):
+def pack(place, rows, row_of, packed_ref, tiles):
     lane = lax.broadcasted_iota(jnp.int32, (NZ, LANES), 1)
-    send_last = place_ref[0] >= 2
+    send_last = place[0] >= 2
     for r in rows:
         t, first, width = PIECES[r]
         row = pltpu.roll(row_of(r), first + jnp.where(send_last, width, 0), axis=1)
@@ -83,16 +83,16 @@
         packed_ref[t] = tiles[t]
 
 
-def own_columns(place_ref, u_ref, packed_ref):
+def own_columns(place, u_ref, packed_ref):
     row_of = lambda r: u_ref[pl.ds(r - HALO, NZ, stride=ROWS), :]
-    pack(place_ref, range(HALO, HALO + ROWS), row_of, packed_ref, [jnp.zeros((NZ, LANES), F32)] * TILES)
-
-
-def edge_columns(place_ref, strips_ref, far_ref, near_ref, packed_ref):
-    even = lax.rem(place_ref[1], 2) == 0
+    pack(place, range(HALO, HALO + ROWS), row_of, packed_ref, [jnp.zeros((NZ, LANES), F32)] * TILES)
+
+
+def edge_columns(place, strips_ref, far_ref, near_ref, packed_ref):
+    even = lax.rem(place[1], 2) == 0
     rows = [r for r in PIECES if not HALO <= r < HALO + ROWS]
     row_of = lambda r: ext_row(r, even, None, far_ref, near_ref)
-    pack(place_ref, rows, row_of, packed_ref, [strips_ref[t] for t in range(TILES)])
+    pack(place, rows, row_of, packed_ref, [strips_ref[t] for t in range(TILES)])
 
 
 def side_cells():
@@ -103,25 +103,25 @@
     return cells
 
 
-def is_late(place_ref):
-    return lax.rem(place_ref[2], LINE) == LINE - 1
-
-
-def early_sources(place_ref, *refs):
-    pl.when(jnp.logical_not(is_late(place_ref)))(lambda: sources(place_ref, *refs))
-
-
-def sources(place_ref, rates_ref, plan_ref, x_ref, y_ref, cells_ref, centre_ref, left_ref, right_ref):
+def is_late(place):
+    return lax.rem(place[2], LINE) == LINE - 1
+
+
+def early_sources(place, *refs):
+    pl.when(jnp.logical_not(is_late(place)))(lambda: sources(place, *refs))
+
+
+def sources(place, rates_ref, plan_ref, x_ref, y_ref, cells_ref, centre_ref, left_ref, right_ref):
     bores = plan_ref.shape[1]
     plan = plan_ref[...]
     rate = jnp.zeros(plan.shape, F32)
     for j in range(NPULSE):
-        rate = jnp.where(plan == j, rates_ref[j], rate)
+        rate = jnp.where(plan == j, rates_ref[:, j : j + 1], rate)
     rate = jnp.concatenate([rate, jnp.zeros((1, bores), F32)], axis=0)
     rate_high = rate.astype(BF16).astype(F32)
     rate_low = rate - rate_high
-    x = x_ref[...] - place_ref[1] * ROWS
-    y = y_ref[...] - place_ref[2] * LANES
+    x = x_ref[...] - place[1] * ROWS
+    y = y_ref[...] - place[2] * LANES
     hit_x = x == lax.broadcasted_iota(jnp.int32, (ZS, bores), 0) - HALO
     hit_y = (y == lax.broadcasted_iota(jnp.int32, (LANES, bores), 0)).astype(F32).astype(BF16)
     contract = lambda p, q: lax.dot_general(p, q, (((1,), (1,)), ((), ())), preferred_element_type=F32)
@@ -143,13 +143,13 @@
         ref[...] = both[:8] + both[8:]
 
 
-def coefs(place_ref, lateral_ref, vertical_ref, ids_ref, out_ref, poly_ref):
+def coefs(place, lateral_ref, vertical_ref, ids_ref, out_ref, poly_ref):
     ids = jnp.broadcast_to(ids_ref[...], (8, LANES))
     lane = lax.broadcasted_iota(jnp.int32, (8, LANES), 1)
     cond, lat = jnp.zeros((8, LANES), F32), jnp.zeros((8, LANES), F32)
     for j in range(NLAYER):
-        cond = jnp.where(ids == j, vertical_ref[j], cond)
-        lat = jnp.where(ids == j, lateral_ref[j], lat)
+        cond = jnp.where(ids == j, vertical_ref[:, j : j + 1], cond)
+        lat = jnp.where(ids == j, lateral_ref[:, j : j + 1], lat)
     cond = jnp.where(lane < NZ, cond, 1.0)
     lat = jnp.where(lane < NZ, lat, 0.0)
     after = pltpu.roll(cond, LANES - 1, axis=1)
@@ -243,7 +243,7 @@
             if 0 <= wave - p < STEPS:
                 step(p, wave - p)
 
-    level = place_ref[0]
+    level = place[0]
     blank = jnp.zeros((SLOT - ZS, LANES), F32)
     for k in range(POWERS):
         block = poly_ref[level, STEPS, k * ZS : (k + 1) * ZS, :]
@@ -295,23 +295,23 @@
             advance(source, target, span, HALO + HALF, count, lambda j, new: edge(j, new) * below)
 
 
-def grid_rows(place_ref):
+def grid_rows(place):
     lane = lax.broadcasted_iota(jnp.int32, (BLOCKS, LANES), 1)
-    above = jnp.where((lane < SLOT) & (place_ref[1] == 0), 0.0, 1.0)
-    below = jnp.where((lane >= SLOT) & (place_ref[1] == place_ref[3]), 0.0, 1.0)
+    above = jnp.where((lane < SLOT) & (place[1] == 0), 0.0, 1.0)
+    below = jnp.where((lane >= SLOT) & (place[1] == place[3]), 0.0, 1.0)
     return above, below
 
 
 def bulk(
-    place_ref, rates_ref, plan_ref, x_ref, y_ref, cells_ref, u_ref, far_ref, near_ref,
+    place, rates_ref, plan_ref, x_ref, y_ref, cells_ref, u_ref, far_ref, near_ref,
     early_centre_ref, early_left_ref, early_right_ref, coef_ref, out_ref, left_ref, right_ref,
     line_ref, field_ref, other_field_ref, total_ref, src_ref,
 ):
-    late = is_late(place_ref)
+    late = is_late(place)
 
     @pl.when(late)
     def _():
-        sources(place_ref, rates_ref, plan_ref, x_ref, y_ref, cells_ref, src_ref, left_ref, right_ref)
+        sources(place, rates_ref, plan_ref, x_ref, y_ref, cells_ref, src_ref, left_ref, right_ref)
 
     @pl.when(jnp.logical_not(late))
     def _():
@@ -319,8 +319,8 @@
         left_ref[...] = early_left_ref[...]
         right_ref[...] = early_right_ref[...]
 
-    ty = place_ref[2]
-    even = lax.rem(place_ref[1], 2) == 0
+    ty = place[2]
+    even = lax.rem(place[1], 2) == 0
     sublane = lax.broadcasted_iota(jnp.int32, (BLOCKS, LANES), 0)
     blank = jnp.zeros((SLOT - ZS, LANES), F32)
     room = jnp.zeros((BACK, LANES), F32)
@@ -334,12 +334,12 @@
         for j in range(SPAN):
             field_ref[i, 8 * j : 8 * j + 8, :] = line_ref[i, pl.ds(j, BLOCKS, stride=SPAN), :]
     left = jnp.where((sublane == 0) & (ty == 0), 0.0, 1.0)
-    right = jnp.where((sublane == BLOCKS - 1) & (ty == place_ref[4]), 0.0, 1.0)
+    right = jnp.where((sublane == BLOCKS - 1) & (ty == place[4]), 0.0, 1.0)
 
     def edge(j, new):
         return new * left if j < BACK else new * right if j >= SPAN - BACK else new
 
-    powers((field_ref, other_field_ref), total_ref, coef_ref, SPAN, edge, *grid_rows(place_ref))
+    powers((field_ref, other_field_ref), total_ref, coef_ref, SPAN, edge, *grid_rows(place))
     for i in range(HALF):
         for j in range(SPAN):
             line_ref[i, pl.ds(j, BLOCKS, stride=SPAN), :] = total_ref[i, 8 * j : 8 * j + 8, :]
@@ -347,10 +347,10 @@
 
 
 def rim(
-    place_ref, own_ref, other_ref, src_left_ref, src_right_ref, coef_ref, bulk_ref,
+    place, own_ref, other_ref, src_left_ref, src_right_ref, coef_ref, bulk_ref,
     out_ref, line_ref, side_ref, field_ref, other_field_ref, total_ref, result_ref, sems,
 ):
-    low_level = place_ref[0] < 2
+    low_level = place[0] < 2
     blank = jnp.zeros((SLOT - ZS, LANES), F32)
     for side, src_ref in enumerate((src_left_ref, src_right_ref)):
         for t in range(TILES):
@@ -371,7 +371,7 @@
         line_ref[i, 2 * RIM - HALO :, :] = jnp.where(in_low_half, halo_of(1, i), halo_of(1, i + HALF))
         for j in range(RIM_SPAN):
             field_ref[i, 8 * j : 8 * j + 8, :] = line_ref[i, pl.ds(j, BLOCKS, stride=RIM_SPAN), :]
-    powers((field_ref, other_field_ref), total_ref, coef_ref, RIM_SPAN, lambda j, new: new, *grid_rows(place_ref))
+    powers((field_ref, other_field_ref), total_ref, coef_ref, RIM_SPAN, lambda j, new: new, *grid_rows(place))
     copies = []
     for i in range(HALF):
         for j in range(RIM_SPAN):
@@ -390,13 +390,16 @@
         copy.wait()
 
 
-SMEM = pl.BlockSpec(memory_space=pltpu.SMEM)
 WHOLE = pl.BlockSpec(memory_space=pltpu.VMEM)
 
 
 def call(kernel, name, ins, outs, scratch=(), cost=0, out_spec=None):
+    def with_place(*refs):
+        sizes = [lax.axis_size(name) for name in ("tx", "ty")]
+        kernel([lax.axis_index(name) for name in ("level", "tx", "ty")] + [size - 1 for size in sizes], *refs)
+
     return pl.pallas_call(
-        kernel,
+        with_place,
         out_shape=outs,
         in_specs=ins,
         out_specs=out_spec or jax.tree.map(lambda _: WHOLE, outs),
@@ -410,25 +413,21 @@
 def on_device(initial, layer_ids, lateral_number, vertical_number, pulse_rates, bore_x, bore_y, plan):
     shape = lambda *s, dtype=F32: jax.ShapeDtypeStruct(s, dtype)
     count_x, count_y = lax.axis_size("tx"), lax.axis_size("ty")
-    indices = [lax.axis_index(name) for name in ("level", "tx", "ty")]
-    place = jnp.stack(indices + [jnp.int32(count_x - 1), jnp.int32(count_y - 1)])
     flat = initial.reshape(NZ * ROWS, LANES)
     slab = shape(HALO, NZ, LANES)
     whole = shape(NZ * ROWS, LANES)
-    far, near, kept = call(edge_rows, "edge_rows", [SMEM, WHOLE], (slab, slab, whole), cost=800 << 20)(place, flat)
+    far, near, kept = call(edge_rows, "edge_rows", [WHOLE], (slab, slab, whole), cost=800 << 20)(flat)
     pairs = lambda first: [(i + a, i + 1 - a) for i in range(first, count_x - 1, 2) for a in (0, 1)]
     far = lax.ppermute(far, "tx", pairs(1))
     near = lax.ppermute(near, "tx", pairs(0))
     packed = shape(TILES, NZ, LANES)
-    strips = call(own_columns, "own_columns", [SMEM, WHOLE], packed, cost=1000 << 20)(place, kept)
+    strips = call(own_columns, "own_columns", [WHOLE], packed, cost=1000 << 20)(kept)
     sides = shape(8, TILES * LANES)
     planes = (shape(ZS * 8, LANES), sides, sides)
-    bores = (pulse_rates, plan.T, bore_x[None, :], bore_y[None, :], side_cells())
-    src = call(early_sources, "early_sources", [SMEM] * 2 + [WHOLE] * 4, planes, cost=1700 << 20)(place, *bores)
+    bores = (pulse_rates[None, :], plan.T, bore_x[None, :], bore_y[None, :], side_cells())
+    src = call(early_sources, "early_sources", [WHOLE] * 5, planes, cost=1700 << 20)(*bores)
     strips, src = lax.optimization_barrier((strips, src))
-    strips = call(edge_columns, "edge_columns", [SMEM] + [WHOLE] * 3, packed, cost=800 << 20)(
-        place, strips, far, near
-    )
+    strips = call(edge_columns, "edge_columns", [WHOLE] * 3, packed, cost=800 << 20)(strips, far, near)
     ids = jnp.pad(layer_ids, (0, LANES - NZ))[None, :]
     strips, ids = lax.optimization_barrier((strips, ids))
     route = []
@@ -440,11 +439,11 @@
     table = call(
         coefs,
         "coefs",
-        [SMEM] * 3 + [WHOLE],
+        [WHOLE] * 3,
         shape(POWERS, 2 * LANES, 2 * LANES, dtype=BF16),
         [pltpu.VMEM((LEVELS, STEPS + 1, POWERS * ZS, LANES), F32)],
         cost=4600 << 20,
-    )(place, lateral_number, vertical_number, ids)
+    )(lateral_number[None, :], vertical_number[None, :], ids)
     own, table = lax.optimization_barrier((own, table))
     other = lax.ppermute(own, "level", [(0, 2), (2, 0), (1, 3), (3, 1)])
     room = lambda span: [pltpu.VMEM((PAIRS, span * BLOCKS, LANES), F32)]
@@ -452,15 +451,15 @@
     inner, src_left, src_right = call(
         bulk,
         "bulk",
-        [SMEM] * 2 + [WHOLE] * 11,
+        [WHOLE] * 12,
         (shape(HALF, LANES, LANES), sides, sides),
         room(SPAN) * 3 + total(SPAN) + [pltpu.VMEM((ZS * 8, LANES), F32)],
         cost=8000 << 20,
-    )(place, *bores, kept, far, near, *src, table)
+    )(*bores, kept, far, near, *src, table)
     result = call(
         rim,
         "rim",
-        [SMEM] + [WHOLE] * 6,
+        [WHOLE] * 6,
         shape(NZ, ROWS, LANES),
         room(RIM_SPAN)
         + [pltpu.VMEM((2, TILES * LANES, LANES), F32)]
@@ -469,7 +468,7 @@
         + [pltpu.VMEM((ROWS // 8, NZ * 8, LANES), F32), pltpu.SemaphoreType.DMA((ROWS // 8,))],
         out_spec=pl.BlockSpec(memory_space=pl.ANY),
         cost=4000 << 20,
-    )(place, own, other, src_left, src_right, table, inner)
+    )(own, other, src_left, src_right, table, inner)
     return result.reshape(1, NZ, ROWS, LANES)
 
 

time: 37.5 us -> 35.8 us (0.955)
  Pallas kernels: 17 us -> 13.2 us
  waiting for transfers between devices: 0.39 us -> 1.51 us
  starting transfers between devices: 18.3 us -> 19.3 us
    pallas_call x7, Pallas kernels: 17 us -> 13.2 us  [the longest x1 5.45 us: on_device(): call(bulk, 'bulk', [WHOLE] * 12, (shape(HALF, LANES, LANES), sides, sides...]
    ppermute x1, starting transfers between devices: 10.9 us -> 12 us  [on_device(): own = lax.ppermute(strips, ('level', 'ty'), route)]
    ppermute x1, waiting for transfers between devices: 0.38 us -> 1.18 us  [on_device(): other = lax.ppermute(own, 'level', [(0, 2), (2, 0), (1, 3), (3, 1)])]
  transfers between devices with their start and end apart: 4 -> 4, of which waited for: 1 -> 2; matrix products, arithmetic and copies ran while one was open for 0% -> 0% of each run, Pallas kernels for 33% -> 29%
where the time goes in v6:
time: 35.8 us; the launch traced here: 35.6 us
  starting transfers between devices  19.3 us (54%)
  Pallas kernels  13.2 us (37%)
  waiting for transfers between devices  1.51 us (4%)
  local copies, waits for them, and re-layouts  1.26 us (4%)
    ppermute x1, starting transfers between devices, on_device(): own = lax.ppermute(strips, ('level', 'ty'), route)  12 us
    pallas_call x1, Pallas kernels, on_device(): call(bulk, 'bulk', [WHOLE] * 12, (shape(HALF, LANES, LANES), sides, sides...  5.45 us
    ppermute x1, starting transfers between devices, on_device(): near = lax.ppermute(near, 'tx', pairs(0))  3.5 us
    pallas_call x1, Pallas kernels, on_device(): call(coefs, 'coefs', [WHOLE] * 3, shape(POWERS, 2 * LANES, 2 * LANES, dty...  3.06 us
    pallas_call x1, Pallas kernels, on_device(): call(rim, 'rim', [WHOLE] * 6, shape(NZ, ROWS, LANES), room(RIM_SPAN) + [p...  2.52 us
    ppermute x1, starting transfers between devices, on_device(): far = lax.ppermute(far, 'tx', pairs(1))  1.92 us
    ppermute x1, starting transfers between devices, on_device(): other = lax.ppermute(own, 'level', [(0, 2), (2, 0), (1, 3), (3, 1)])  1.91 us
    unnamed x18, local copies, waits for them, and re-layouts  1.25 us
  transfers between devices with their start and end apart: 4, of which 2 were waited for; matrix products, arithmetic and copies ran while one was open for 0% of the time, Pallas kernels for 29%

profile of v6, /device:TPU:26, one launch (start us, length us, event | category | flops | bytes accessed | tf_op | source)
XLA Modules:
  0.0 35.6 jit_solution(17911359978115194943)
XLA Ops:
  0.0 0.0 copy-start
  0.0 1.1 %copy-done = f32[48,32,128]{2,1,0:T(8,128)S(1)} copy-done((f32[48,32,128]{2,1,0:T(8,128)S(1)}, f32[48,32,128]{2,1,0:T(8,128)}, u32[]{:S(2)}) %copy-start) | copy-done | bytes 786456
  1.1 0.0 copy-start.1
  1.1 0.0 copy-start.2
  1.1 0.0 copy-start.3
  1.1 0.0 copy-start.6
  1.1 0.0 copy-start.7
  1.2 0.3 edge_rows.1
  1.5 1.9 %collective-permute-start = (f32[9,48,128]{2,1,0:T(8,128)S(1)}, f32[9,48,128]{2,1,0:T(8,128)S(1)}, u32[]{:S(2)}, u32[]{:S(2)}) collective-permute-start(f32[9,48,128]{2,1,0:T(8,128)S(1)} %get-tuple-element.27), channel_id=1, source_target_pairs={{16,32},{32,16},{48,64},{64,48},{80,96},{96,80},{17,33},{33,17},{4... | collective-permute-start | bytes 663560 | tf_op jit(solution)/shard_map/ppermute | solution.py:421
  3.4 3.5 %collective-permute-start.1 = (f32[9,48,128]{2,1,0:T(8,128)S(1)}, f32[9,48,128]{2,1,0:T(8,128)S(1)}, u32[]{:S(2)}, u32[]{:S(2)}) collective-permute-start(f32[9,48,128]{2,1,0:T(8,128)S(1)} %get-tuple-element.28), channel_id=1, source_target_pairs={{0,16},{16,0},{32,48},{48,32},{64,80},{80,64},{96,112},{112,96},{1... | collective-permute-start | bytes 663560 | tf_op jit(solution)/shard_map/ppermute | solution.py:422
  6.9 0.0 copy-done.1
  6.9 0.0 copy-done.2
  6.9 0.0 copy-done.3
  6.9 0.0 copy-done.6
  6.9 0.0 copy-done.7
  7.0 1.1 %early_sources.1 = (f32[448,128]{1,0:T(8,128)S(1)}, f32[8,384]{1,0:T(8,128)S(1)}, f32[8,384]{1,0:T(8,128)S(1)}) custom-call(f32[1,8]{1,0:T(1,128)S(1)} %bitcast.19, s32[7,1024]{1,0:T(8,128)S(1)} %bitcast.11, s32[1,1024]{1,0:T(1,128)S(1)} %bitcast.13, s32[1,1024]{1,0:T(1,128)S(1)} %bitcast.15, f32[8,384]{1,0:T(8,128)S(1)} %copy-done.7), custom_call_target="tpu_custom_call" | custom-call | flops 1782579200 | bytes 1048576 | tf_op jit(solution)/shard_map/early_sources/pallas_call | solution.py:428
  8.1 0.0 copy-start.8
  8.1 0.6 %own_columns.1.refs_0_ = f32[3,48,128]{2,1,0:T(8,128)S(1)} custom-call(f32[1536,128]{1,0:T(8,128)S(1)} %get-tuple-element.22.refs_0_.refs_5_), custom_call_target="tpu_custom_call" | custom-call | flops 1048576000 | bytes 1048576 | tf_op jit(solution)/shard_map/own_columns/pallas_call | solution.py:424
  8.6 0.1 copy-done.8
  8.7 0.0 copy-start.4
  8.7 0.0 collective-permute-done.refs_1_.refs_6_
  8.8 0.0 collective-permute-done.1.refs_2_.refs_7_
  8.8 0.2 edge_columns.1
  8.9 12.0 %collective-permute-start.2 = (f32[3,48,128]{2,1,0:T(8,128)S(1)}, f32[3,48,128]{2,1,0:T(8,128)S(1)}, u32[]{:S(2)}, u32[]{:S(2)}) collective-permute-start(f32[3,48,128]{2,1,0:T(8,128)S(1)} %edge_columns.1), channel_id=1, source_target_pairs={{256,1},{1,256},{384,129},{129,384},{257,2},{2,257},{385,130},{130... | collective-permute-start | bytes 221192 | tf_op jit(solution)/shard_map/ppermute | solution.py:438
  20.9 0.0 copy-done.4
  20.9 0.0 copy-done.5
  21.0 3.1 %coefs.1.refs_11_.refs_4_ = bf16[10,256,256]{2,1,0:T(8,128)(2,1)S(1)} custom-call(f32[1,6]{1,0:T(1,128)S(1)} %bitcast.17, f32[1,6]{1,0:T(1,128)S(1)} %bitcast.18, s32[1,128]{1,0:T(1,128)S(1)} %pad_bitcast_fusion.refs_2_), custom_call_target="tpu_custom_call" | custom-call | flops 4823449600 | bytes 1048576 | tf_op jit(solution)/shard_map/coefs/pallas_call | solution.py:439
  24.0 0.3 collective-permute-done.2.refs_0_
  24.3 1.9 %collective-permute-start.3 = (f32[3,48,128]{2,1,0:T(8,128)S(1)}, f32[3,48,128]{2,1,0:T(8,128)S(1)}, u32[]{:S(2)}, u32[]{:S(2)}) collective-permute-start(f32[3,48,128]{2,1,0:T(8,128)S(1)} %collective-permute-done.2.refs_0_), channel_id=1, source_target_pairs={{0,256},{256,0},{128,384},{384,128},{1,257},{257,1},{129,385},{385... | collective-permute-start | bytes 221192 | tf_op jit(solution)/shard_map/ppermute | solution.py:448
  26.2 5.4 %bulk.1 = (f32[16,128,128]{2,1,0:T(8,128)S(1)}, f32[8,384]{1,0:T(8,128)S(1)}, f32[8,384]{1,0:T(8,128)S(1)}) custom-call(f32[1,8]{1,0:T(1,128)S(1)} %bitcast.20, s32[7,1024]{1,0:T(8,128)S(1)} %bitcast.12, s32[1,1024]{1,0:T(1,128)S(1)} %bitcast.14, s32[1,1024]{1,0:T(1,128)S(1)} %bitcast.16, f32[8,384]{1,0:T(8,128)S(1)} %copy-done.7, ...), custom_call_target="tpu_custom_call" | custom-call | flops 8388608000 | bytes 1048576 | tf_op jit(solution)/shard_map/bulk/pallas_call | solution.py:451
  31.7 1.2 %collective-permute-done.3.refs_1_ = f32[3,48,128]{2,1,0:T(8,128)S(1)} collective-permute-done((f32[3,48,128]{2,1,0:T(8,128)S(1)}, f32[3,48,128]{2,1,0:T(8,128)S(1)}, u32[]{:S(2)}, u32[]{:S(2)}) %collective-permute-start.3) | collective-permute-done | bytes 73760 | tf_op jit(solution)/shard_map/ppermute | solution.py:448
  32.9 2.5 %rim.1 = f32[48,32,128]{2,1,0:T(8,128)} custom-call(f32[3,48,128]{2,1,0:T(8,128)S(1)} %collective-permute-done.2.refs_0_, f32[3,48,128]{2,1,0:T(8,128)S(1)} %collective-permute-done.3.refs_1_, f32[8,384]{1,0:T(8,128)S(1)} %get-tuple-element.36.refs_2_, f32[8,384]{1,0:T(8,128)S(1)} %get-tuple-element.37.refs_3_, ...), custom_call_target="tpu_custom_call" | custom-call | flops 4194304000 | bytes 1048576 | tf_op jit(solution)/shard_map/rim/pallas_call | solution.py:459
  (2 shorter events, 0.0 us)
Async XLA Ops:
  0.0 1.1 %copy-start = (f32[48,32,128]{2,1,0:T(8,128)S(1)}, f32[48,32,128]{2,1,0:T(8,128)}, u32[]{:S(2)}) copy-start(f32[48,32,128]{2,1,0:T(8,128)} %param.9) | copy-start | bytes 2359300
  1.1 5.8 %copy-start.1 = (s32[1024,7]{0,1:T(8,128)S(1)}, s32[1024,7]{0,1:T(8,128)}, u32[]{:S(2)}) copy-start(s32[1024,7]{0,1:T(8,128)} %param.16) | copy-start | bytes 86020
  1.1 5.8 %copy-start.2 = (s32[1024]{0:T(1024)S(1)}, s32[1024]{0:T(1024)}, u32[]{:S(2)}) copy-start(s32[1024]{0:T(1024)} %param.14) | copy-start | bytes 12292
  1.1 5.8 %copy-start.3 = (s32[1024]{0:T(1024)S(1)}, s32[1024]{0:T(1024)}, u32[]{:S(2)}) copy-start(s32[1024]{0:T(1024)} %param.15) | copy-start | bytes 12292
  1.1 5.8 %copy-start.6 = (f32[8]{0:T(128)S(1)}, f32[8]{0:T(128)}, u32[]{:S(2)}) copy-start(f32[8]{0:T(128)} %param.13) | copy-start | bytes 100
  1.1 5.8 %copy-start.7 = (f32[8,384]{1,0:T(8,128)S(1)}, f32[8,384]{1,0:T(8,128)}, u32[]{:S(2)}) copy-start(f32[8,384]{1,0:T(8,128)} %constant.4.clone.refs_4_) | copy-start | bytes 36868
  1.5 7.3 %collective-permute-start = (f32[9,48,128]{2,1,0:T(8,128)S(1)}, f32[9,48,128]{2,1,0:T(8,128)S(1)}, u32[]{:S(2)}, u32[]{:S(2)}) collective-permute-start(f32[9,48,128]{2,1,0:T(8,128)S(1)} %get-tuple-element.27), channel_id=1, source_target_pairs={{16,32},{32,16},{48,64},{64,48},{80,96},{96,80},{17,33},{33,17},{4... | collective-permute-start | bytes 663560 | tf_op jit(solution)/shard_map/ppermute | solution.py:421
  3.4 5.4 %collective-permute-start.1 = (f32[9,48,128]{2,1,0:T(8,128)S(1)}, f32[9,48,128]{2,1,0:T(8,128)S(1)}, u32[]{:S(2)}, u32[]{:S(2)}) collective-permute-start(f32[9,48,128]{2,1,0:T(8,128)S(1)} %get-tuple-element.28), channel_id=1, source_target_pairs={{0,16},{16,0},{32,48},{48,32},{64,80},{80,64},{96,112},{112,96},{1... | collective-permute-start | bytes 663560 | tf_op jit(solution)/shard_map/ppermute | solution.py:422
  8.1 0.7 %copy-start.8 = (s32[48]{0:T(128)S(1)}, s32[48]{0:T(128)}, u32[]{:S(2)}) copy-start(s32[48]{0:T(128)} %param.10) | copy-start | bytes 580
  8.7 12.2 %copy-start.4 = (f32[6]{0:T(128)S(1)}, f32[6]{0:T(128)}, u32[]{:S(2)}) copy-start(f32[6]{0:T(128)} %param.11) | copy-start | bytes 76
  8.7 12.2 %copy-start.5 = (f32[6]{0:T(128)S(1)}, f32[6]{0:T(128)}, u32[]{:S(2)}) copy-start(f32[6]{0:T(128)} %param.12) | copy-start | bytes 76
  8.9 15.4 %collective-permute-start.2 = (f32[3,48,128]{2,1,0:T(8,128)S(1)}, f32[3,48,128]{2,1,0:T(8,128)S(1)}, u32[]{:S(2)}, u32[]{:S(2)}) collective-permute-start(f32[3,48,128]{2,1,0:T(8,128)S(1)} %edge_columns.1), channel_id=1, source_target_pairs={{256,1},{1,256},{384,129},{129,384},{257,2},{2,257},{385,130},{130... | collective-permute-start | bytes 221192 | tf_op jit(solution)/shard_map/ppermute | solution.py:438
  24.3 8.5 %collective-permute-start.3 = (f32[3,48,128]{2,1,0:T(8,128)S(1)}, f32[3,48,128]{2,1,0:T(8,128)S(1)}, u32[]{:S(2)}, u32[]{:S(2)}) collective-permute-start(f32[3,48,128]{2,1,0:T(8,128)S(1)} %collective-permute-done.2.refs_0_), channel_id=1, source_target_pairs={{0,256},{256,0},{128,384},{384,128},{1,257},{257,1},{129,385},{385... | collective-permute-start | bytes 221192 | tf_op jit(solution)/shard_map/ppermute | solution.py:448
